TPU v7x, 32 devices: a whole 2x2x4 slice. The times are simulated.
32 devices in a mesh: groups: 2 (over x), seq: 16 (over z, y, core).
Axes of the slice: x: 2, y: 2, z: 4, core: 2. Of those that a mesh axis runs over, the one named last changes fastest.
Arguments:
- tokens: bfloat16 [8192, 4096], P(('groups', 'seq')), parts along dimension 0, may hold values from -14 to 14, as said below
- norm_gain: float32 [4096], replicated, may hold values from 0.25 to 1.75
- w_query: bfloat16 [4096, 2048], P('seq'), may hold values from -1 to 1, as said below
- w_key: bfloat16 [4096, 512], P('seq'), may hold values from -24 to 24
- w_value: bfloat16 [4096, 512], P('seq'), may hold values from -0.09375 to 0.09375
- passage_blocks: int32 [64], P(('groups', 'seq')), parts along dimension 0, may hold values from 0 to 9, as said below
Outputs:
- attended: bfloat16 [8192, 2048], P(('groups', 'seq')), parts along dimension 0
There are 2 independent parts, one for each index of `groups`. A program takes and returns all parts, laid end to end along the dimension named above; an argument that names none is the same for every part. Nothing has to cross between parts.
Inputs may be any that keep to these rules, and one draw needn't show every extreme that they name: `passage_blocks`: passage numbers never fall along the row; each passage covers 1 to 7 whole blocks; the first and the last passage of the row cover exactly 7. `tokens`: hidden states of order one. `w_query`: entries of order 4096 ** -0.5.
All inputs are finite; a program needn't handle non-finite values.
Results may differ from a plain program's by a relative error of at most 0.0049.
The roundings to bfloat16 on the way count: a program that leaves them out, or rounds other values in their place, can miss the bound.
Values may be sent and summed in bfloat16 or wider, within the bound.
No kernel may reach another device: no remote copies, remote signals or barrier semaphores. Data moves between devices by JAX's collectives and lax.ppermute only.
A program may use at most 128 MiB of HBM per device.

v0:
```python
import jax
import jax.numpy as jnp
from jax import lax
from jax.sharding import PartitionSpec as P

HD = 128
QH = 16
KVH = 4
REACH = 3


def passed_along(value, axis, by):
    peers = lax.axis_size(axis)
    pairs = [(i, i + by) for i in range(peers) if 0 <= i + by < peers]
    return lax.ppermute(value, axis, pairs)


def normalize(tokens, norm_gain):
    widened = tokens.astype(jnp.float32)
    inverse = lax.rsqrt(jnp.mean(widened * widened, axis=-1, keepdims=True) + 1e-05)
    return (widened * inverse * norm_gain).astype(jnp.bfloat16)


def dense_attention(query_heads, all_keys, all_values, query_ids, key_ids):
    row_count = query_heads.shape[1]
    key_count = all_keys.shape[0]
    key_heads = all_keys.reshape(key_count, KVH, HD).transpose(1, 0, 2)
    value_heads = all_values.reshape(key_count, KVH, HD).transpose(1, 0, 2)
    allowed = query_ids[:, None] == key_ids[None, :]

    def one_head(operands):
        head_query, head_keys, head_values = operands
        scores = jnp.einsum(
            "tgd,sd->gts", head_query, head_keys, preferred_element_type=jnp.float32
        ) * HD ** (-0.5)
        scores = jnp.where(allowed[None], scores, -1e30)
        row_max = jnp.max(scores, axis=-1, keepdims=True)
        weights = jnp.exp(scores - row_max)
        row_total = jnp.sum(weights, axis=-1)
        rounded = weights.astype(jnp.bfloat16)
        mixed = jnp.einsum("gts,sd->tgd", rounded, head_values, preferred_element_type=jnp.float32)
        return mixed / row_total.transpose(1, 0)[:, :, None]

    stacked = lax.map(one_head, (query_heads, key_heads, value_heads))
    return stacked.transpose(1, 0, 2, 3).reshape(row_count, QH * HD)


def on_device(tokens, norm_gain, w_query, w_key, w_value, passage_blocks):
    row_count = tokens.shape[0]
    block_len = row_count // passage_blocks.shape[0]
    normed = normalize(tokens, norm_gain)

    def add_rows(piece):
        return jnp.dot(normed, piece, preferred_element_type=jnp.float32)

    pieces = (
        lax.all_gather(w_query, "seq", axis=0, tiled=True),
        lax.all_gather(w_key, "seq", axis=0, tiled=True),
        lax.all_gather(w_value, "seq", axis=0, tiled=True),
    )
    query = add_rows(pieces[0])
    keys = add_rows(pieces[1])
    values = add_rows(pieces[2])
    key_rounded = keys.astype(jnp.bfloat16)
    value_rounded = values.astype(jnp.bfloat16)
    passage_ids = jnp.repeat(passage_blocks + 1, block_len).astype(jnp.bfloat16)
    own = (key_rounded, value_rounded, passage_ids)
    earlier = []
    later = []
    for distance in range(1, REACH + 1):
        for direction in (1, -1):
            moved = passed_along(
                (key_rounded, value_rounded, passage_ids), "seq", direction * distance
            )
            if direction == 1:
                earlier.insert(0, moved)
            else:
                later.append(moved)
    pieces = earlier + [own] + later
    query_rounded = query.astype(jnp.bfloat16)
    query_heads = query_rounded.reshape(row_count, KVH, QH // KVH, HD).transpose(1, 0, 2, 3)
    all_keys = jnp.concatenate([piece[0] for piece in pieces], axis=0)
    all_values = jnp.concatenate([piece[1] for piece in pieces], axis=0)
    all_ids = jnp.concatenate([piece[2] for piece in pieces], axis=0)
    result = dense_attention(query_heads, all_keys, all_values, passage_ids, all_ids)
    return result.astype(jnp.bfloat16)


def solution(mesh):
    in_specs = (
        P(("groups", "seq"), None),
        P(),
        P("seq", None),
        P("seq", None),
        P("seq", None),
        P(("groups", "seq")),
    )
    out_specs = P(("groups", "seq"), None)
    return jax.shard_map(
        on_device, mesh=mesh, in_specs=in_specs, out_specs=out_specs, check_vma=False
    )
```

profile of v0, /device:TPU:1, one launch (start us, length us, event | category | flops | bytes accessed | tf_op | source)
XLA Modules:
  0.0 314.1 jit_solution(10154052325057209868)
XLA Ops:
  6.5 0.7 all-gather.6.cloned.1.call-update
  7.3 0.7 all-gather.4.cloned.1.call-update
  8.1 0.7 all-gather.8.cloned.1.call-update
  8.7 0.7 add_convert_fusion
  9.5 4.6 %collective-permute-start.6 = (bf16[256]{0:T(256)(128)(2,1)S(1)}, bf16[256]{0:T(256)(128)(2,1)S(1)}, u32[]{:S(2)}, u32[]{:S(2)}) collective-permute-start(bf16[256]{0:T(256)(128)(2,1)S(1)} %broadcast_bitcast_fusion), channel_id=1, source_target_pairs={{0,3},{1,4},{2,5},{3,6},{4,7},{5,8},{6,9},{7,10},{8,11},{9,12},{10... | collective-permute-start | bytes 1544 | tf_op jit(solution)/shard_map/ppermute | solution.py:15
  14.1 3.1 collective-permute-start.7
  17.2 3.1 collective-permute-start.8
  20.3 1.9 collective-permute-start.9
  22.3 1.3 collective-permute-start.10
  23.6 2.1 fusion.31
  25.7 1.3 collective-permute-start.11
  27.0 0.2 dynamic-update-slice
  28.3 4.7 %collective-permute-done.11 = bf16[256]{0:T(256)(128)(2,1)S(1)} collective-permute-done((bf16[256]{0:T(256)(128)(2,1)S(1)}, bf16[256]{0:T(256)(128)(2,1)S(1)}, u32[]{:S(2)}, u32[]{:S(2)}) %collective-permute-start.11) | collective-permute-done | bytes 544 | tf_op jit(solution)/shard_map/ppermute | solution.py:15
  33.2 29.6 %all-gather.6.cloned.1.call-done = bf16[4096,512]{1,0:T(8,128)(2,1)} async-done(((bf16[256,512]{1,0:T(8,128)(2,1)}), bf16[4096,512]{1,0:T(8,128)(2,1)}) %all-gather.6.cloned.1.call-update) | async-done | bytes 4194320 | tf_op jit(solution)/shard_map/all_gather | solution.py:58
  62.8 3.5 %convolution_convert_fusion.1 = bf16[256,512]{1,0:T(8,128)(2,1)S(1)} fusion(bf16[4096,512]{1,0:T(8,128)(2,1)} %all-gather.6.cloned.1.call-done, bf16[256,4096]{1,0:T(8,128)(2,1)S(1)} %copy-done, f32[4096]{0:T(1024)S(1)} %copy-done.1, f32[256]{0:T(256)S(1)} %add_rsqrt_fusion), kind=kOutput, calls=%fused_computation.31 | convolution fusion | flops 1078067200 | bytes 6571008 | tf_op jit(solution)/shard_map/dot_general | solution.py:54
  66.3 4.0 %collective-permute-start.12 = (bf16[256,512]{1,0:T(8,128)(2,1)S(1)}, bf16[256,512]{1,0:T(8,128)(2,1)}, u32[]{:S(2)}, u32[]{:S(2)}) collective-permute-start(bf16[256,512]{1,0:T(8,128)(2,1)S(1)} %convolution_convert_fusion.1), channel_id=1, source_target_pairs={{0,3},{1,4},{2,5},{3,6},{4,7},{5,8},{6,9},{7,10},{8,11},{9,12},{10... | collective-permute-start | bytes 786440 | tf_op jit(solution)/shard_map/ppermute | solution.py:15
  70.3 1.5 collective-permute-start.13
  71.8 3.7 %collective-permute-start.14 = (bf16[256,512]{1,0:T(8,128)(2,1)S(1)}, bf16[256,512]{1,0:T(8,128)(2,1)S(1)}, u32[]{:S(2)}, u32[]{:S(2)}) collective-permute-start(bf16[256,512]{1,0:T(8,128)(2,1)S(1)} %convolution_convert_fusion.1), channel_id=1, source_target_pairs={{0,1},{1,2},{2,3},{3,4},{4,5},{5,6},{6,7},{7,8},{8,9},{9,10},{10,1... | collective-permute-start | bytes 786440 | tf_op jit(solution)/shard_map/ppermute | solution.py:15
  75.4 1.9 collective-permute-start.15
  77.4 1.3 collective-permute-start.16
  78.7 40.8 %all-gather.4.cloned.1.call-done = bf16[4096,512]{1,0:T(8,128)(2,1)} async-done(((bf16[256,512]{1,0:T(8,128)(2,1)}), bf16[4096,512]{1,0:T(8,128)(2,1)}) %all-gather.4.cloned.1.call-update) | async-done | bytes 4194320 | tf_op jit(solution)/shard_map/all_gather | solution.py:59
  119.4 3.5 %convolution_convert_fusion.2 = bf16[256,512]{1,0:T(8,128)(2,1)S(1)} fusion(bf16[4096,512]{1,0:T(8,128)(2,1)} %all-gather.4.cloned.1.call-done, bf16[256,4096]{1,0:T(8,128)(2,1)S(1)} %copy-done, f32[4096]{0:T(1024)S(1)} %copy-done.1, f32[256]{0:T(256)S(1)} %add_rsqrt_fusion), kind=kOutput, calls=%fused_computation.32 | convolution fusion | flops 1078067200 | bytes 6571008 | tf_op jit(solution)/shard_map/dot_general | solution.py:54
  123.0 3.3 %collective-permute-start = (bf16[256,512]{1,0:T(8,128)(2,1)S(1)}, bf16[256,512]{1,0:T(8,128)(2,1)S(1)}, u32[]{:S(2)}, u32[]{:S(2)}) collective-permute-start(bf16[256,512]{1,0:T(8,128)(2,1)S(1)} %convolution_convert_fusion.2), channel_id=1, source_target_pairs={{0,3},{1,4},{2,5},{3,6},{4,7},{5,8},{6,9},{7,10},{8,11},{9,12},{10... | collective-permute-start | bytes 786440 | tf_op jit(solution)/shard_map/ppermute | solution.py:15
  126.3 1.7 constant_dynamic-update-slice_fusion.13
  128.0 2.1 collective-permute-start.1
  130.1 0.7 constant_dynamic-update-slice_fusion.12
  130.8 3.5 %collective-permute-start.2 = (bf16[256,512]{1,0:T(8,128)(2,1)S(1)}, bf16[256,512]{1,0:T(8,128)(2,1)S(1)}, u32[]{:S(2)}, u32[]{:S(2)}) collective-permute-start(bf16[256,512]{1,0:T(8,128)(2,1)S(1)} %convolution_convert_fusion.2), channel_id=1, source_target_pairs={{0,1},{1,2},{2,3},{3,4},{4,5},{5,6},{6,7},{7,8},{8,9},{9,10},{10,1... | collective-permute-start | bytes 786440 | tf_op jit(solution)/shard_map/ppermute | solution.py:15
  134.3 0.7 constant_dynamic-update-slice_fusion.11
  135.0 0.7 constant_dynamic-update-slice_fusion.10
  135.8 1.9 collective-permute-start.3
  137.7 3.4 %collective-permute-done.1 = bf16[256,512]{1,0:T(8,128)(2,1)S(1)} collective-permute-done((bf16[256,512]{1,0:T(8,128)(2,1)S(1)}, bf16[256,512]{1,0:T(8,128)(2,1)S(1)}, u32[]{:S(2)}, u32[]{:S(2)}) %collective-permute-start.1) | collective-permute-done | bytes 262176 | tf_op jit(solution)/shard_map/ppermute | solution.py:15
  141.2 1.3 collective-permute-start.4
  142.5 9.9 %collective-permute-done.2 = bf16[256,512]{1,0:T(8,128)(2,1)S(1)} collective-permute-done((bf16[256,512]{1,0:T(8,128)(2,1)S(1)}, bf16[256,512]{1,0:T(8,128)(2,1)S(1)}, u32[]{:S(2)}, u32[]{:S(2)}) %collective-permute-start.2) | collective-permute-done | bytes 262176 | tf_op jit(solution)/shard_map/ppermute | solution.py:15
  152.3 1.3 collective-permute-start.5
  153.7 1.5 collective-permute-start.17
  155.2 25.2 %collective-permute-done.5 = bf16[256,512]{1,0:T(8,128)(2,1)S(1)} collective-permute-done((bf16[256,512]{1,0:T(8,128)(2,1)S(1)}, bf16[256,512]{1,0:T(8,128)(2,1)S(1)}, u32[]{:S(2)}, u32[]{:S(2)}) %collective-permute-start.5) | collective-permute-done | bytes 262176 | tf_op jit(solution)/shard_map/ppermute | solution.py:15
  180.5 2.5 copy.13
  183.0 0.7 constant_dynamic-update-slice_fusion.9
  183.7 0.7 constant_dynamic-update-slice_fusion.8
  184.4 0.2 collective-permute-done.17
  184.7 0.7 constant_dynamic-update-slice_fusion.7
  185.4 1.8 bitcast_bitcast_fusion
  187.2 76.2 %all-gather.8.cloned.1.call-done = bf16[4096,2048]{1,0:T(8,128)(2,1)} async-done(((bf16[256,2048]{1,0:T(8,128)(2,1)}), bf16[4096,2048]{1,0:T(8,128)(2,1)}) %all-gather.8.cloned.1.call-update) | async-done | bytes 16777232 | tf_op jit(solution)/shard_map/all_gather | solution.py:57
  263.4 10.9 %convolution_convert_fusion = bf16[256,2048]{1,0:T(8,128)(2,1)S(1)} fusion(bf16[4096,2048]{1,0:T(8,128)(2,1)} %all-gather.8.cloned.1.call-done, bf16[256,4096]{1,0:T(8,128)(2,1)} %param.8, f32[4096]{0:T(1024)S(1)} %copy-done.1, f32[256]{0:T(256)S(1)} %add_rsqrt_fusion), kind=kOutput, calls=%fused_computation.29 | convolution fusion | flops 4299685888 | bytes 19940352 | tf_op jit(solution)/shard_map/dot_general | solution.py:54
  274.4 1.5 reshape.33
  275.9 1.5 copy.18
  277.4 27.9 %while.11 = (s32[]{:T(128)}, bf16[4,256,4,128]{1,3,2,0:T(8,128)(2,1)}, bf16[4,1792,128]{1,2,0:T(8,128)(2,1)}, bf16[4,1792,128]{2,1,0:T(8,128)(2,1)S(1)}, bf16[4,...) while((s32[]{:T(128)}, ...), condition=%wide.region_4.5_spmd.clone, body=%wide.region_1.4_spmd.clone.sunk | while | flops 960296960 | bytes 25585748 | solution.py:44
  277.4 0.3 broadcast_compare_fusion.2
  277.8 1.3 fusion.48
  279.1 1.6 fusion.49
  280.6 3.7 %fusion.50 = bf16[4,256,4,128]{1,3,2,0:T(8,128)(2,1)} fusion(bf16[4,256,4,128]{1,3,2,0:T(8,128)(2,1)} %get-tuple-element.128, s32[]{:T(128)} %get-tuple-element.127, f32[1792,256,4]{1,0,2:T(8,128)S(1)} %get-tuple-element.117, f32[4,256]{1,0:T(4,128)S(1)} %get-tuple-element.118, pred[256,1792]{0,1:T(8,128)(4,1)S(1)} %broadcast_compare_fusion.2, ...), kind=kOutput, calls=%fused_computation.11.clone.1 | convolution fusion | flops 477233152 | bytes 8791040 | tf_op jit(solution)/shard_map/while/body/eval_jaxpr/gts,sd->tgd/dot_general | solution.py:41
  284.4 0.3 broadcast_compare_fusion.2
  284.7 1.3 fusion.48
  286.0 1.6 fusion.49
  287.6 3.8 %fusion.50 = bf16[4,256,4,128]{1,3,2,0:T(8,128)(2,1)} fusion(bf16[4,256,4,128]{1,3,2,0:T(8,128)(2,1)} %get-tuple-element.128, s32[]{:T(128)} %get-tuple-element.127, f32[1792,256,4]{1,0,2:T(8,128)S(1)} %get-tuple-element.117, f32[4,256]{1,0:T(4,128)S(1)} %get-tuple-element.118, pred[256,1792]{0,1:T(8,128)(4,1)S(1)} %broadcast_compare_fusion.2, ...), kind=kOutput, calls=%fused_computation.11.clone.1 | convolution fusion | flops 477233152 | bytes 8791040 | tf_op jit(solution)/shard_map/while/body/eval_jaxpr/gts,sd->tgd/dot_general | solution.py:41
  291.4 0.3 broadcast_compare_fusion.2
  291.7 1.3 fusion.48
  293.0 1.6 fusion.49
  294.6 3.8 %fusion.50 = bf16[4,256,4,128]{1,3,2,0:T(8,128)(2,1)} fusion(bf16[4,256,4,128]{1,3,2,0:T(8,128)(2,1)} %get-tuple-element.128, s32[]{:T(128)} %get-tuple-element.127, f32[1792,256,4]{1,0,2:T(8,128)S(1)} %get-tuple-element.117, f32[4,256]{1,0:T(4,128)S(1)} %get-tuple-element.118, pred[256,1792]{0,1:T(8,128)(4,1)S(1)} %broadcast_compare_fusion.2, ...), kind=kOutput, calls=%fused_computation.11.clone.1 | convolution fusion | flops 477233152 | bytes 8791040 | tf_op jit(solution)/shard_map/while/body/eval_jaxpr/gts,sd->tgd/dot_general | solution.py:41
  298.3 0.3 broadcast_compare_fusion.2
  298.7 1.3 fusion.48
  300.0 1.6 fusion.49
  301.6 3.7 %fusion.50 = bf16[4,256,4,128]{1,3,2,0:T(8,128)(2,1)} fusion(bf16[4,256,4,128]{1,3,2,0:T(8,128)(2,1)} %get-tuple-element.128, s32[]{:T(128)} %get-tuple-element.127, f32[1792,256,4]{1,0,2:T(8,128)S(1)} %get-tuple-element.117, f32[4,256]{1,0:T(4,128)S(1)} %get-tuple-element.118, pred[256,1792]{0,1:T(8,128)(4,1)S(1)} %broadcast_compare_fusion.2, ...), kind=kOutput, calls=%fused_computation.11.clone.1 | convolution fusion | flops 477233152 | bytes 8791040 | tf_op jit(solution)/shard_map/while/body/eval_jaxpr/gts,sd->tgd/dot_general | solution.py:41
  305.3 2.3 copy.14
  (37 shorter events, 1.6 us)
Async XLA Ops:
  6.5 56.2 %copy-start = (bf16[256,4096]{1,0:T(8,128)(2,1)S(1)}, bf16[256,4096]{1,0:T(8,128)(2,1)}, u32[]{:S(2)}) copy-start(bf16[256,4096]{1,0:T(8,128)(2,1)} %param.8) | copy-start | bytes 6291460
  6.5 56.2 %copy-start.1 = (f32[4096]{0:T(1024)S(1)}, f32[4096]{0:T(1024)}, u32[]{:S(2)}) copy-start(f32[4096]{0:T(1024)} %param.9) | copy-start | bytes 49156
  6.5 56.2 %all-gather.6.cloned.1.call-start = ((), (), s32[]{:S(2)}) async-start(), calls=%async_computation.1 | async-start | bytes 4456448 | tf_op jit(solution)/shard_map/all_gather | solution.py:58
  7.3 112.2 %all-gather.4.cloned.1.call-start = ((), (), s32[]{:S(2)}) async-start(), calls=%async_computation | async-start | bytes 4456448 | tf_op jit(solution)/shard_map/all_gather | solution.py:59
  8.0 255.4 %all-gather.8.cloned.1.call-start = ((), (), s32[]{:S(2)}) async-start(), calls=%async_computation.2 | async-start | bytes 17825792 | tf_op jit(solution)/shard_map/all_gather | solution.py:57
  9.5 16.2 %collective-permute-start.6 = (bf16[256]{0:T(256)(128)(2,1)S(1)}, bf16[256]{0:T(256)(128)(2,1)S(1)}, u32[]{:S(2)}, u32[]{:S(2)}) collective-permute-start(bf16[256]{0:T(256)(128)(2,1)S(1)} %broadcast_bitcast_fusion), channel_id=1, source_target_pairs={{0,3},{1,4},{2,5},{3,6},{4,7},{5,8},{6,9},{7,10},{8,11},{9,12},{10... | collective-permute-start | bytes 1544 | tf_op jit(solution)/shard_map/ppermute | solution.py:15
  14.1 13.1 %collective-permute-start.7 = (bf16[256]{0:T(256)(128)(2,1)S(1)}, bf16[256]{0:T(256)(128)(2,1)S(1)}, u32[]{:S(2)}, u32[]{:S(2)}) collective-permute-start(bf16[256]{0:T(256)(128)(2,1)S(1)} %broadcast_bitcast_fusion), channel_id=1, source_target_pairs={{0,2},{1,3},{2,4},{3,5},{4,6},{5,7},{6,8},{7,9},{8,10},{9,11},{10,... | collective-permute-start | bytes 1544 | tf_op jit(solution)/shard_map/ppermute | solution.py:15
  17.2 10.2 %collective-permute-start.8 = (bf16[256]{0:T(256)(128)(2,1)S(1)}, bf16[256]{0:T(256)(128)(2,1)S(1)}, u32[]{:S(2)}, u32[]{:S(2)}) collective-permute-start(bf16[256]{0:T(256)(128)(2,1)S(1)} %broadcast_bitcast_fusion), channel_id=1, source_target_pairs={{0,1},{1,2},{2,3},{3,4},{4,5},{5,6},{6,7},{7,8},{8,9},{9,10},{10,1... | collective-permute-start | bytes 1544 | tf_op jit(solution)/shard_map/ppermute | solution.py:15
  20.3 7.6 %collective-permute-start.9 = (bf16[256]{0:T(256)(128)(2,1)S(1)}, bf16[256]{0:T(256)(128)(2,1)S(1)}, u32[]{:S(2)}, u32[]{:S(2)}) collective-permute-start(bf16[256]{0:T(256)(128)(2,1)S(1)} %broadcast_bitcast_fusion), channel_id=1, source_target_pairs={{1,0},{2,1},{3,2},{4,3},{5,4},{6,5},{7,6},{8,7},{9,8},{10,9},{11,1... | collective-permute-start | bytes 1544 | tf_op jit(solution)/shard_map/ppermute | solution.py:15
  22.3 5.8 %collective-permute-start.10 = (bf16[256]{0:T(256)(128)(2,1)S(1)}, bf16[256]{0:T(256)(128)(2,1)S(1)}, u32[]{:S(2)}, u32[]{:S(2)}) collective-permute-start(bf16[256]{0:T(256)(128)(2,1)S(1)} %broadcast_bitcast_fusion), channel_id=1, source_target_pairs={{2,0},{3,1},{4,2},{5,3},{6,4},{7,5},{8,6},{9,7},{10,8},{11,9},{12,... | collective-permute-start | bytes 1544 | tf_op jit(solution)/shard_map/ppermute | solution.py:15
  25.7 7.4 %collective-permute-start.11 = (bf16[256]{0:T(256)(128)(2,1)S(1)}, bf16[256]{0:T(256)(128)(2,1)S(1)}, u32[]{:S(2)}, u32[]{:S(2)}) collective-permute-start(bf16[256]{0:T(256)(128)(2,1)S(1)} %broadcast_bitcast_fusion), channel_id=1, source_target_pairs={{3,0},{4,1},{5,2},{6,3},{7,4},{8,5},{9,6},{10,7},{11,8},{12,9},{13... | collective-permute-start | bytes 1544 | tf_op jit(solution)/shard_map/ppermute | solution.py:15
  66.3 56.6 %collective-permute-start.12 = (bf16[256,512]{1,0:T(8,128)(2,1)S(1)}, bf16[256,512]{1,0:T(8,128)(2,1)}, u32[]{:S(2)}, u32[]{:S(2)}) collective-permute-start(bf16[256,512]{1,0:T(8,128)(2,1)S(1)} %convolution_convert_fusion.1), channel_id=1, source_target_pairs={{0,3},{1,4},{2,5},{3,6},{4,7},{5,8},{6,9},{7,10},{8,11},{9,12},{10... | collective-permute-start | bytes 786440 | tf_op jit(solution)/shard_map/ppermute | solution.py:15
  70.3 57.7 %collective-permute-start.13 = (bf16[256,512]{1,0:T(8,128)(2,1)S(1)}, bf16[256,512]{1,0:T(8,128)(2,1)S(1)}, u32[]{:S(2)}, u32[]{:S(2)}) collective-permute-start(bf16[256,512]{1,0:T(8,128)(2,1)S(1)} %convolution_convert_fusion.1), channel_id=1, source_target_pairs={{0,2},{1,3},{2,4},{3,5},{4,6},{5,7},{6,8},{7,9},{8,10},{9,11},{10,... | collective-permute-start | bytes 786440 | tf_op jit(solution)/shard_map/ppermute | solution.py:15
  71.8 59.1 %collective-permute-start.14 = (bf16[256,512]{1,0:T(8,128)(2,1)S(1)}, bf16[256,512]{1,0:T(8,128)(2,1)S(1)}, u32[]{:S(2)}, u32[]{:S(2)}) collective-permute-start(bf16[256,512]{1,0:T(8,128)(2,1)S(1)} %convolution_convert_fusion.1), channel_id=1, source_target_pairs={{0,1},{1,2},{2,3},{3,4},{4,5},{5,6},{6,7},{7,8},{8,9},{9,10},{10,1... | collective-permute-start | bytes 786440 | tf_op jit(solution)/shard_map/ppermute | solution.py:15
  75.4 107.6 %collective-permute-start.15 = (bf16[256,512]{1,0:T(8,128)(2,1)S(1)}, bf16[256,512]{1,0:T(8,128)(2,1)S(1)}, u32[]{:S(2)}, u32[]{:S(2)}) collective-permute-start(bf16[256,512]{1,0:T(8,128)(2,1)S(1)} %convolution_convert_fusion.1), channel_id=1, source_target_pairs={{1,0},{2,1},{3,2},{4,3},{5,4},{6,5},{7,6},{8,7},{9,8},{10,9},{11,1... | collective-permute-start | bytes 786440 | tf_op jit(solution)/shard_map/ppermute | solution.py:15
  77.4 106.4 %collective-permute-start.16 = (bf16[256,512]{1,0:T(8,128)(2,1)S(1)}, bf16[256,512]{1,0:T(8,128)(2,1)S(1)}, u32[]{:S(2)}, u32[]{:S(2)}) collective-permute-start(bf16[256,512]{1,0:T(8,128)(2,1)S(1)} %convolution_convert_fusion.1), channel_id=1, source_target_pairs={{2,0},{3,1},{4,2},{5,3},{6,4},{7,5},{8,6},{9,7},{10,8},{11,9},{12,... | collective-permute-start | bytes 786440 | tf_op jit(solution)/shard_map/ppermute | solution.py:15
  123.0 12.8 %collective-permute-start = (bf16[256,512]{1,0:T(8,128)(2,1)S(1)}, bf16[256,512]{1,0:T(8,128)(2,1)S(1)}, u32[]{:S(2)}, u32[]{:S(2)}) collective-permute-start(bf16[256,512]{1,0:T(8,128)(2,1)S(1)} %convolution_convert_fusion.2), channel_id=1, source_target_pairs={{0,3},{1,4},{2,5},{3,6},{4,7},{5,8},{6,9},{7,10},{8,11},{9,12},{10... | collective-permute-start | bytes 786440 | tf_op jit(solution)/shard_map/ppermute | solution.py:15
  128.0 13.2 %collective-permute-start.1 = (bf16[256,512]{1,0:T(8,128)(2,1)S(1)}, bf16[256,512]{1,0:T(8,128)(2,1)S(1)}, u32[]{:S(2)}, u32[]{:S(2)}) collective-permute-start(bf16[256,512]{1,0:T(8,128)(2,1)S(1)} %convolution_convert_fusion.2), channel_id=1, source_target_pairs={{0,2},{1,3},{2,4},{3,5},{4,6},{5,7},{6,8},{7,9},{8,10},{9,11},{10,... | collective-permute-start | bytes 786440 | tf_op jit(solution)/shard_map/ppermute | solution.py:15
  130.8 21.5 %collective-permute-start.2 = (bf16[256,512]{1,0:T(8,128)(2,1)S(1)}, bf16[256,512]{1,0:T(8,128)(2,1)S(1)}, u32[]{:S(2)}, u32[]{:S(2)}) collective-permute-start(bf16[256,512]{1,0:T(8,128)(2,1)S(1)} %convolution_convert_fusion.2), channel_id=1, source_target_pairs={{0,1},{1,2},{2,3},{3,4},{4,5},{5,6},{6,7},{7,8},{8,9},{9,10},{10,1... | collective-permute-start | bytes 786440 | tf_op jit(solution)/shard_map/ppermute | solution.py:15
  135.8 17.9 %collective-permute-start.3 = (bf16[256,512]{1,0:T(8,128)(2,1)S(1)}, bf16[256,512]{1,0:T(8,128)(2,1)S(1)}, u32[]{:S(2)}, u32[]{:S(2)}) collective-permute-start(bf16[256,512]{1,0:T(8,128)(2,1)S(1)} %convolution_convert_fusion.2), channel_id=1, source_target_pairs={{1,0},{2,1},{3,2},{4,3},{5,4},{6,5},{7,6},{8,7},{9,8},{10,9},{11,1... | collective-permute-start | bytes 786440 | tf_op jit(solution)/shard_map/ppermute | solution.py:15
  141.2 14.1 %collective-permute-start.4 = (bf16[256,512]{1,0:T(8,128)(2,1)S(1)}, bf16[256,512]{1,0:T(8,128)(2,1)S(1)}, u32[]{:S(2)}, u32[]{:S(2)}) collective-permute-start(bf16[256,512]{1,0:T(8,128)(2,1)S(1)} %convolution_convert_fusion.2), channel_id=1, source_target_pairs={{2,0},{3,1},{4,2},{5,3},{6,4},{7,5},{8,6},{9,7},{10,8},{11,9},{12,... | collective-permute-start | bytes 786440 | tf_op jit(solution)/shard_map/ppermute | solution.py:15
  152.3 28.1 %collective-permute-start.5 = (bf16[256,512]{1,0:T(8,128)(2,1)S(1)}, bf16[256,512]{1,0:T(8,128)(2,1)S(1)}, u32[]{:S(2)}, u32[]{:S(2)}) collective-permute-start(bf16[256,512]{1,0:T(8,128)(2,1)S(1)} %convolution_convert_fusion.2), channel_id=1, source_target_pairs={{3,0},{4,1},{5,2},{6,3},{7,4},{8,5},{9,6},{10,7},{11,8},{12,9},{13... | collective-permute-start | bytes 786440 | tf_op jit(solution)/shard_map/ppermute | solution.py:15
  153.7 31.0 %collective-permute-start.17 = (bf16[256,512]{1,0:T(8,128)(2,1)S(1)}, bf16[256,512]{1,0:T(8,128)(2,1)S(1)}, u32[]{:S(2)}, u32[]{:S(2)}) collective-permute-start(bf16[256,512]{1,0:T(8,128)(2,1)S(1)} %convolution_convert_fusion.1), channel_id=1, source_target_pairs={{3,0},{4,1},{5,2},{6,3},{7,4},{8,5},{9,6},{10,7},{11,8},{12,9},{13... | collective-permute-start | bytes 786440 | tf_op jit(solution)/shard_map/ppermute | solution.py:15
Sparse Core Ops, SparseCore 0:
  9.5 53.2 all-gather.5
  64.9 54.4 all-gather.3
  121.6 141.7 all-gather.7
where the time goes:
time: 315 us; the launch traced here: 314 us
  waiting for transfers between devices  192 us (61%)
  starting transfers between devices  42.6 us (14%)
  matrix products  38.2 us (12%)
  local copies, waits for them, and re-layouts  17.3 us (5%)
  between operations  13.4 us (4%)
  other arithmetic  10.4 us (3%)
    all_gather x1, waiting for transfers between devices, on_device(): lax.all_gather(w_query, 'seq', axis=0, tiled=True)  76.2 us
    ppermute x18, waiting for transfers between devices, passed_along(): return lax.ppermute(value, axis, pairs)  43.5 us
    ppermute x18, starting transfers between devices, passed_along(): return lax.ppermute(value, axis, pairs)  42.5 us
    all_gather x1, waiting for transfers between devices, on_device(): lax.all_gather(w_value, 'seq', axis=0, tiled=True)  40.8 us
    all_gather x1, waiting for transfers between devices, on_device(): lax.all_gather(w_key, 'seq', axis=0, tiled=True)  29.6 us
    dot_general x3, matrix products, add_rows(): return jnp.dot(normed, piece, preferred_element_type=jnp.float32)  18 us
    dot_general x4, matrix products, one_head(): jnp.einsum('gts,sd->tgd', rounded, head_values, preferred_element_type=jn...  15 us
    unnamed x22, local copies, waits for them, and re-layouts  6.73 us
  transfers between devices with their start and end apart: 21, of which 8 were waited for; matrix products, arithmetic and copies ran while one was open for 7% of the time, Pallas kernels for 0%

commit v1 on v0

v1 whole, which is shorter than its diff:
```python
import functools

import jax
import jax.numpy as jnp
from jax import lax
from jax.experimental import pallas as pl
from jax.experimental.pallas import tpu as pltpu
from jax.sharding import PartitionSpec as P

HD = 128
MOST_BLK = 7
LANES = 128
AXES = ("groups", "seq")
VMEM_LIMIT = 56 * 1024 * 1024


def normalize(tokens, norm_gain):
    widened = tokens.astype(jnp.float32)
    inverse = lax.rsqrt(jnp.mean(widened * widened, axis=-1, keepdims=True) + 1e-05)
    return (widened * inverse * norm_gain).astype(jnp.bfloat16)


def swap(value, team, group_bits, layer_bits, member_bits):
    groups, peers = lax.axis_size("groups"), lax.axis_size("seq")
    pairs = []
    for g in range(groups):
        for s in range(peers):
            layer, member = divmod(s, team)
            to = (layer ^ layer_bits) * team + (member ^ member_bits)
            pairs.append((g * peers + s, (g ^ group_bits) * peers + to))
    return lax.ppermute(value, AXES, pairs)


def from_layer(value, team, by):
    groups, peers = lax.axis_size("groups"), lax.axis_size("seq")
    pairs = []
    for g in range(groups):
        for s in range(peers):
            to = s - by * team
            if 0 <= to < peers:
                pairs.append((g * peers + s, g * peers + to))
    return lax.ppermute(value, AXES, pairs)


def gather_columns(blocks, team, place):
    groups = lax.axis_size("groups")
    layers = lax.axis_size("seq") // team
    group = place[0]
    depth = blocks[0].shape[0]
    part = depth // groups

    def share(value):
        return lax.dynamic_slice_in_dim(value, group * part, part, 0)

    near = swap(blocks[1], team, 0, 0, 1)
    far = [swap(share(blocks[r]), team, 0, 0, r) for r in range(2, team)]
    far = jnp.concatenate(far, axis=0)
    held = {(0, 0): jnp.concatenate([share(blocks[0]), share(near), far], axis=0)}
    found = [
        (blocks[0], [(0, 0, None)]),
        (near, [(0, 1, None)]),
        (far, [(0, r, 0) for r in range(2, team)]),
    ]
    for bits in range(1, layers):
        low = bits & -bits
        held[(bits, 0)] = swap(held[(bits ^ low, 0)], team, 0, low, 0)
        found.append((held[(bits, 0)], [(bits, r, 0) for r in range(team)]))
    for other in range(1, groups):
        found.append(
            (swap(far, team, other, 0, 0), [(0, r, other) for r in range(2, team)])
        )
        for bits in range(1, layers):
            moved = swap(held[(bits, 0)], team, other, 0, 0)
            found.append((moved, [(bits, r, other) for r in range(team)]))
    return found


def project_kernel(pieces, team, groups, depth, place, *refs):
    token_refs = refs[:team]
    weight_refs = refs[team : team + len(pieces)]
    out_ref = refs[team + len(pieces)]
    tokens, weights, total, token_sems, weight_sems = refs[team + len(pieces) + 1 :]
    rows = token_refs[0].shape[0]
    part = depth // groups
    group, layer, member = place[0], place[1], place[2]
    token_copies = [
        pltpu.make_async_copy(
            token_refs[t], tokens.at[pl.ds(t * rows, rows)], token_sems.at[t]
        )
        for t in range(team)
    ]
    weight_copies = []
    offset = 0
    spans = []
    for i, ref in enumerate(weight_refs):
        spans.append((offset, ref.shape[0]))
        weight_copies.append(
            pltpu.make_async_copy(
                ref, weights.at[pl.ds(offset, ref.shape[0])], weight_sems.at[i]
            )
        )
        offset += ref.shape[0]
    for copy in token_copies:
        copy.start()
    for copy in weight_copies:
        copy.start()
    for copy in token_copies:
        copy.wait()
    for i, described in enumerate(pieces):
        weight_copies[i].wait()
        columns = []
        for layer_bits, member_bits, group_bits in described:
            owner = (layer ^ layer_bits) * team + (member ^ member_bits)
            first, length = owner * depth, depth
            if group_bits is not None:
                first, length = first + (group ^ group_bits) * part, part
            columns.append(
                tokens[:, pl.ds(pl.multiple_of(first, LANES), length)]
            )
        left = columns[0] if len(columns) == 1 else jnp.concatenate(columns, axis=1)
        start, length = spans[i]
        term = jnp.dot(
            left, weights[pl.ds(start, length), :], preferred_element_type=jnp.float32
        )
        if i == 0:
            total[...] = term
        else:
            total[...] += term
    for t in range(team):
        first = pl.multiple_of((member ^ t) * rows, rows)
        out_ref[pl.ds(first, rows), :] = total[pl.ds(t * rows, rows), :].astype(
            jnp.bfloat16
        )


def project(place, team_tokens, found, groups, depth):
    team = len(team_tokens)
    rows, width = team_tokens[0].shape
    arrays = [array for array, _ in found]
    pieces = [described for _, described in found]
    columns = arrays[0].shape[1]
    kernel = functools.partial(project_kernel, pieces, team, groups, depth)
    return pl.pallas_call(
        kernel,
        out_shape=jax.ShapeDtypeStruct((team * rows, columns), jnp.bfloat16),
        in_specs=[pl.BlockSpec(memory_space=pltpu.SMEM)]
        + [pl.BlockSpec(memory_space=pl.ANY)] * (team + len(arrays)),
        out_specs=pl.BlockSpec(memory_space=pltpu.VMEM),
        scratch_shapes=[
            pltpu.VMEM((team * rows, width), jnp.bfloat16),
            pltpu.VMEM((width, columns), jnp.bfloat16),
            pltpu.VMEM((team * rows, columns), jnp.float32),
            pltpu.SemaphoreType.DMA((team,)),
            pltpu.SemaphoreType.DMA((len(arrays),)),
        ],
        compiler_params=pltpu.CompilerParams(vmem_limit_bytes=VMEM_LIMIT),
        cost_estimate=pl.CostEstimate(
            flops=2 * team * rows * width * columns,
            bytes_accessed=2 * (team * rows * (width + columns) + width * columns),
            transcendentals=0,
        ),
        name="project",
    )(place, *team_tokens, *arrays)


def attend_kernel(heads, most, first_ref, count_ref, q_ref, before, own, after, out_ref,
                  window, sems):
    step = pl.program_id(0)
    block = q_ref.shape[0]

    @pl.when(step == 0)
    def _():
        copies = []
        offset = 0
        for i, ref in enumerate((before, own, after)):
            copies.append(
                pltpu.make_async_copy(
                    ref, window.at[pl.ds(offset, ref.shape[0])], sems.at[i]
                )
            )
            offset += ref.shape[0]
        for copy in copies:
            copy.start()
        for copy in copies:
            copy.wait()

    first = pl.multiple_of(first_ref[step] * block, block)
    keys = window[pl.ds(first, most * block), :HD]
    values = window[pl.ds(first, most * block), HD:]
    column = lax.broadcasted_iota(jnp.int32, (block, most * block), 1)
    allowed = column < count_ref[step] * block
    for h in range(heads):
        query = q_ref[:, h * HD : (h + 1) * HD]
        scores = lax.dot_general(
            query, keys, (((1,), (1,)), ((), ())), preferred_element_type=jnp.float32
        ) * HD ** (-0.5)
        scores = jnp.where(allowed, scores, -1e30)
        weights = jnp.exp(scores - jnp.max(scores, axis=-1, keepdims=True))
        row_total = jnp.sum(weights, axis=-1, keepdims=True)
        mixed = jnp.dot(
            weights.astype(jnp.bfloat16), values, preferred_element_type=jnp.float32
        )
        out_ref[:, h * HD : (h + 1) * HD] = (mixed / row_total).astype(jnp.bfloat16)


def attend(first, count, query, before, own, after, block):
    rows, columns = query.shape
    heads = columns // HD
    span = before.shape[0] + own.shape[0] + after.shape[0]
    return pl.pallas_call(
        functools.partial(attend_kernel, heads, MOST_BLK),
        out_shape=jax.ShapeDtypeStruct((rows, columns), jnp.bfloat16),
        grid_spec=pltpu.PrefetchScalarGridSpec(
            num_scalar_prefetch=2,
            grid=(rows // block,),
            in_specs=[
                pl.BlockSpec((block, columns), lambda i, *_: (i, 0)),
                pl.BlockSpec(memory_space=pl.ANY),
                pl.BlockSpec(memory_space=pl.ANY),
                pl.BlockSpec(memory_space=pl.ANY),
            ],
            out_specs=pl.BlockSpec((block, columns), lambda i, *_: (i, 0)),
            scratch_shapes=[
                pltpu.VMEM((span, own.shape[1]), jnp.bfloat16),
                pltpu.SemaphoreType.DMA((3,)),
            ],
        ),
        compiler_params=pltpu.CompilerParams(vmem_limit_bytes=VMEM_LIMIT),
        cost_estimate=pl.CostEstimate(
            flops=4 * rows * MOST_BLK * block * columns,
            bytes_accessed=4 * rows * columns + 2 * span * own.shape[1],
            transcendentals=rows * MOST_BLK * block * heads,
        ),
        name="attend",
    )(first, count, query, before, own, after)


def on_device(tokens, norm_gain, w_query, w_key, w_value, passage_blocks):
    groups, peers = lax.axis_size("groups"), lax.axis_size("seq")
    team = w_key.shape[1] // HD
    depth = w_key.shape[0]
    rows = tokens.shape[0]
    blocks = passage_blocks.shape[0]
    block = rows // blocks
    index = lax.axis_index("seq")
    group, layer, member = lax.axis_index("groups"), index // team, index % team
    place = jnp.stack([group, layer, member]).astype(jnp.int32)
    q_columns = w_query.shape[1] // team

    def columns_of(weight, r):
        width = weight.shape[1] // team
        return lax.dynamic_slice_in_dim(weight, (member ^ r) * width, width, 1)

    kv_blocks = [
        jnp.concatenate([columns_of(w_key, r), columns_of(w_value, r)], axis=1)
        for r in range(team)
    ]
    q_blocks = [columns_of(w_query, r) for r in range(team)]

    normed = normalize(tokens, norm_gain)
    near = swap(normed, team, 0, 0, 1)
    far = [swap(normed, team, 0, 0, 2)]
    far.append(swap(far[0], team, 0, 0, 1))
    team_tokens = [normed, near] + far

    if depth // groups % LANES == 0:
        kv_found = gather_columns(kv_blocks, team, place)
        q_found = gather_columns(q_blocks, team, place)
        keys_values = project(place, team_tokens, kv_found, groups, depth)
        query = project(place, team_tokens, q_found, groups, depth)
    else:
        in_order = [None] * team
        stacked = jnp.stack(team_tokens)
        in_order = jnp.concatenate(
            [lax.dynamic_index_in_dim(stacked, member ^ t, 0, False) for t in range(team)]
        )

        def whole(weight):
            full = lax.all_gather(weight, "seq", axis=0, tiled=True)
            return columns_of(full, 0)

        def dense(weight):
            product = jnp.dot(in_order, weight, preferred_element_type=jnp.float32)
            return product.astype(jnp.bfloat16)

        keys_values = jnp.concatenate([dense(whole(w_key)), dense(whole(w_value))], axis=1)
        query = dense(whole(w_query))

    margin = (MOST_BLK - 1) * block
    before = from_layer(keys_values[-margin:], team, -1)
    after = from_layer(keys_values[:margin], team, 1)

    ids = lax.all_gather(passage_blocks, "seq", axis=0, tiled=True)
    mine = lax.dynamic_slice_in_dim(ids, layer * team * blocks, team * blocks, 0)
    same = mine[:, None] == ids[None, :]
    count = jnp.sum(same.astype(jnp.int32), axis=1)
    first = jnp.sum((ids[None, :] < mine[:, None]).astype(jnp.int32), axis=1)
    first = first - layer * team * blocks + (MOST_BLK - 1)

    attended = attend(first, count, query, before, keys_values, after, block)

    def rows_of(r):
        return lax.dynamic_slice_in_dim(attended, (member ^ r) * rows, rows, 0)

    out = jnp.zeros((rows, w_query.shape[1]), jnp.bfloat16)
    for r in range(team):
        piece = rows_of(r)
        if r:
            piece = swap(piece, team, 0, 0, r)
        out = lax.dynamic_update_slice(out, piece, (0, (member ^ r) * q_columns))
    return out


def solution(mesh):
    in_specs = (
        P(("groups", "seq"), None),
        P(),
        P("seq", None),
        P("seq", None),
        P("seq", None),
        P(("groups", "seq")),
    )
    out_specs = P(("groups", "seq"), None)
    return jax.shard_map(
        on_device, mesh=mesh, in_specs=in_specs, out_specs=out_specs, check_vma=False
    )
```

time: 315 us -> 217 us (0.69)
  waiting for transfers between devices: 192 us -> 105 us
  matrix products: 38.2 us -> 0 us
  Pallas kernels: 0 us -> 37.7 us
  blocking collectives: 0 us -> 14.6 us
  between operations: 13.4 us -> 1.04 us
  local copies, waits for them, and re-layouts: 17.3 us -> 10.9 us
  starting transfers between devices: 42.6 us -> 38 us
    all_gather x3 -> x0, waiting for transfers between devices: 147 us -> none  [the longest x1 76.2 us: on_device(): lax.all_gather(w_query, 'seq', axis=0, tiled=True)]
    ppermute x18 -> x28, waiting for transfers between devices: 43.5 us -> 105 us  [the longest x26 105 us: swap(): return lax.ppermute(value, AXES, pairs)]
    dot_general x11 -> x0, matrix products: 38.2 us -> none  [the longest x3 18 us: add_rows(): return jnp.dot(normed, piece, preferred_element_type=jnp.float32)]
    pallas_call x0 -> x3, Pallas kernels: none -> 37.7 us  [the longest x2 21.6 us: project(): pl.pallas_call(kernel, out_shape=jax.ShapeDtypeStruct((team * rows, colum...]
    unnamed x0 -> x1, blocking collectives: none -> 14.6 us
    reshape x3 -> x0, local copies, waits for them, and re-layouts: 5.55 us -> none  [the longest x2 3.04 us: on_device(): query_rounded.reshape(row_count, KVH, QH // KVH, HD).transpose(1, 0, 2, 3)]
    reduce_sum x4 -> x1, other arithmetic: 6.23 us -> 0.77 us  [on_device(): count = jnp.sum(same.astype(jnp.int32), axis=1)]
    dynamic_slice x0 -> x7, local copies, waits for them, and re-layouts: none -> 5.13 us  [the longest x2 2.6 us: columns_of(): return lax.dynamic_slice_in_dim(weight, (member ^ r) * width, width, 1)]
  transfers between devices with their start and end apart: 21 -> 28, of which waited for: 8 -> 10; matrix products, arithmetic and copies ran while one was open for 7% -> 6% of each run, Pallas kernels for 0% -> 10%
where the time goes in v1:
time: 217 us; the launch traced here: 216 us
  waiting for transfers between devices  105 us (48%)
  starting transfers between devices  38 us (18%)
  Pallas kernels  37.7 us (17%)
  blocking collectives  14.6 us (7%)
  local copies, waits for them, and re-layouts  10.9 us (5%)
  other arithmetic  9.2 us (4%)
    ppermute x26, waiting for transfers between devices, swap(): return lax.ppermute(value, AXES, pairs)  105 us
    ppermute x26, starting transfers between devices, swap(): return lax.ppermute(value, AXES, pairs)  33.5 us
    pallas_call x2, Pallas kernels, project(): pl.pallas_call(kernel, out_shape=jax.ShapeDtypeStruct((team * rows, colum...  21.6 us
    pallas_call x1, Pallas kernels, attend(): pl.pallas_call(functools.partial(attend_kernel, heads, MOST_BLK), out_sha...  16.1 us
    unnamed x1, blocking collectives  14.6 us
    ppermute x2, starting transfers between devices, from_layer(): return lax.ppermute(value, AXES, pairs)  4.57 us
  transfers between devices with their start and end apart: 28, of which 10 were waited for; matrix products, arithmetic and copies ran while one was open for 6% of the time, Pallas kernels for 10%

profile of v1, /device:TPU:1, one launch (start us, length us, event | category | flops | bytes accessed | tf_op | source)
XLA Modules:
  0.0 216.4 jit_solution(14167340065801768409)
XLA Ops:
  0.0 2.2 %fusion = f32[256]{0:T(256)S(1)} fusion(bf16[256,4096]{1,0:T(8,128)(2,1)} %param.6), kind=kLoop, calls=%fused_computation.2 | loop fusion | flops 3145472 | bytes 2098176 | tf_op jit(solution)/shard_map/reduce_sum | solution.py:19
  2.3 1.4 fusion.2.refs_0_
  3.7 2.1 collective-permute-start.1
  5.9 1.0 collective-permute-start
  6.8 0.8 constant_dynamic-slice_fusion.13
  7.7 1.8 constant_dynamic-slice_fusion.4
  9.4 0.7 pad_maximum_fusion.3
  10.1 0.5 collective-permute-start.13
  10.6 1.4 fusion.4
  12.0 0.2 fusion.6
  12.3 39.1 %collective-permute-done.1.refs_2_ = bf16[256,4096]{1,0:T(8,128)(2,1)} collective-permute-done((bf16[256,4096]{1,0:T(8,128)(2,1)S(1)}, bf16[256,4096]{1,0:T(8,128)(2,1)}, u32[]{:S(2)}, u32[]{:S(2)}) %collective-permute-start.1) | collective-permute-done | bytes 2097184 | tf_op jit(solution)/shard_map/ppermute | solution.py:31
  51.3 1.9 collective-permute-start.2
  53.3 2.0 collective-permute-start.15
  55.3 0.8 constant_dynamic-update-slice_fusion.3
  56.1 1.5 collective-permute-done.15
  57.7 1.6 collective-permute-start.4
  59.3 0.4 collective-permute-start.5
  59.8 0.9 pad_maximum_fusion.1
  60.7 1.7 collective-permute-start.19
  62.3 0.9 constant_dynamic-slice_fusion.12
  63.3 1.4 collective-permute-start.16
  64.6 1.5 collective-permute-done.5
  66.2 2.5 %collective-permute-start.17 = (bf16[512,256]{1,0:T(8,128)(2,1)S(1)}, bf16[512,256]{1,0:T(8,128)(2,1)}, u32[]{:S(2)}, u32[]{:S(2)}) collective-permute-start(bf16[512,256]{1,0:T(8,128)(2,1)S(1)} %pad_maximum_fusion.1), channel_id=1, source_target_pairs={{0,8},{1,9},{2,10},{3,11},{4,12},{5,13},{6,14},{7,15},{8,0},{9,1},... | collective-permute-start | bytes 786440 | tf_op jit(solution)/shard_map/ppermute | solution.py:31
  68.8 23.3 %collective-permute-done.17.refs_8_ = bf16[512,256]{1,0:T(8,128)(2,1)} collective-permute-done((bf16[512,256]{1,0:T(8,128)(2,1)S(1)}, bf16[512,256]{1,0:T(8,128)(2,1)}, u32[]{:S(2)}, u32[]{:S(2)}) %collective-permute-start.17) | collective-permute-done | bytes 262176 | tf_op jit(solution)/shard_map/ppermute | solution.py:31
  92.1 0.8 collective-permute-start.18
  92.9 1.2 collective-permute-start.20
  94.2 0.6 dynamic-slice
  95.4 0.2 dynamic-update-slice
  95.7 14.6 %all-reduce = s32[32]{0:T(128)S(1)} all-reduce(s32[32]{0:T(128)S(1)} %dynamic-update-slice), channel_id=1, replica_groups=mesh['groups'=2,'seq'=16] {'seq'}, use_global_device_ids=true, to_apply=%add | all-reduce | flops 32 | bytes 256
  110.3 0.1 dynamic_slice.71
  110.4 1.3 collective-permute-start.21
  111.6 0.8 convert_reduce_fusion
  112.4 3.8 %collective-permute-start.6 = (bf16[512,512]{1,0:T(8,128)(2,1)S(1)}, bf16[512,512]{1,0:T(8,128)(2,1)}, u32[]{:S(2)}, u32[]{:S(2)}) collective-permute-start(bf16[512,512]{1,0:T(8,128)(2,1)S(1)} %pad_maximum_fusion), channel_id=1, source_target_pairs={{0,4},{1,5},{2,6},{3,7},{4,0},{5,1},{6,2},{7,3},{8,12},{9,13},{10,... | collective-permute-start | bytes 1572872 | tf_op jit(solution)/shard_map/ppermute | solution.py:31
  116.3 0.5 subtract_add_fusion.first_ref
  116.8 0.7 collective-permute-done.21.refs_12_
  117.4 1.3 collective-permute-start.22
  118.7 0.6 pad_add_fusion.place
  119.3 0.7 pad_maximum_fusion.2.refs_4_
  120.0 7.0 %collective-permute-done.6.refs_7_ = bf16[512,512]{1,0:T(8,128)(2,1)} collective-permute-done((bf16[512,512]{1,0:T(8,128)(2,1)S(1)}, bf16[512,512]{1,0:T(8,128)(2,1)}, u32[]{:S(2)}, u32[]{:S(2)}) %collective-permute-start.6) | collective-permute-done | bytes 524320 | tf_op jit(solution)/shard_map/ppermute | solution.py:31
  126.9 0.3 collective-permute-start.11
  127.2 1.2 collective-permute-start.10
  128.4 9.8 %collective-permute-done.8.refs_9_ = bf16[512,512]{1,0:T(8,128)(2,1)} collective-permute-done((bf16[512,512]{1,0:T(8,128)(2,1)}, bf16[512,512]{1,0:T(8,128)(2,1)}, u32[]{:S(2)}, u32[]{:S(2)}) %collective-permute-start.8) | collective-permute-done | bytes 524320 | tf_op jit(solution)/shard_map/ppermute | solution.py:31
  138.2 0.3 collective-permute-start.12
  138.5 1.3 collective-permute-start.9
  139.8 10.3 %project.3.own = bf16[1024,256]{1,0:T(8,128)(2,1)} custom-call(s32[3]{0:T(128)} %pad_add_fusion.place, bf16[256,4096]{1,0:T(8,128)(2,1)} %copy-done.1, bf16[256,4096]{1,0:T(8,128)(2,1)} %collective-permute-done.refs_1_, bf16[256,4096]{1,0:T(8,128)(2,1)} %collective-permute-done.1.refs_2_, bf16[256,4096]{1,0:T(8,128)(2,1)} %collective-permute-done.2.refs_3_, ...), custom_call_target="tpu_custom_call" | custom-call | flops 2147483648 | bytes 11010048 | tf_op jit(solution)/shard_map/project/pallas_call | solution.py:143
  150.1 1.2 fusion.7
  151.3 3.1 %collective-permute-start.23 = (bf16[768,256]{1,0:T(8,128)(2,1)S(1)}, bf16[768,256]{1,0:T(8,128)(2,1)S(1)}, u32[]{:S(2)}, u32[]{:S(2)}) collective-permute-start(bf16[768,256]{1,0:T(8,128)(2,1)S(1)} %get-tuple-element.17), channel_id=1, source_target_pairs={{0,4},{1,5},{2,6},{3,7},{4,8},{5,9},{6,10},{7,11},{8,12},{9,13},{1... | collective-permute-start | bytes 1179656 | tf_op jit(solution)/shard_map/ppermute | solution.py:42
  154.4 10.2 %collective-permute-done.9.refs_10_ = bf16[256,512]{1,0:T(8,128)(2,1)S(1)} collective-permute-done((bf16[256,512]{1,0:T(8,128)(2,1)S(1)}, bf16[256,512]{1,0:T(8,128)(2,1)S(1)}, u32[]{:S(2)}, u32[]{:S(2)}) %collective-permute-start.9) | collective-permute-done | bytes 262176 | tf_op jit(solution)/shard_map/ppermute | solution.py:31
  164.6 1.5 collective-permute-start.24
  166.1 0.7 copy-done.9
  166.9 0.2 copy-done.8
  167.1 0.2 copy-done.10
  167.3 11.3 %project.2.q_ref = bf16[1024,512]{1,0:T(8,128)(2,1)} custom-call(s32[3]{0:T(128)} %pad_add_fusion.place, bf16[256,4096]{1,0:T(8,128)(2,1)} %copy-done.1, bf16[256,4096]{1,0:T(8,128)(2,1)} %collective-permute-done.refs_1_, bf16[256,4096]{1,0:T(8,128)(2,1)} %collective-permute-done.1.refs_2_, bf16[256,4096]{1,0:T(8,128)(2,1)} %collective-permute-done.2.refs_3_, ...), custom_call_target="tpu_custom_call" | custom-call | flops 4294967296 | bytes 13631488 | tf_op jit(solution)/shard_map/project/pallas_call | solution.py:143
  178.6 0.7 copy-done.11
  179.3 0.1 copy-done.12
  179.4 16.1 %attend.1 = bf16[1024,512]{1,0:T(8,128)(2,1)} custom-call(s32[8]{0:T(128)} %subtract_add_fusion.first_ref, s32[8]{0:T(128)} %get-tuple-element.5.count_ref, bf16[1024,512]{1,0:T(8,128)(2,1)} %project.2.q_ref, bf16[768,256]{1,0:T(8,128)(2,1)} %copy-done.11, bf16[1024,256]{1,0:T(8,128)(2,1)} %project.3.own, bf16[768,256]{1,0:T(8,128)(2,1)} %copy-done.12), custom_call_target="tpu_custom_call" | custom-call | flops 1879048192 | bytes 3407872 | tf_op jit(solution)/shard_map/attend/pallas_call | solution.py:210
  195.6 0.1 broadcast_in_dim.2
  195.7 1.3 constant_dynamic-slice_fusion
  197.0 5.1 %collective-permute-start.25 = (bf16[256,512]{1,0:T(8,128)(2,1)S(1)}, bf16[256,512]{1,0:T(8,128)(2,1)S(1)}, u32[]{:S(2)}, u32[]{:S(2)}) collective-permute-start(bf16[256,512]{1,0:T(8,128)(2,1)S(1)} %get-tuple-element.9), channel_id=1, source_target_pairs={{0,1},{1,0},{2,3},{3,2},{4,5},{5,4},{6,7},{7,6},{8,9},{9,8},{10,11... | collective-permute-start | bytes 786440 | tf_op jit(solution)/shard_map/ppermute | solution.py:31
  202.1 1.3 collective-permute-start.26
  203.3 0.5 collective-permute-start.27
  203.8 6.1 %collective-permute-done.26 = bf16[256,512]{1,0:T(8,128)(2,1)S(1)} collective-permute-done((bf16[256,512]{1,0:T(8,128)(2,1)S(1)}, bf16[256,512]{1,0:T(8,128)(2,1)S(1)}, u32[]{:S(2)}, u32[]{:S(2)}) %collective-permute-start.26) | collective-permute-done | bytes 262176 | tf_op jit(solution)/shard_map/ppermute | solution.py:31
  210.0 5.7 %collective-permute-done.27 = bf16[256,512]{1,0:T(8,128)(2,1)S(1)} collective-permute-done((bf16[256,512]{1,0:T(8,128)(2,1)S(1)}, bf16[256,512]{1,0:T(8,128)(2,1)S(1)}, u32[]{:S(2)}, u32[]{:S(2)}) %collective-permute-start.27) | collective-permute-done | bytes 262176 | tf_op jit(solution)/shard_map/ppermute | solution.py:31
  215.7 0.7 constant_dynamic-update-slice_fusion.4
  (60 shorter events, 0.4 us)
Async XLA Ops:
  0.0 2.2 %copy-start = (bf16[256,4096]{1,0:T(8,128)(2,1)S(1)}, bf16[256,4096]{1,0:T(8,128)(2,1)}, u32[]{:S(2)}) copy-start(bf16[256,4096]{1,0:T(8,128)(2,1)} %param.6) | copy-start | bytes 6291460
  2.3 4.6 %copy-start.3 = (bf16[256,2048]{1,0:T(8,128)(2,1)S(1)}, bf16[256,2048]{1,0:T(8,128)(2,1)}, u32[]{:S(2)}) copy-start(bf16[256,2048]{1,0:T(8,128)(2,1)} %param.8) | copy-start | bytes 3145732
  3.7 56.1 %copy-start.1 = (bf16[256,4096]{1,0:T(8,128)(2,1)}, bf16[256,4096]{1,0:T(8,128)(2,1)S(1)}, u32[]{:S(2)}) copy-start(bf16[256,4096]{1,0:T(8,128)(2,1)S(1)} %fusion.2.refs_0_) | copy-start | bytes 6291460
  3.7 47.6 %collective-permute-start.1 = (bf16[256,4096]{1,0:T(8,128)(2,1)S(1)}, bf16[256,4096]{1,0:T(8,128)(2,1)}, u32[]{:S(2)}, u32[]{:S(2)}) collective-permute-start(bf16[256,4096]{1,0:T(8,128)(2,1)S(1)} %fusion.2.refs_0_), channel_id=1, source_target_pairs={{0,2},{1,3},{2,0},{3,1},{4,6},{5,7},{6,4},{7,5},{8,10},{9,11},{10,... | collective-permute-start | bytes 6291464 | tf_op jit(solution)/shard_map/ppermute | solution.py:31
  5.9 132.6 %collective-permute-start = (bf16[256,4096]{1,0:T(8,128)(2,1)S(1)}, bf16[256,4096]{1,0:T(8,128)(2,1)}, u32[]{:S(2)}, u32[]{:S(2)}) collective-permute-start(bf16[256,4096]{1,0:T(8,128)(2,1)S(1)} %fusion.2.refs_0_), channel_id=1, source_target_pairs={{0,1},{1,0},{2,3},{3,2},{4,5},{5,4},{6,7},{7,6},{8,9},{9,8},{10,11... | collective-permute-start | bytes 6291464 | tf_op jit(solution)/shard_map/ppermute | solution.py:31
  7.6 53.0 %collective-permute-start.3 = (bf16[256,512]{1,0:T(8,128)(2,1)}, bf16[256,512]{1,0:T(8,128)(2,1)}, u32[]{:S(2)}, u32[]{:S(2)}) collective-permute-start(bf16[256,512]{1,0:T(8,128)(2,1)} %get-tuple-element.14), channel_id=1, source_target_pairs={{0,1},{1,0},{2,3},{3,2},{4,5},{5,4},{6,7},{7,6},{8,9},{9,8},{10,11... | collective-permute-start | bytes 786440 | tf_op jit(solution)/shard_map/ppermute | solution.py:31
  9.4 84.7 %copy-start.15 = (u32[32]{0:T(128)S(1)}, u32[32]{0:T(128)}, u32[]{:S(2)}) copy-start(u32[32]{0:T(128)} %constant.98) | copy-start | bytes 388
  9.4 86.0 %copy-start.14 = (s32[2]{0:T(128)S(1)}, s32[2]{0:T(128)}, u32[]{:S(2)}) copy-start(s32[2]{0:T(128)} %param.11) | copy-start | bytes 28
  10.1 49.2 %collective-permute-start.13 = (bf16[256,256]{1,0:T(8,128)(2,1)}, bf16[256,256]{1,0:T(8,128)(2,1)S(1)}, u32[]{:S(2)}, u32[]{:S(2)}) collective-permute-start(bf16[256,256]{1,0:T(8,128)(2,1)} %pad_maximum_fusion.3), channel_id=1, source_target_pairs={{0,1},{1,0},{2,3},{3,2},{4,5},{5,4},{6,7},{7,6},{8,9},{9,8},{10,11... | collective-permute-start | bytes 393224 | tf_op jit(solution)/shard_map/ppermute | solution.py:31
  12.0 41.3 %collective-permute-start.14 = (bf16[128,256]{1,0:T(8,128)(2,1)}, bf16[128,256]{1,0:T(8,128)(2,1)}, u32[]{:S(2)}, u32[]{:S(2)}) collective-permute-start(bf16[128,256]{1,0:T(8,128)(2,1)} %fusion.4), channel_id=1, source_target_pairs={{0,2},{1,3},{2,0},{3,1},{4,6},{5,7},{6,4},{7,5},{8,10},{9,11},{10,... | collective-permute-start | bytes 196616 | tf_op jit(solution)/shard_map/ppermute | solution.py:31
  51.3 88.4 %collective-permute-start.2 = (bf16[256,4096]{1,0:T(8,128)(2,1)}, bf16[256,4096]{1,0:T(8,128)(2,1)}, u32[]{:S(2)}, u32[]{:S(2)}) collective-permute-start(bf16[256,4096]{1,0:T(8,128)(2,1)} %collective-permute-done.1.refs_2_), channel_id=1, source_target_pairs={{0,1},{1,0},{2,3},{3,2},{4,5},{5,4},{6,7},{7,6},{8,9},{9,8},{10,11... | collective-permute-start | bytes 6291464 | tf_op jit(solution)/shard_map/ppermute | solution.py:31
  53.3 4.4 %collective-permute-start.15 = (bf16[128,256]{1,0:T(8,128)(2,1)S(1)}, bf16[128,256]{1,0:T(8,128)(2,1)S(1)}, u32[]{:S(2)}, u32[]{:S(2)}) collective-permute-start(bf16[128,256]{1,0:T(8,128)(2,1)S(1)} %fusion.3), channel_id=1, source_target_pairs={{0,3},{1,2},{2,1},{3,0},{4,7},{5,6},{6,5},{7,4},{8,11},{9,10},{10,... | collective-permute-start | bytes 196616 | tf_op jit(solution)/shard_map/ppermute | solution.py:31
  57.7 5.6 %collective-permute-start.4 = (bf16[128,512]{1,0:T(8,128)(2,1)S(1)}, bf16[128,512]{1,0:T(8,128)(2,1)S(1)}, u32[]{:S(2)}, u32[]{:S(2)}) collective-permute-start(bf16[128,512]{1,0:T(8,128)(2,1)S(1)} %get-tuple-element.12), channel_id=1, source_target_pairs={{0,2},{1,3},{2,0},{3,1},{4,6},{5,7},{6,4},{7,5},{8,10},{9,11},{10,... | collective-permute-start | bytes 393224 | tf_op jit(solution)/shard_map/ppermute | solution.py:31
  59.3 80.4 %copy-start.5 = (bf16[256,256]{1,0:T(8,128)(2,1)}, bf16[256,256]{1,0:T(8,128)(2,1)S(1)}, u32[]{:S(2)}) copy-start(bf16[256,256]{1,0:T(8,128)(2,1)S(1)} %constant_dynamic-update-slice_fusion.2.refs_6_) | copy-start | bytes 393220
  59.3 80.4 %copy-start.4 = (bf16[256,256]{1,0:T(8,128)(2,1)}, bf16[256,256]{1,0:T(8,128)(2,1)S(1)}, u32[]{:S(2)}) copy-start(bf16[256,256]{1,0:T(8,128)(2,1)S(1)} %collective-permute-done.13.refs_5_) | copy-start | bytes 393220
  59.3 6.8 %collective-permute-start.5 = (bf16[128,512]{1,0:T(8,128)(2,1)S(1)}, bf16[128,512]{1,0:T(8,128)(2,1)S(1)}, u32[]{:S(2)}, u32[]{:S(2)}) collective-permute-start(bf16[128,512]{1,0:T(8,128)(2,1)S(1)} %get-tuple-element.13), channel_id=1, source_target_pairs={{0,3},{1,2},{2,1},{3,0},{4,7},{5,6},{6,5},{7,4},{8,11},{9,10},{10,... | collective-permute-start | bytes 393224 | tf_op jit(solution)/shard_map/ppermute | solution.py:31
  60.7 8.1 %collective-permute-start.19 = (bf16[256,256]{1,0:T(8,128)(2,1)S(1)}, bf16[256,256]{1,0:T(8,128)(2,1)S(1)}, u32[]{:S(2)}, u32[]{:S(2)}) collective-permute-start(bf16[256,256]{1,0:T(8,128)(2,1)S(1)} %constant_dynamic-update-slice_fusion.2.refs_6_), channel_id=1, source_target_pairs={{0,16},{1,17},{2,18},{3,19},{4,20},{5,21},{6,22},{7,23},{8,24},{9,... | collective-permute-start | bytes 393224 | tf_op jit(solution)/shard_map/ppermute | solution.py:31
  63.3 29.7 %collective-permute-start.16 = (bf16[512,256]{1,0:T(8,128)(2,1)S(1)}, bf16[512,256]{1,0:T(8,128)(2,1)}, u32[]{:S(2)}, u32[]{:S(2)}) collective-permute-start(bf16[512,256]{1,0:T(8,128)(2,1)S(1)} %pad_maximum_fusion.1), channel_id=1, source_target_pairs={{0,4},{1,5},{2,6},{3,7},{4,0},{5,1},{6,2},{7,3},{8,12},{9,13},{10,... | collective-permute-start | bytes 786440 | tf_op jit(solution)/shard_map/ppermute | solution.py:31
  66.2 26.0 %collective-permute-start.17 = (bf16[512,256]{1,0:T(8,128)(2,1)S(1)}, bf16[512,256]{1,0:T(8,128)(2,1)}, u32[]{:S(2)}, u32[]{:S(2)}) collective-permute-start(bf16[512,256]{1,0:T(8,128)(2,1)S(1)} %pad_maximum_fusion.1), channel_id=1, source_target_pairs={{0,8},{1,9},{2,10},{3,11},{4,12},{5,13},{6,14},{7,15},{8,0},{9,1},... | collective-permute-start | bytes 786440 | tf_op jit(solution)/shard_map/ppermute | solution.py:31
  68.8 71.0 %copy-start.6 = (bf16[256,256]{1,0:T(8,128)(2,1)}, bf16[256,256]{1,0:T(8,128)(2,1)S(1)}, u32[]{:S(2)}) copy-start(bf16[256,256]{1,0:T(8,128)(2,1)S(1)} %collective-permute-done.19.refs_10_) | copy-start | bytes 393220
  68.8 47.4 %collective-permute-start.7 = (bf16[512,512]{1,0:T(8,128)(2,1)S(1)}, bf16[512,512]{1,0:T(8,128)(2,1)}, u32[]{:S(2)}, u32[]{:S(2)}) collective-permute-start(bf16[512,512]{1,0:T(8,128)(2,1)S(1)} %pad_maximum_fusion), channel_id=1, source_target_pairs={{0,8},{1,9},{2,10},{3,11},{4,12},{5,13},{6,14},{7,15},{8,0},{9,1},... | collective-permute-start | bytes 1572872 | tf_op jit(solution)/shard_map/ppermute | solution.py:31
  92.1 18.2 %collective-permute-start.18 = (bf16[512,256]{1,0:T(8,128)(2,1)}, bf16[512,256]{1,0:T(8,128)(2,1)}, u32[]{:S(2)}, u32[]{:S(2)}) collective-permute-start(bf16[512,256]{1,0:T(8,128)(2,1)} %collective-permute-done.17.refs_8_), channel_id=1, source_target_pairs={{0,4},{1,5},{2,6},{3,7},{4,0},{5,1},{6,2},{7,3},{8,12},{9,13},{10,... | collective-permute-start | bytes 786440 | tf_op jit(solution)/shard_map/ppermute | solution.py:31
  92.9 19.4 %collective-permute-start.20 = (bf16[512,256]{1,0:T(8,128)(2,1)}, bf16[512,256]{1,0:T(8,128)(2,1)}, u32[]{:S(2)}, u32[]{:S(2)}) collective-permute-start(bf16[512,256]{1,0:T(8,128)(2,1)} %collective-permute-done.16.refs_7_), channel_id=1, source_target_pairs={{0,16},{1,17},{2,18},{3,19},{4,20},{5,21},{6,22},{7,23},{8,24},{9,... | collective-permute-start | bytes 786440 | tf_op jit(solution)/shard_map/ppermute | solution.py:31
  110.4 7.1 %collective-permute-start.21 = (bf16[512,256]{1,0:T(8,128)(2,1)}, bf16[512,256]{1,0:T(8,128)(2,1)}, u32[]{:S(2)}, u32[]{:S(2)}) collective-permute-start(bf16[512,256]{1,0:T(8,128)(2,1)} %collective-permute-done.17.refs_8_), channel_id=1, source_target_pairs={{0,16},{1,17},{2,18},{3,19},{4,20},{5,21},{6,22},{7,23},{8,24},{9,... | collective-permute-start | bytes 786440 | tf_op jit(solution)/shard_map/ppermute | solution.py:31
  112.4 14.6 %collective-permute-start.6 = (bf16[512,512]{1,0:T(8,128)(2,1)S(1)}, bf16[512,512]{1,0:T(8,128)(2,1)}, u32[]{:S(2)}, u32[]{:S(2)}) collective-permute-start(bf16[512,512]{1,0:T(8,128)(2,1)S(1)} %pad_maximum_fusion), channel_id=1, source_target_pairs={{0,4},{1,5},{2,6},{3,7},{4,0},{5,1},{6,2},{7,3},{8,12},{9,13},{10,... | collective-permute-start | bytes 1572872 | tf_op jit(solution)/shard_map/ppermute | solution.py:31
  116.2 22.0 %collective-permute-start.8 = (bf16[512,512]{1,0:T(8,128)(2,1)}, bf16[512,512]{1,0:T(8,128)(2,1)}, u32[]{:S(2)}, u32[]{:S(2)}) collective-permute-start(bf16[512,512]{1,0:T(8,128)(2,1)} %collective-permute-done.7.refs_8_), channel_id=1, source_target_pairs={{0,4},{1,5},{2,6},{3,7},{4,0},{5,1},{6,2},{7,3},{8,12},{9,13},{10,... | collective-permute-start | bytes 1572872 | tf_op jit(solution)/shard_map/ppermute | solution.py:31
  117.4 9.8 %collective-permute-start.22 = (bf16[512,256]{1,0:T(8,128)(2,1)}, bf16[512,256]{1,0:T(8,128)(2,1)}, u32[]{:S(2)}, u32[]{:S(2)}) collective-permute-start(bf16[512,256]{1,0:T(8,128)(2,1)} %collective-permute-done.18.refs_9_), channel_id=1, source_target_pairs={{0,16},{1,17},{2,18},{3,19},{4,20},{5,21},{6,22},{7,23},{8,24},{9,... | collective-permute-start | bytes 786440 | tf_op jit(solution)/shard_map/ppermute | solution.py:31
  126.9 39.2 %collective-permute-start.11 = (bf16[512,512]{1,0:T(8,128)(2,1)}, bf16[512,512]{1,0:T(8,128)(2,1)S(1)}, u32[]{:S(2)}, u32[]{:S(2)}) collective-permute-start(bf16[512,512]{1,0:T(8,128)(2,1)} %collective-permute-done.7.refs_8_), channel_id=1, source_target_pairs={{0,16},{1,17},{2,18},{3,19},{4,20},{5,21},{6,22},{7,23},{8,24},{9,... | collective-permute-start | bytes 1572872 | tf_op jit(solution)/shard_map/ppermute | solution.py:31
  127.2 38.9 %collective-permute-start.10 = (bf16[512,512]{1,0:T(8,128)(2,1)}, bf16[512,512]{1,0:T(8,128)(2,1)S(1)}, u32[]{:S(2)}, u32[]{:S(2)}) collective-permute-start(bf16[512,512]{1,0:T(8,128)(2,1)} %collective-permute-done.6.refs_7_), channel_id=1, source_target_pairs={{0,16},{1,17},{2,18},{3,19},{4,20},{5,21},{6,22},{7,23},{8,24},{9,... | collective-permute-start | bytes 1572872 | tf_op jit(solution)/shard_map/ppermute | solution.py:31
  138.2 27.9 %collective-permute-start.12 = (bf16[512,512]{1,0:T(8,128)(2,1)}, bf16[512,512]{1,0:T(8,128)(2,1)S(1)}, u32[]{:S(2)}, u32[]{:S(2)}) collective-permute-start(bf16[512,512]{1,0:T(8,128)(2,1)} %collective-permute-done.8.refs_9_), channel_id=1, source_target_pairs={{0,16},{1,17},{2,18},{3,19},{4,20},{5,21},{6,22},{7,23},{8,24},{9,... | collective-permute-start | bytes 1572872 | tf_op jit(solution)/shard_map/ppermute | solution.py:31
  138.4 11.6 %copy-start.7 = (bf16[256,512]{1,0:T(8,128)(2,1)}, bf16[256,512]{1,0:T(8,128)(2,1)S(1)}, u32[]{:S(2)}) copy-start(bf16[256,512]{1,0:T(8,128)(2,1)S(1)} %constant_dynamic-update-slice_fusion.refs_6_) | copy-start | bytes 786436
  138.5 26.1 %collective-permute-start.9 = (bf16[256,512]{1,0:T(8,128)(2,1)S(1)}, bf16[256,512]{1,0:T(8,128)(2,1)S(1)}, u32[]{:S(2)}, u32[]{:S(2)}) collective-permute-start(bf16[256,512]{1,0:T(8,128)(2,1)S(1)} %constant_dynamic-update-slice_fusion.refs_6_), channel_id=1, source_target_pairs={{0,16},{1,17},{2,18},{3,19},{4,20},{5,21},{6,22},{7,23},{8,24},{9,... | collective-permute-start | bytes 786440 | tf_op jit(solution)/shard_map/ppermute | solution.py:31
  151.3 27.3 %collective-permute-start.23 = (bf16[768,256]{1,0:T(8,128)(2,1)S(1)}, bf16[768,256]{1,0:T(8,128)(2,1)S(1)}, u32[]{:S(2)}, u32[]{:S(2)}) collective-permute-start(bf16[768,256]{1,0:T(8,128)(2,1)S(1)} %get-tuple-element.17), channel_id=1, source_target_pairs={{0,4},{1,5},{2,6},{3,7},{4,8},{5,9},{6,10},{7,11},{8,12},{9,13},{1... | collective-permute-start | bytes 1179656 | tf_op jit(solution)/shard_map/ppermute | solution.py:42
  164.6 1.5 copy-start.13
  164.6 14.0 %collective-permute-start.24 = (bf16[768,256]{1,0:T(8,128)(2,1)S(1)}, bf16[768,256]{1,0:T(8,128)(2,1)S(1)}, u32[]{:S(2)}, u32[]{:S(2)}) collective-permute-start(bf16[768,256]{1,0:T(8,128)(2,1)S(1)} %get-tuple-element.16), channel_id=1, source_target_pairs={{4,0},{5,1},{6,2},{7,3},{8,4},{9,5},{10,6},{11,7},{12,8},{13,9},{1... | collective-permute-start | bytes 1179656 | tf_op jit(solution)/shard_map/ppermute | solution.py:42
  166.1 0.8 copy-start.9
  166.1 1.0 copy-start.8
  166.1 1.1 copy-start.10
  178.5 0.8 copy-start.11
  178.6 0.9 copy-start.12
  197.0 6.8 %collective-permute-start.25 = (bf16[256,512]{1,0:T(8,128)(2,1)S(1)}, bf16[256,512]{1,0:T(8,128)(2,1)S(1)}, u32[]{:S(2)}, u32[]{:S(2)}) collective-permute-start(bf16[256,512]{1,0:T(8,128)(2,1)S(1)} %get-tuple-element.9), channel_id=1, source_target_pairs={{0,1},{1,0},{2,3},{3,2},{4,5},{5,4},{6,7},{7,6},{8,9},{9,8},{10,11... | collective-permute-start | bytes 786440 | tf_op jit(solution)/shard_map/ppermute | solution.py:31
  202.1 7.9 %collective-permute-start.26 = (bf16[256,512]{1,0:T(8,128)(2,1)S(1)}, bf16[256,512]{1,0:T(8,128)(2,1)S(1)}, u32[]{:S(2)}, u32[]{:S(2)}) collective-permute-start(bf16[256,512]{1,0:T(8,128)(2,1)S(1)} %get-tuple-element.8), channel_id=1, source_target_pairs={{0,2},{1,3},{2,0},{3,1},{4,6},{5,7},{6,4},{7,5},{8,10},{9,11},{10,... | collective-permute-start | bytes 786440 | tf_op jit(solution)/shard_map/ppermute | solution.py:31
  203.3 12.4 %collective-permute-start.27 = (bf16[256,512]{1,0:T(8,128)(2,1)S(1)}, bf16[256,512]{1,0:T(8,128)(2,1)S(1)}, u32[]{:S(2)}, u32[]{:S(2)}) collective-permute-start(bf16[256,512]{1,0:T(8,128)(2,1)S(1)} %get-tuple-element.7), channel_id=1, source_target_pairs={{0,3},{1,2},{2,1},{3,0},{4,7},{5,6},{6,5},{7,4},{8,11},{9,10},{10,... | collective-permute-start | bytes 786440 | tf_op jit(solution)/shard_map/ppermute | solution.py:31
  210.0 5.7 %copy-start.2 = (bf16[256,2048]{1,0:T(8,128)(2,1)}, bf16[256,2048]{1,0:T(8,128)(2,1)S(1)}, u32[]{:S(2)}) copy-start(bf16[256,2048]{1,0:T(8,128)(2,1)S(1)} %constant_dynamic-update-slice_fusion.5) | copy-start | bytes 3145732

commit v2 on v0

v2 whole, which is shorter than its diff:
```python
import functools

import jax
import jax.numpy as jnp
from jax import lax
from jax.experimental import pallas as pl
from jax.experimental.pallas import tpu as pltpu
from jax.sharding import PartitionSpec as P

HD = 128
MOST_BLK = 7
LANES = 128
NOTES = 16
AXES = ("groups", "seq")
LOG2_E = 1.4426950408889634
VMEM_LIMIT = 63 * 1024 * 1024
IN_VMEM = pl.BlockSpec(memory_space=pltpu.VMEM)
IN_SMEM = pl.BlockSpec(memory_space=pltpu.SMEM)
IN_HBM = pl.BlockSpec(memory_space=pltpu.HBM)
PARAMS = pltpu.CompilerParams(vmem_limit_bytes=VMEM_LIMIT)


def cost(flops, size, transcendentals=0):
    return pl.CostEstimate(
        flops=flops, bytes_accessed=size, transcendentals=transcendentals
    )


def swap(value, team, group_bits, layer_bits, member_bits):
    groups, peers = lax.axis_size("groups"), lax.axis_size("seq")
    pairs = []
    for g in range(groups):
        for s in range(peers):
            layer, member = divmod(s, team)
            to = (layer ^ layer_bits) * team + (member ^ member_bits)
            pairs.append((g * peers + s, (g ^ group_bits) * peers + to))
    return lax.ppermute(value, AXES, pairs)


def from_layer(value, team, by):
    groups, peers = lax.axis_size("groups"), lax.axis_size("seq")
    pairs = []
    for g in range(groups):
        for s in range(peers):
            to = s - by * team
            if 0 <= to < peers:
                pairs.append((g * peers + s, g * peers + to))
    return lax.ppermute(value, AXES, pairs)


def tie(value, *others):
    return lax.optimization_barrier((value,) + others)[0] if others else value


def norm_kernel(tokens_ref, gain_ref, *outs):
    first = 0
    for out in outs:
        widened = tokens_ref[first : first + out.shape[0], :].astype(jnp.float32)
        square = jnp.mean(widened * widened, axis=-1, keepdims=True)
        out[...] = (widened * lax.rsqrt(square + 1e-05) * gain_ref[...]).astype(jnp.bfloat16)
        first += out.shape[0]


def normalize(tokens, norm_gain, lengths):
    rows, width = tokens.shape
    return pl.pallas_call(
        norm_kernel,
        out_shape=[jax.ShapeDtypeStruct((n, width), jnp.bfloat16) for n in lengths],
        in_specs=[IN_VMEM] * 2,
        out_specs=[IN_VMEM] * len(lengths),
        compiler_params=PARAMS,
        cost_estimate=cost(6 * rows * width, 4 * rows * width, rows),
        name="normalize",
    )(tokens, norm_gain.reshape(1, width))


def pack_kernel(team, part, count, place, numbers, *refs):
    weights, outs = refs[:count], refs[count : count + team]
    loaded, sems = refs[count + team : -1], refs[-1]
    copies = [
        pltpu.make_async_copy(weight, there, sems.at[i])
        for i, (weight, there) in enumerate(zip(weights, loaded))
    ]
    for copy in copies:
        copy.start()
    row = lax.broadcasted_iota(jnp.int32, (NOTES, outs[0].shape[1]), 0)
    noted = jnp.zeros((NOTES, outs[0].shape[1]), jnp.float32)
    for i in range(numbers.shape[0]):
        noted = jnp.where(row == i, numbers[i].astype(jnp.float32), noted)
    noted = noted.astype(jnp.bfloat16)
    for out in outs:
        out[out.shape[0] - NOTES :, :] = noted
    column = 0
    for copy, weight in zip(copies, loaded):
        copy.wait()
        width = weight.shape[1] // team
        for r, out in enumerate(outs):
            length = out.shape[0] - NOTES
            first = 0 if r < 2 else pl.multiple_of(place[0] * part, part)
            columns = pl.ds(pl.multiple_of((place[2] ^ r) * width, width), width)
            out[:length, column : column + width] = weight[pl.ds(first, length), columns]
        column += width


def pack(place, numbers, weights, team, groups):
    depth = weights[0].shape[0]
    width = sum(weight.shape[1] for weight in weights) // team
    lengths = [depth if r < 2 else depth // groups for r in range(team)]
    return pl.pallas_call(
        functools.partial(pack_kernel, team, depth // groups, len(weights)),
        out_shape=[
            jax.ShapeDtypeStruct((length + NOTES, width), jnp.bfloat16)
            for length in lengths
        ],
        in_specs=[IN_SMEM] * 2 + [IN_HBM] * len(weights),
        out_specs=[IN_VMEM] * team,
        scratch_shapes=[pltpu.VMEM(w.shape, w.dtype) for w in weights]
        + [pltpu.SemaphoreType.DMA((len(weights),))],
        compiler_params=PARAMS,
        cost_estimate=cost(0, 4 * team * depth * width),
        name="pack",
    )(place, numbers, *weights)


def shards_kernel(team, part, blocks, place, *refs):
    ins, shards, far = refs[:team], refs[team:-1], refs[-1]
    mine = pl.ds(pl.multiple_of(place[0] * part, part), part)
    for r, ref in enumerate(ins):
        rows = mine if r < 2 else pl.ds(0, part)
        column = 0
        for shard in shards:
            width = shard.shape[1]
            shard[r * part : (r + 1) * part, :] = ref[rows, column : column + width]
            column += width
        if r >= 2:
            far[(r - 2) * part : (r - 1) * part, :] = ref[rows, :]
    noted_in = shards[0]
    row = lax.broadcasted_iota(jnp.int32, (NOTES, noted_in.shape[1]), 0)
    noted = jnp.zeros((NOTES, noted_in.shape[1]), jnp.float32)
    for r, ref in enumerate(ins):
        held = ref[ref.shape[0] - NOTES :, : noted_in.shape[1]].astype(jnp.float32)
        for i in range(blocks):
            noted = jnp.where(row == r * blocks + i, held[i : i + 1, :], noted)
    noted_in[team * part :, :] = noted.astype(jnp.bfloat16)


def make_shards(place, packed, moved, widths, depth, groups, blocks):
    part, width = depth // groups, packed.shape[1]
    team = 1 + len(moved)
    shapes = [(team * part + (0 if i else NOTES), w) for i, w in enumerate(widths)]
    shapes.append(((team - 2) * part, width))
    return pl.pallas_call(
        functools.partial(shards_kernel, team, part, blocks),
        out_shape=[jax.ShapeDtypeStruct(shape, jnp.bfloat16) for shape in shapes],
        in_specs=[IN_SMEM] + [IN_VMEM] * team,
        out_specs=[IN_VMEM] * len(shapes),
        compiler_params=PARAMS,
        cost_estimate=cost(0, 6 * team * part * width),
        name="shards",
    )(place, packed, *moved)


def project_kernel(items, counts, chunk, margin, rest, team, groups, depth, place, *refs):
    held, arrays, wanted = counts
    sources, refs = refs[:held], refs[held:]
    stored, refs = refs[:arrays], refs[arrays:]
    outs, (tokens, weights, total, token_sems, sems) = refs[:-5], refs[-5:]
    part = depth // groups
    group, layer, member = place[0], place[1], place[2]
    span = tokens.shape[0] // 2
    token_copies, offset = ([], []), 0
    for i, ref in enumerate(sources):
        there = tokens.at[pl.ds(offset, ref.shape[0])]
        copy = pltpu.make_async_copy(ref, there, token_sems.at[i])
        token_copies[offset // span].append(copy)
        offset += ref.shape[0]
    for copy in token_copies[0]:
        copy.start()
    plan, offset, copies = [], 0, 0
    for described, parts in items:
        deep = sum(depth if bits[2] is None else part for bits in described)
        loads = []
        for c, (source, first, column) in enumerate(parts):
            copy = pltpu.make_async_copy(
                stored[source].at[pl.ds(first, deep), pl.ds(column, chunk)],
                weights.at[pl.ds(offset, deep), pl.ds(c * chunk, chunk)],
                sems.at[copies],
            )
            copy.start()
            loads.append(copy)
            copies += 1
        plan.append((described, offset, deep, loads))
        offset += deep

    def columns_of(own, described):
        lefts = []
        for layer_bits, member_bits, group_bits in described:
            owner = (layer ^ layer_bits) * team + (member ^ member_bits)
            first, wide = owner * depth, depth
            if group_bits is not None:
                first, wide = first + (group ^ group_bits) * part, part
            lefts.append(tokens[own, pl.ds(pl.multiple_of(first, LANES), wide)])
        return lefts[0] if len(lefts) == 1 else jnp.concatenate(lefts, axis=1)

    for half in range(2):
        own = pl.ds(half * span, span)
        for copy in token_copies[half]:
            copy.wait()
        if half == 0:
            for copy in token_copies[1]:
                copy.start()
        for i, (described, offset, deep, loads) in enumerate(plan):
            if half == 0:
                for copy in loads:
                    copy.wait()
            wide = len(loads) * chunk
            right = weights[pl.ds(offset, deep), :wide]
            term = jnp.dot(
                columns_of(own, described), right, preferred_element_type=jnp.float32
            )
            if i == 0:
                total[own, :wide] = term
            else:
                total[own, :wide] += term
        column = 0
        for described in rest if wanted else ():
            left = columns_of(own, described)
            outs[-1][own, column : column + left.shape[1]] = left
            column += left.shape[1]
    rows = total.shape[0] // team
    chunks = total.shape[1] // chunk
    for c in range(chunks):
        columns = slice(c * chunk, (c + 1) * chunk)
        if rest and c + 1 == chunks:
            outs[c][...] = total[:, columns]
            continue
        for r in range(team):
            first = r * rows
            if c == 0 and margin is not None:
                first = pl.multiple_of((member ^ r) * rows, rows)
            made = total[r * rows : (r + 1) * rows, columns]
            outs[c][pl.ds(first, rows), :] = made.astype(jnp.bfloat16)
    if margin is not None:
        outs[chunks][...] = outs[0][total.shape[0] - margin :, :]
        outs[chunks + 1][...] = outs[0][:margin, :]


def project(
    place, team, tokens, arrays, items, chunk, groups, depth, margin=None, rest=(), wanted=False
):
    count, width = sum(value.shape[0] for value in tokens), tokens[0].shape[1]
    chunks = max(len(parts) for _, parts in items)
    names = sorted({name for _, parts in items for name, _, _ in parts})
    items = [
        (described, [(names.index(n), first, column) for n, first, column in parts])
        for described, parts in items
        if parts
    ]

    def deep_of(listed):
        return sum(depth // (1 if b[2] is None else groups) for d in listed for b in d)

    deep = deep_of([described for described, _ in items])
    copies = sum(len(parts) for _, parts in items)
    kinds = [jnp.bfloat16] * (chunks - bool(rest)) + [jnp.float32] * bool(rest)
    shapes = [jax.ShapeDtypeStruct((count, chunk), kind) for kind in kinds]
    if margin is not None:
        shapes += [jax.ShapeDtypeStruct((margin, chunk), jnp.bfloat16)] * 2
    if wanted:
        shapes.append(jax.ShapeDtypeStruct((count, deep_of(rest)), jnp.bfloat16))
    return pl.pallas_call(
        functools.partial(
            project_kernel,
            items,
            (len(tokens), len(names), wanted),
            chunk,
            margin,
            rest,
            team,
            groups,
            depth,
        ),
        out_shape=shapes,
        in_specs=[IN_SMEM] + [IN_HBM] * (len(tokens) + len(names)),
        out_specs=[IN_VMEM] * len(shapes),
        scratch_shapes=[
            pltpu.VMEM((count, width), jnp.bfloat16),
            pltpu.VMEM((deep, chunks * chunk), jnp.bfloat16),
            pltpu.VMEM((count, chunks * chunk), jnp.float32),
            pltpu.SemaphoreType.DMA((len(tokens),)),
            pltpu.SemaphoreType.DMA((copies,)),
        ],
        compiler_params=PARAMS,
        cost_estimate=cost(
            2 * count * deep * chunks * chunk,
            2 * chunks * chunk * (count + deep) + 2 * count * width,
        ),
        name="project",
    )(place, *tokens, *[arrays[name] for name in names])


def attend_kernel(
    base, block, deep, firsts, first_ref, count_ref, before, own, after, *refs
):
    outs, (window, query) = refs[:-2][-(len(refs) - 2 - firsts[0]) :], refs[-2:]
    ins = refs[: firsts[0]]
    per_out = outs[0].shape[0] // block
    total_blocks = per_out * len(outs)
    mine = pl.ds(base * block, total_blocks * block)
    if deep:
        *sums, left = ins[: len(firsts[1]) + 1]
        weights = iter(ins[len(firsts[1]) + 1 :])
        for c, (begun, starts) in enumerate(zip(sums, firsts[1])):
            total = begun[mine, :]
            for i, start in enumerate(starts):
                total += jnp.dot(
                    left[mine, i * deep : (i + 1) * deep],
                    next(weights)[start : start + deep, :],
                    preferred_element_type=jnp.float32,
                )
            wide = total.shape[1]
            query[:, c * wide : (c + 1) * wide] = total.astype(jnp.bfloat16)
    else:
        query[...] = ins[0][mine, :]
    offset = 0
    for ref in (before, own, after):
        window[offset : offset + ref.shape[0], :] = ref[...]
        offset += ref.shape[0]
    heads = query.shape[1] // HD
    span = MOST_BLK * block
    row = lax.broadcasted_iota(jnp.int32, (span, 1), 0)

    def place_of(b):
        return pl.ds(pl.multiple_of(first_ref[base + b] * block, block), span)

    def score(b):
        rows = pl.ds(b * block, block)
        stacked = jnp.concatenate(
            [query[rows, h * HD : (h + 1) * HD] for h in range(heads)], axis=0
        )
        return lax.dot_general(
            window[place_of(b), :HD],
            stacked,
            (((1,), (1,)), ((), ())),
            preferred_element_type=jnp.float32,
        )

    scores = score(0)
    for b in range(total_blocks):
        upcoming = score(b + 1) if b + 1 < total_blocks else None
        scores = jnp.where(row < count_ref[base + b] * block, scores, -1e30)
        row_max = jnp.max(scores, axis=0, keepdims=True)
        weights = jnp.exp2((scores - row_max) * (HD ** (-0.5) * LOG2_E))
        row_total = jnp.sum(weights, axis=0, keepdims=True)
        mixed = lax.dot_general(
            window[place_of(b), HD:],
            weights.astype(jnp.bfloat16),
            (((0,), (0,)), ((), ())),
            preferred_element_type=jnp.float32,
        )
        mixed = mixed / row_total
        out = outs[b // per_out]
        rows = pl.ds((b % per_out) * block, block)
        for h in range(heads):
            turned = mixed[:, h * block : (h + 1) * block].T
            out[rows, h * HD : (h + 1) * HD] = turned.astype(jnp.bfloat16)
        scores = upcoming


def attend(first, count, query, before, own, after, block, base, rows, parts):
    if isinstance(query, tuple):
        *sums, left, lates = query
        ins = [*sums, left] + [array for late in lates for array, _ in late]
        firsts = (len(ins), [[start for _, start in late] for late in lates])
        deep = left.shape[1] // len(lates[0])
        columns = sum(value.shape[1] for value in sums)
    else:
        ins, firsts, deep, columns = [query], (1, []), 0, query.shape[1]
    span = before.shape[0] + own.shape[0] + after.shape[0]
    return pl.pallas_call(
        functools.partial(attend_kernel, base, block, deep, firsts),
        out_shape=[jax.ShapeDtypeStruct((rows, columns), jnp.bfloat16)] * parts,
        in_specs=[IN_SMEM] * 2 + [IN_VMEM] * (3 + len(ins)),
        out_specs=[IN_VMEM] * parts,
        scratch_shapes=[
            pltpu.VMEM((span, own.shape[1]), jnp.bfloat16),
            pltpu.VMEM((parts * rows, columns), jnp.bfloat16),
        ],
        compiler_params=PARAMS,
        cost_estimate=cost(
            4 * parts * rows * MOST_BLK * block * columns,
            4 * rows * columns + 2 * span * own.shape[1],
            parts * rows * MOST_BLK * block * (columns // HD),
        ),
        name="attend",
    )(first, count, before, own, after, *ins)


def assemble_kernel(place, *refs):
    pieces, out = refs[:-1], refs[-1]
    for r, piece in enumerate(pieces):
        width = piece.shape[1]
        first = pl.multiple_of((place[2] ^ r) * width, width)
        out[:, pl.ds(first, width)] = piece[...]


def assemble(place, pieces):
    rows, width = pieces[0].shape
    return pl.pallas_call(
        assemble_kernel,
        out_shape=jax.ShapeDtypeStruct((rows, width * len(pieces)), jnp.bfloat16),
        in_specs=[IN_SMEM] + [IN_VMEM] * len(pieces),
        out_specs=IN_VMEM,
        compiler_params=PARAMS,
        cost_estimate=cost(0, 4 * rows * width * len(pieces)),
        name="assemble",
    )(place, *pieces)


def on_device(tokens, norm_gain, w_query, w_key, w_value, passage_blocks):
    groups, peers = lax.axis_size("groups"), lax.axis_size("seq")
    team = w_key.shape[1] // HD
    layers = peers // team
    depth = w_key.shape[0]
    rows = tokens.shape[0]
    blocks = passage_blocks.shape[0]
    block = rows // blocks
    index = lax.axis_index("seq")
    group, layer, member = lax.axis_index("groups"), index // team, index % team
    place = jnp.stack([group, layer, member]).astype(jnp.int32)
    widths = [2 * HD] * ((w_key.shape[1] + w_value.shape[1] + w_query.shape[1]) // (2 * HD * team))
    margin = (MOST_BLK - 1) * block

    if depth // groups % LANES == 0 and team * blocks <= NOTES:
        chunk = 2 * HD
        packed = pack(place, passage_blocks, [w_key, w_value, w_query], team, groups)
        moved = [swap(packed[r], team, 0, 0, r) for r in range(1, team)]
        steps = range(1, 4)
        lengths = [rows * n // 16 for n in (4, 6, 6)]
        normed = normalize(tie(tokens, packed[0]), norm_gain, lengths)
        *shards, far = make_shards(
            tie(place, normed[0]), packed[0], moved, widths, depth, groups, blocks
        )

        chunks = len(shards)
        hops = max(bits.bit_count() for bits in range(layers))
        arrays = {"own": packed[0], "far": far}
        arrays.update({f"normed{i}": value for i, value in zip(steps, normed)})
        arrays.update({f"moved{r}": value for r, value in enumerate(moved, 1)})
        arrays.update({f"shard{c}": shard for c, shard in enumerate(shards)})
        held = {(c, 0): (f"shard{c}", 0, shard.shape[0]) for c, shard in enumerate(shards)}
        crossed, far_tokens, diagonal = {}, [], []
        part = depth // groups

        def join(parts):
            views = [arrays[name][first : first + n] for name, first, n in parts]
            return views[0] if len(views) == 1 else jnp.concatenate(views, axis=0)

        def items_of(cs, layer_bits=range(layers), others=range(groups)):
            items = []
            if 0 in layer_bits:
                for r, name in enumerate(["own"] + [f"moved{r}" for r in range(1, team)]):
                    described = [(0, r, None if r < 2 else 0)]
                    items.append((described, [(name, 0, c * chunk) for c in cs]))
                for other in range(1, groups):
                    described = [(0, r, other) for r in range(2, team)]
                    items.append((described, [(f"far{other}", 0, c * chunk) for c in cs]))
            for other in others:
                for bits in layer_bits:
                    if bits:
                        described = [(bits, r, other) for r in range(team)]
                        where = [crossed[c, bits, other] if other else held[c, bits] for c in cs]
                        items.append((described, [(n, first, 0) for n, first, _ in where]))
            return items

        hardest = [bits for bits in range(layers) if bits.bit_count() == hops]

        def without_last(cs):
            items, rest, late = [], [], []
            for described, parts in items_of(cs):
                if described[0][2] and described[0][0] in hardest:
                    name, first, _ = parts[-1]
                    late.append((name, first))
                    rest.append(described)
                    parts = parts[:-1]
                items.append((described, parts))
            late = [(arrays[n], f) for n, f in late if n in arrays]
            return items, rest, late

        for phase in range(1, chunks + hops + 1):
            arrays = lax.optimization_barrier(arrays)
            sends = []
            ways = {}
            for c in range(chunks):
                for bits in range(1, layers):
                    low = bits & -bits
                    if c + bits.bit_count() == phase:
                        ways.setdefault((0, low), []).append((c, bits, held[c, bits ^ low]))
                    elif c + bits.bit_count() + 1 == phase:
                        for other in range(1, groups):
                            way = ways.setdefault((other, 0), [])
                            way.append((c, bits, held[c, bits]))
            for (other, low), listed in ways.items():
                name = f"phase{phase}from{other}{low}"
                value = join([p for _, _, p in listed])
                sends.append((other, low, 0, name, value))
                first = 0
                for c, bits, (_, _, n) in listed:
                    if other:
                        crossed[c, bits, other] = (name, first, n)
                    else:
                        held[c, bits] = (name, first, n)
                    first += n
            if phase in steps:
                sends.append((0, 0, 2, f"tokens{phase}", arrays[f"normed{phase}"]))
            if phase - 1 in steps:
                value = arrays[f"tokens{phase - 1}"]
                sends.append((0, 0, 1, f"diagonal{phase - 1}", value))
            if phase == 1:
                for i in steps:
                    sends.append((0, 0, 1, f"near{i}", arrays[f"normed{i}"]))
                for other in range(1, groups):
                    sends.append((other, 0, 0, f"far{other}", arrays["far"]))
            new = {}
            for group_bits, layer_bits, member_bits, name, value in sends:
                new[name] = swap(value, team, group_bits, layer_bits, member_bits)
            arrays.update(new)
            if phase == chunks + hops - 1:
                team_tokens = [arrays[f"normed{i}"] for i in steps]
                team_tokens += [arrays[f"near{i}"] for i in steps]
                team_tokens += [arrays[f"tokens{i}"] for i in steps]
                team_tokens += [arrays[f"diagonal{i}"] for i in steps]
                items, rest, _ = without_last(range(chunks - 1))
                made = project(
                    place,
                    team,
                    team_tokens,
                    arrays,
                    items,
                    chunk,
                    groups,
                    depth,
                    margin,
                    rest,
                    True,
                )
                names = ["keys_values"] + [f"sum{c}" for c in range(1, chunks - 1)]
                arrays.update(zip(names + ["tail", "head", "left"], made))
        team_tokens = [arrays[f"normed{i}"] for i in steps]
        team_tokens += [arrays[f"near{i}"] for i in steps]
        team_tokens += [arrays[f"tokens{i}"] for i in steps]
        team_tokens += [arrays[f"diagonal{i}"] for i in steps]
        keys_values, tail, head = (arrays[n] for n in ("keys_values", "tail", "head"))
        items, rest, late = without_last([chunks - 1])
        (begun,) = project(
            place, team, team_tokens, arrays, items, chunk, groups, depth, rest=rest
        )
        lates = [without_last([chunks - 2])[2], late]
        query = (arrays[f"sum{chunks - 2}"], begun, arrays["left"], lates)
        assert chunks == 3
        ids = []
        for s in range(layers):
            name, first, n = held[0, s]
            noted = arrays[name][first + team * part : first + n]
            ids.append(noted[: team * blocks, 0])
        ids = jnp.stack(ids).astype(jnp.int32)
        mine = ids[0]
        ids = ids.reshape(-1)
    else:
        (normed,) = normalize(tokens, norm_gain, [rows])
        team_tokens = [normed] + [swap(normed, team, 0, 0, r) for r in range(1, team)]
        stacked = jnp.stack(team_tokens)
        in_order = jnp.concatenate(
            [lax.dynamic_index_in_dim(stacked, member ^ t, 0, False) for t in range(team)]
        )

        def dense(weight, rows_of_tokens):
            whole = lax.all_gather(weight, "seq", axis=0, tiled=True)
            width = weight.shape[1] // team
            own = lax.dynamic_slice_in_dim(whole, member * width, width, 1)
            product = jnp.dot(rows_of_tokens, own, preferred_element_type=jnp.float32)
            return product.astype(jnp.bfloat16)

        keys_values = jnp.concatenate(
            [dense(w_key, in_order), dense(w_value, in_order)], axis=1
        )
        tail, head = keys_values[-margin:], keys_values[:margin]
        query = dense(w_query, stacked.reshape(team * rows, tokens.shape[1]))
        ids = lax.all_gather(passage_blocks, "seq", axis=0, tiled=True)
        mine = jnp.concatenate(
            [
                lax.dynamic_slice_in_dim(ids, (layer * team + (member ^ r)) * blocks, blocks)
                for r in range(team)
            ]
        )

    before = from_layer(tail, team, -1)
    after = from_layer(head, team, 1)

    count = jnp.sum((mine[:, None] == ids[None, :]).astype(jnp.int32), axis=1)
    first = jnp.sum((ids[None, :] < mine[:, None]).astype(jnp.int32), axis=1)
    first = first - layer * team * blocks + (MOST_BLK - 1)

    pieces = [None] * team
    for start, end in ((1, team), (0, 1)):
        made = attend(
            first,
            count,
            query,
            before,
            keys_values,
            after,
            block,
            start * blocks,
            rows,
            end - start,
        )
        for r, piece in enumerate(made, start):
            pieces[r] = swap(piece, team, 0, 0, r) if r else piece
    return assemble(place, pieces)


def solution(mesh):
    in_specs = (
        P(("groups", "seq"), None),
        P(),
        P("seq", None),
        P("seq", None),
        P("seq", None),
        P(("groups", "seq")),
    )
    out_specs = P(("groups", "seq"), None)
    return jax.shard_map(
        on_device, mesh=mesh, in_specs=in_specs, out_specs=out_specs, check_vma=False
    )
```

time: 315 us -> 164 us (0.52)
  waiting for transfers between devices: 192 us -> 62.2 us
  Pallas kernels: 0 us -> 49.8 us
  matrix products: 38.2 us -> 0 us
  between operations: 13.4 us -> 0.22 us
  local copies, waits for them, and re-layouts: 17.3 us -> 6.22 us
  other arithmetic: 10.4 us -> 5.65 us
    all_gather x3 -> x0, waiting for transfers between devices: 147 us -> none  [the longest x1 76.2 us: on_device(): lax.all_gather(w_query, 'seq', axis=0, tiled=True)]
    pallas_call x0 -> x8, Pallas kernels: none -> 49.8 us  [the longest x2 24.8 us: project(): pl.pallas_call(functools.partial(project_kernel, items, (len(tokens), len...]
    dot_general x11 -> x0, matrix products: 38.2 us -> none  [the longest x3 18 us: add_rows(): return jnp.dot(normed, piece, preferred_element_type=jnp.float32)]
    ppermute x18 -> x29, waiting for transfers between devices: 43.5 us -> 62.2 us  [the longest x27 62.2 us: swap(): return lax.ppermute(value, AXES, pairs)]
    reduce_sum x5 -> x1, other arithmetic: 8.32 us -> 0.69 us  [on_device(): count = jnp.sum((mine[:, None] == ids[None, :]).astype(jnp.int32), axis=1)]
    reshape x3 -> x0, local copies, waits for them, and re-layouts: 5.55 us -> none  [the longest x2 3.04 us: on_device(): query_rounded.reshape(row_count, KVH, QH // KVH, HD).transpose(1, 0, 2, 3)]
    ppermute x18 -> x29, starting transfers between devices: 42.5 us -> 39.6 us  [the longest x27 34.7 us: swap(): return lax.ppermute(value, AXES, pairs)]
    unnamed x22 -> x48, local copies, waits for them, and re-layouts: 6.73 us -> 4.6 us
  transfers between devices with their start and end apart: 21 -> 29, of which waited for: 8 -> 11; matrix products, arithmetic and copies ran while one was open for 7% -> 3% of each run, Pallas kernels for 0% -> 21%
where the time goes in v2:
time: 164 us
  waiting for transfers between devices  62.2 us (38%)
  Pallas kernels  49.8 us (30%)
  starting transfers between devices  39.6 us (24%)
  local copies, waits for them, and re-layouts  6.22 us (4%)
  other arithmetic  5.65 us (3%)
    ppermute x27, waiting for transfers between devices, swap(): return lax.ppermute(value, AXES, pairs)  62.2 us
    ppermute x27, starting transfers between devices, swap(): return lax.ppermute(value, AXES, pairs)  34.7 us
    pallas_call x2, Pallas kernels, project(): pl.pallas_call(functools.partial(project_kernel, items, (len(tokens), len...  24.8 us
    pallas_call x2, Pallas kernels, attend(): pl.pallas_call(functools.partial(attend_kernel, base, block, deep, firsts...  13.6 us
    ppermute x2, starting transfers between devices, from_layer(): return lax.ppermute(value, AXES, pairs)  4.89 us
    unnamed x48, local copies, waits for them, and re-layouts  4.6 us
    pallas_call x1, Pallas kernels, normalize(): pl.pallas_call(norm_kernel, out_shape=[jax.ShapeDtypeStruct((n, width), j...  3.6 us
  transfers between devices with their start and end apart: 29, of which 11 were waited for; matrix products, arithmetic and copies ran while one was open for 3% of the time, Pallas kernels for 21%

profile of v2, /device:TPU:1, one launch (start us, length us, event | category | flops | bytes accessed | tf_op | source)
XLA Modules:
  0.0 163.6 jit_solution(11870896486967398743)
XLA Ops:
  0.0 0.7 pad_add_fusion.place
  0.7 3.2 %pack.1 = (bf16[272,768]{1,0:T(8,128)(2,1)}, bf16[272,768]{1,0:T(8,128)(2,1)}, bf16[144,768]{1,0:T(8,128)(2,1)}, bf16[144,768]{1,0:T(8,128)(2,1)}) custom-call(s32[3]{0:T(128)} %pad_add_fusion.place, s32[2]{0:T(128)} %numbers.1, bf16[256,512]{1,0:T(8,128)(2,1)} %refs_0_.1, bf16[256,512]{1,0:T(8,128)(2,1)} %refs_1_.1, bf16[256,2048]{1,0:T(8,128)(2,1)} %refs_2_.1), custom_call_target="tpu_custom_call" | custom-call | bytes 3145728 | tf_op jit(solution)/shard_map/pack/pallas_call | solution.py:109
  3.8 0.1 collective-permute-start
  4.0 2.7 %collective-permute-start.1 = (bf16[144,768]{1,0:T(8,128)(2,1)}, bf16[144,768]{1,0:T(8,128)(2,1)S(1)}, u32[]{:S(2)}, u32[]{:S(2)}) collective-permute-start(bf16[144,768]{1,0:T(8,128)(2,1)} %get-tuple-element.135), channel_id=1, source_target_pairs={{0,2},{1,3},{2,0},{3,1},{4,6},{5,7},{6,4},{7,5},{8,10},{9,11},{10,... | collective-permute-start | bytes 663560 | tf_op jit(solution)/shard_map/ppermute | solution.py:37
  6.7 0.0 collective-permute-start.2
  6.7 3.6 %normalize.1 = (bf16[64,4096]{1,0:T(8,128)(2,1)}, bf16[96,4096]{1,0:T(8,128)(2,1)}, bf16[96,4096]{1,0:T(8,128)(2,1)}) custom-call(bf16[256,4096]{1,0:T(8,128)(2,1)} %tokens_ref, f32[1,4096]{1,0:T(1,128)} %bitcast.8), custom_call_target="tpu_custom_call" | custom-call | flops 6291456 | bytes 4194304 | tf_op jit(solution)/shard_map/normalize/pallas_call | solution.py:66
  10.3 2.3 %collective-permute-done.1.refs_2_.refs_14_ = bf16[144,768]{1,0:T(8,128)(2,1)S(1)} collective-permute-done((bf16[144,768]{1,0:T(8,128)(2,1)}, bf16[144,768]{1,0:T(8,128)(2,1)S(1)}, u32[]{:S(2)}, u32[]{:S(2)}) %collective-permute-start.1) | collective-permute-done | bytes 221216 | tf_op jit(solution)/shard_map/ppermute | solution.py:37
  12.6 4.7 %collective-permute-done.2.refs_3_.refs_15_ = bf16[144,768]{1,0:T(8,128)(2,1)S(1)} collective-permute-done((bf16[144,768]{1,0:T(8,128)(2,1)}, bf16[144,768]{1,0:T(8,128)(2,1)S(1)}, u32[]{:S(2)}, u32[]{:S(2)}) %collective-permute-start.2) | collective-permute-done | bytes 221216 | tf_op jit(solution)/shard_map/ppermute | solution.py:37
  17.3 0.0 collective-permute-done.refs_1_.refs_13_
  17.3 0.7 copy-done.6
  18.0 0.7 copy-done.2
  18.8 2.3 %shards.1 = (bf16[528,256]{1,0:T(8,128)(2,1)}, bf16[512,256]{1,0:T(8,128)(2,1)}, bf16[512,256]{1,0:T(8,128)(2,1)}, bf16[256,768]{1,0:T(8,128)(2,1)}) custom-call(s32[3]{0:T(128)} %pad_add_fusion.place, bf16[272,768]{1,0:T(8,128)(2,1)} %get-tuple-element.246.refs_0_.refs_16_, bf16[272,768]{1,0:T(8,128)(2,1)} %copy-done.2, bf16[144,768]{1,0:T(8,128)(2,1)} %copy-done.5, ...), custom_call_target="tpu_custom_call" | custom-call | bytes 2359296 | tf_op jit(solution)/shard_map/shards/pallas_call | solution.py:152
  21.1 2.5 %collective-permute-start.8 = (bf16[528,256]{1,0:T(8,128)(2,1)}, bf16[528,256]{1,0:T(8,128)(2,1)S(1)}, u32[]{:S(2)}, u32[]{:S(2)}) collective-permute-start(bf16[528,256]{1,0:T(8,128)(2,1)} %get-tuple-element.222), channel_id=1, source_target_pairs={{0,8},{1,9},{2,10},{3,11},{4,12},{5,13},{6,14},{7,15},{8,0},{9,1},... | collective-permute-start | bytes 811016 | tf_op jit(solution)/shard_map/ppermute | solution.py:37
  23.6 0.5 collective-permute-start.5
  24.1 1.3 collective-permute-start.7
  25.4 1.2 collective-permute-start.9
  26.6 9.4 %collective-permute-done.8.refs_18_ = bf16[528,256]{1,0:T(8,128)(2,1)S(1)} collective-permute-done((bf16[528,256]{1,0:T(8,128)(2,1)}, bf16[528,256]{1,0:T(8,128)(2,1)S(1)}, u32[]{:S(2)}, u32[]{:S(2)}) %collective-permute-start.8) | collective-permute-done | bytes 270368 | tf_op jit(solution)/shard_map/ppermute | solution.py:37
  36.0 1.1 collective-permute-start.4
  37.1 1.3 collective-permute-start.3
  38.4 8.9 %collective-permute-done.3.refs_12_ = bf16[256,768]{1,0:T(8,128)(2,1)S(1)} collective-permute-done((bf16[256,768]{1,0:T(8,128)(2,1)}, bf16[256,768]{1,0:T(8,128)(2,1)S(1)}, u32[]{:S(2)}, u32[]{:S(2)}) %collective-permute-start.3) | collective-permute-done | bytes 393248 | tf_op jit(solution)/shard_map/ppermute | solution.py:37
  47.3 0.7 copy-done.15
  48.1 1.3 collective-permute-start.14
  49.4 1.3 collective-permute-start.13
  50.7 1.0 pad_maximum_fusion.3
  51.7 0.2 collective-permute-start.11
  51.9 2.7 %collective-permute-start.10 = (bf16[64,4096]{1,0:T(8,128)(2,1)S(1)}, bf16[64,4096]{1,0:T(8,128)(2,1)S(1)}, u32[]{:S(2)}, u32[]{:S(2)}) collective-permute-start(bf16[64,4096]{1,0:T(8,128)(2,1)S(1)} %collective-permute-done.9.refs_6_), channel_id=1, source_target_pairs={{0,1},{1,0},{2,3},{3,2},{4,5},{5,4},{6,7},{7,6},{8,9},{9,8},{10,11... | collective-permute-start | bytes 1572872 | tf_op jit(solution)/shard_map/ppermute | solution.py:37
  54.6 3.0 %collective-permute-start.12 = (bf16[512,256]{1,0:T(8,128)(2,1)S(1)}, bf16[512,256]{1,0:T(8,128)(2,1)S(1)}, u32[]{:S(2)}, u32[]{:S(2)}) collective-permute-start(bf16[512,256]{1,0:T(8,128)(2,1)S(1)} %copy-done.21), channel_id=1, source_target_pairs={{0,8},{1,9},{2,10},{3,11},{4,12},{5,13},{6,14},{7,15},{8,0},{9,1},... | collective-permute-start | bytes 786440 | tf_op jit(solution)/shard_map/ppermute | solution.py:37
  57.6 8.9 %collective-permute-done.12.refs_20_ = bf16[512,256]{1,0:T(8,128)(2,1)S(1)} collective-permute-done((bf16[512,256]{1,0:T(8,128)(2,1)S(1)}, bf16[512,256]{1,0:T(8,128)(2,1)S(1)}, u32[]{:S(2)}, u32[]{:S(2)}) %collective-permute-start.12) | collective-permute-done | bytes 262176 | tf_op jit(solution)/shard_map/ppermute | solution.py:37
  66.5 2.4 %collective-permute-done.11.refs_19_ = bf16[1040,256]{1,0:T(8,128)(2,1)S(1)} collective-permute-done((bf16[1040,256]{1,0:T(8,128)(2,1)S(1)}, bf16[1040,256]{1,0:T(8,128)(2,1)S(1)}, u32[]{:S(2)}, u32[]{:S(2)}) %collective-permute-start.11) | collective-permute-done | bytes 532512 | tf_op jit(solution)/shard_map/ppermute | solution.py:37
  68.9 0.8 copy-done.23
  69.7 0.1 pad_maximum_fusion
  69.7 0.3 collective-permute-start.18
  70.0 3.3 %collective-permute-start.15 = (bf16[96,4096]{1,0:T(8,128)(2,1)S(1)}, bf16[96,4096]{1,0:T(8,128)(2,1)S(1)}, u32[]{:S(2)}, u32[]{:S(2)}) collective-permute-start(bf16[96,4096]{1,0:T(8,128)(2,1)S(1)} %collective-permute-done.14.refs_7_), channel_id=1, source_target_pairs={{0,1},{1,0},{2,3},{3,2},{4,5},{5,4},{6,7},{7,6},{8,9},{9,8},{10,11... | collective-permute-start | bytes 2359304 | tf_op jit(solution)/shard_map/ppermute | solution.py:37
  73.4 0.2 collective-permute-start.19
  73.6 3.6 %collective-permute-start.16 = (bf16[1024,256]{1,0:T(8,128)(2,1)S(1)}, bf16[1024,256]{1,0:T(8,128)(2,1)S(1)}, u32[]{:S(2)}, u32[]{:S(2)}) collective-permute-start(bf16[1024,256]{1,0:T(8,128)(2,1)S(1)} %pad_maximum_fusion.4), channel_id=1, source_target_pairs={{0,4},{1,5},{2,6},{3,7},{4,0},{5,1},{6,2},{7,3},{8,12},{9,13},{10,... | collective-permute-start | bytes 1572872 | tf_op jit(solution)/shard_map/ppermute | solution.py:37
  77.2 0.7 collective-permute-start.17
  77.9 16.0 %collective-permute-done.17.refs_18_ = bf16[512,256]{1,0:T(8,128)(2,1)} collective-permute-done((bf16[512,256]{1,0:T(8,128)(2,1)S(1)}, bf16[512,256]{1,0:T(8,128)(2,1)}, u32[]{:S(2)}, u32[]{:S(2)}) %collective-permute-start.17) | collective-permute-done | bytes 262176 | tf_op jit(solution)/shard_map/ppermute | solution.py:37
  93.9 1.1 collective-permute-done.16.refs_22_.refs_17_
  94.9 0.9 copy-done.9
  95.8 0.8 collective-permute-start.20
  96.6 1.9 %pad_maximum_fusion.1 = bf16[1536,256]{1,0:T(8,128)(2,1)} fusion(bf16[512,256]{1,0:T(8,128)(2,1)} %collective-permute-done.17.refs_18_, bf16[1024,256]{1,0:T(8,128)(2,1)S(1)} %collective-permute-done.16.refs_22_.refs_17_), kind=kLoop, calls=%fused_computation.1 | loop fusion | flops 1572864 | bytes 1572864 | tf_op jit(solution)/shard_map/concatenate | solution.py:457
  98.5 1.2 collective-permute-start.22
  99.8 0.8 collective-permute-start.21
  100.5 15.5 %project.2 = (bf16[1024,256]{1,0:T(8,128)(2,1)}, f32[1024,256]{1,0:T(8,128)}, bf16[768,256]{1,0:T(8,128)(2,1)}, bf16[768,256]{1,0:T(8,128)(2,1)}, bf16[1024,512]{1,0:T(8,128)(2,1)}) custom-call(s32[3]{0:T(128)} %pad_add_fusion.place, bf16[64,4096]{1,0:T(8,128)(2,1)} %get-tuple-element.230.refs_0_, bf16[96,4096]{1,0:T(8,128)(2,1)} %get-tuple-element.231.refs_1_, ...), custom_call_target="tpu_custom_call" | custom-call | flops 4294967296 | bytes 13631488 | tf_op jit(solution)/shard_map/project/pallas_call | solution.py:271
  116.0 1.6 collective-permute-done.22.refs_20_.refs_3_
  117.6 0.7 convert_reduce_fusion
  118.3 0.8 slice_reduce_fusion.2
  119.1 1.3 collective-permute-start.25
  120.4 3.4 %collective-permute-start.23 = (bf16[768,256]{1,0:T(8,128)(2,1)}, bf16[768,256]{1,0:T(8,128)(2,1)}, u32[]{:S(2)}, u32[]{:S(2)}) collective-permute-start(bf16[768,256]{1,0:T(8,128)(2,1)} %get-tuple-element.226), channel_id=1, source_target_pairs={{0,4},{1,5},{2,6},{3,7},{4,8},{5,9},{6,10},{7,11},{8,12},{9,13},{1... | collective-permute-start | bytes 1179656 | tf_op jit(solution)/shard_map/ppermute | solution.py:48
  123.8 1.5 collective-permute-start.24
  125.3 0.7 slice_reduce_fusion
  126.0 9.3 %project.3.refs_1_ = f32[1024,256]{1,0:T(8,128)} custom-call(s32[3]{0:T(128)} %pad_add_fusion.place, bf16[64,4096]{1,0:T(8,128)(2,1)} %get-tuple-element.230.refs_0_, bf16[96,4096]{1,0:T(8,128)(2,1)} %get-tuple-element.231.refs_1_, bf16[96,4096]{1,0:T(8,128)(2,1)} %get-tuple-element.232.refs_2_, bf16[64,4096]{1,0:T(8,128)(2,1)} %copy-done.13, ...), custom_call_target="tpu_custom_call" | custom-call | flops 1879048192 | bytes 10747904 | tf_op jit(solution)/shard_map/project/pallas_call | solution.py:271
  135.4 0.1 reshape.13
  135.5 0.7 convert_reduce_fusion.1
  136.2 0.5 subtract_add_fusion.first_ref
  136.7 8.4 %attend.3 = (bf16[256,512]{1,0:T(8,128)(2,1)}, bf16[256,512]{1,0:T(8,128)(2,1)}, bf16[256,512]{1,0:T(8,128)(2,1)}) custom-call(s32[8]{0:T(128)} %subtract_add_fusion.first_ref, s32[8]{0:T(128)} %get-tuple-element.255.count_ref, bf16[768,256]{1,0:T(8,128)(2,1)} %collective-permute-done.23.before, bf16[1024,256]{1,0:T(8,128)(2,1)} %get-tuple-element.227.own, ...), custom_call_target="tpu_custom_call" | custom-call | flops 1409286144 | bytes 1835008 | tf_op jit(solution)/shard_map/attend/pallas_call | solution.py:380
  145.1 1.7 %collective-permute-start.26 = (bf16[256,512]{1,0:T(8,128)(2,1)}, bf16[256,512]{1,0:T(8,128)(2,1)S(1)}, u32[]{:S(2)}, u32[]{:S(2)}) collective-permute-start(bf16[256,512]{1,0:T(8,128)(2,1)} %get-tuple-element.252), channel_id=1, source_target_pairs={{0,1},{1,0},{2,3},{3,2},{4,5},{5,4},{6,7},{7,6},{8,9},{9,8},{10,11... | collective-permute-start | bytes 786440 | tf_op jit(solution)/shard_map/ppermute | solution.py:37
  146.8 1.3 collective-permute-start.27
  148.1 0.4 collective-permute-start.28
  148.5 5.2 %attend.2.refs_0_ = bf16[256,512]{1,0:T(8,128)(2,1)} custom-call(s32[8]{0:T(128)} %subtract_add_fusion.first_ref, s32[8]{0:T(128)} %get-tuple-element.255.count_ref, bf16[768,256]{1,0:T(8,128)(2,1)} %collective-permute-done.23.before, bf16[1024,256]{1,0:T(8,128)(2,1)} %get-tuple-element.227.own, bf16[768,256]{1,0:T(8,128)(2,1)} %collective-permute-done.24.after, ...), custom_call_target="tpu_custom_call" | custom-call | flops 469762048 | bytes 1835008 | tf_op jit(solution)/shard_map/attend/pallas_call | solution.py:380
  153.7 1.3 collective-permute-done.27.refs_2_
  154.9 5.7 %collective-permute-done.28.refs_3_ = bf16[256,512]{1,0:T(8,128)(2,1)S(1)} collective-permute-done((bf16[256,512]{1,0:T(8,128)(2,1)}, bf16[256,512]{1,0:T(8,128)(2,1)S(1)}, u32[]{:S(2)}, u32[]{:S(2)}) %collective-permute-start.28) | collective-permute-done | bytes 262176 | tf_op jit(solution)/shard_map/ppermute | solution.py:37
  160.7 0.7 copy-done.19
  161.4 2.2 %assemble.1 = bf16[256,2048]{1,0:T(8,128)(2,1)} custom-call(s32[3]{0:T(128)} %pad_add_fusion.place, bf16[256,512]{1,0:T(8,128)(2,1)} %attend.2.refs_0_, bf16[256,512]{1,0:T(8,128)(2,1)} %copy-done.17, bf16[256,512]{1,0:T(8,128)(2,1)} %copy-done.18, bf16[256,512]{1,0:T(8,128)(2,1)} %copy-done.19), custom_call_target="tpu_custom_call" | custom-call | bytes 2097152 | tf_op jit(solution)/shard_map/assemble/pallas_call | solution.py:409
  (63 shorter events, 0.2 us)
Async XLA Ops:
  3.8 13.5 %collective-permute-start = (bf16[272,768]{1,0:T(8,128)(2,1)}, bf16[272,768]{1,0:T(8,128)(2,1)S(1)}, u32[]{:S(2)}, u32[]{:S(2)}) collective-permute-start(bf16[272,768]{1,0:T(8,128)(2,1)} %get-tuple-element.134), channel_id=1, source_target_pairs={{0,1},{1,0},{2,3},{3,2},{4,5},{5,4},{6,7},{7,6},{8,9},{9,8},{10,11... | collective-permute-start | bytes 1253384 | tf_op jit(solution)/shard_map/ppermute | solution.py:37
  4.0 8.6 %collective-permute-start.1 = (bf16[144,768]{1,0:T(8,128)(2,1)}, bf16[144,768]{1,0:T(8,128)(2,1)S(1)}, u32[]{:S(2)}, u32[]{:S(2)}) collective-permute-start(bf16[144,768]{1,0:T(8,128)(2,1)} %get-tuple-element.135), channel_id=1, source_target_pairs={{0,2},{1,3},{2,0},{3,1},{4,6},{5,7},{6,4},{7,5},{8,10},{9,11},{10,... | collective-permute-start | bytes 663560 | tf_op jit(solution)/shard_map/ppermute | solution.py:37
  6.7 10.7 %collective-permute-start.2 = (bf16[144,768]{1,0:T(8,128)(2,1)}, bf16[144,768]{1,0:T(8,128)(2,1)S(1)}, u32[]{:S(2)}, u32[]{:S(2)}) collective-permute-start(bf16[144,768]{1,0:T(8,128)(2,1)} %get-tuple-element.136), channel_id=1, source_target_pairs={{0,3},{1,2},{2,1},{3,0},{4,7},{5,6},{6,5},{7,4},{8,11},{9,10},{10,... | collective-permute-start | bytes 663560 | tf_op jit(solution)/shard_map/ppermute | solution.py:37
  12.6 4.7 %copy-start.5 = (bf16[144,768]{1,0:T(8,128)(2,1)}, bf16[144,768]{1,0:T(8,128)(2,1)S(1)}, u32[]{:S(2)}) copy-start(bf16[144,768]{1,0:T(8,128)(2,1)S(1)} %collective-permute-done.1.refs_2_.refs_14_) | copy-start | bytes 663556
  17.3 0.7 copy-start.6
  18.0 0.7 copy-start.2
  21.1 33.5 %copy-start.21 = (bf16[512,256]{1,0:T(8,128)(2,1)S(1)}, bf16[512,256]{1,0:T(8,128)(2,1)}, u32[]{:S(2)}) copy-start(bf16[512,256]{1,0:T(8,128)(2,1)} %get-tuple-element.168) | copy-start | bytes 786436
  21.1 14.9 %collective-permute-start.8 = (bf16[528,256]{1,0:T(8,128)(2,1)}, bf16[528,256]{1,0:T(8,128)(2,1)S(1)}, u32[]{:S(2)}, u32[]{:S(2)}) collective-permute-start(bf16[528,256]{1,0:T(8,128)(2,1)} %get-tuple-element.222), channel_id=1, source_target_pairs={{0,8},{1,9},{2,10},{3,11},{4,12},{5,13},{6,14},{7,15},{8,0},{9,1},... | collective-permute-start | bytes 811016 | tf_op jit(solution)/shard_map/ppermute | solution.py:37
  23.6 23.7 %collective-permute-start.5 = (bf16[96,4096]{1,0:T(8,128)(2,1)}, bf16[96,4096]{1,0:T(8,128)(2,1)}, u32[]{:S(2)}, u32[]{:S(2)}) collective-permute-start(bf16[96,4096]{1,0:T(8,128)(2,1)} %get-tuple-element.231.refs_1_), channel_id=1, source_target_pairs={{0,1},{1,0},{2,3},{3,2},{4,5},{5,4},{6,7},{7,6},{8,9},{9,8},{10,11... | collective-permute-start | bytes 2359304 | tf_op jit(solution)/shard_map/ppermute | solution.py:37
  24.1 23.2 %collective-permute-start.6 = (bf16[96,4096]{1,0:T(8,128)(2,1)}, bf16[96,4096]{1,0:T(8,128)(2,1)}, u32[]{:S(2)}, u32[]{:S(2)}) collective-permute-start(bf16[96,4096]{1,0:T(8,128)(2,1)} %get-tuple-element.232.refs_2_), channel_id=1, source_target_pairs={{0,1},{1,0},{2,3},{3,2},{4,5},{5,4},{6,7},{7,6},{8,9},{9,8},{10,11... | collective-permute-start | bytes 2359304 | tf_op jit(solution)/shard_map/ppermute | solution.py:37
  24.1 13.0 %collective-permute-start.7 = (bf16[528,256]{1,0:T(8,128)(2,1)}, bf16[528,256]{1,0:T(8,128)(2,1)S(1)}, u32[]{:S(2)}, u32[]{:S(2)}) collective-permute-start(bf16[528,256]{1,0:T(8,128)(2,1)} %get-tuple-element.222), channel_id=1, source_target_pairs={{0,4},{1,5},{2,6},{3,7},{4,0},{5,1},{6,2},{7,3},{8,12},{9,13},{10,... | collective-permute-start | bytes 811016 | tf_op jit(solution)/shard_map/ppermute | solution.py:37
  25.4 21.9 %collective-permute-start.9 = (bf16[64,4096]{1,0:T(8,128)(2,1)}, bf16[64,4096]{1,0:T(8,128)(2,1)S(1)}, u32[]{:S(2)}, u32[]{:S(2)}) collective-permute-start(bf16[64,4096]{1,0:T(8,128)(2,1)} %get-tuple-element.230.refs_0_), channel_id=1, source_target_pairs={{0,2},{1,3},{2,0},{3,1},{4,6},{5,7},{6,4},{7,5},{8,10},{9,11},{10,... | collective-permute-start | bytes 1572872 | tf_op jit(solution)/shard_map/ppermute | solution.py:37
  36.0 14.7 %copy-start.3 = (bf16[528,256]{1,0:T(8,128)(2,1)}, bf16[528,256]{1,0:T(8,128)(2,1)S(1)}, u32[]{:S(2)}) copy-start(bf16[528,256]{1,0:T(8,128)(2,1)S(1)} %collective-permute-done.8.refs_18_) | copy-start | bytes 811012
  36.0 11.3 %collective-permute-start.4 = (bf16[64,4096]{1,0:T(8,128)(2,1)}, bf16[64,4096]{1,0:T(8,128)(2,1)S(1)}, u32[]{:S(2)}, u32[]{:S(2)}) collective-permute-start(bf16[64,4096]{1,0:T(8,128)(2,1)} %get-tuple-element.230.refs_0_), channel_id=1, source_target_pairs={{0,1},{1,0},{2,3},{3,2},{4,5},{5,4},{6,7},{7,6},{8,9},{9,8},{10,11... | collective-permute-start | bytes 1572872 | tf_op jit(solution)/shard_map/ppermute | solution.py:37
  37.1 12.2 %copy-start.16 = (bf16[528,256]{1,0:T(8,128)(2,1)}, bf16[528,256]{1,0:T(8,128)(2,1)S(1)}, u32[]{:S(2)}) copy-start(bf16[528,256]{1,0:T(8,128)(2,1)S(1)} %collective-permute-done.7.refs_17_) | copy-start | bytes 811012
  37.1 10.2 %collective-permute-start.3 = (bf16[256,768]{1,0:T(8,128)(2,1)}, bf16[256,768]{1,0:T(8,128)(2,1)S(1)}, u32[]{:S(2)}, u32[]{:S(2)}) collective-permute-start(bf16[256,768]{1,0:T(8,128)(2,1)} %get-tuple-element.143), channel_id=1, source_target_pairs={{0,16},{1,17},{2,18},{3,19},{4,20},{5,21},{6,22},{7,23},{8,24},{9,... | collective-permute-start | bytes 1179656 | tf_op jit(solution)/shard_map/ppermute | solution.py:37
  47.3 0.8 copy-start.15
  47.3 21.5 %copy-start.12 = (bf16[64,4096]{1,0:T(8,128)(2,1)}, bf16[64,4096]{1,0:T(8,128)(2,1)S(1)}, u32[]{:S(2)}) copy-start(bf16[64,4096]{1,0:T(8,128)(2,1)S(1)} %collective-permute-done.9.refs_6_) | copy-start | bytes 1572868
  47.3 2.1 %copy-start.13 = (bf16[64,4096]{1,0:T(8,128)(2,1)}, bf16[64,4096]{1,0:T(8,128)(2,1)S(1)}, u32[]{:S(2)}) copy-start(bf16[64,4096]{1,0:T(8,128)(2,1)S(1)} %collective-permute-done.4.refs_3_) | copy-start | bytes 1572868
  48.1 20.8 %collective-permute-start.14 = (bf16[96,4096]{1,0:T(8,128)(2,1)}, bf16[96,4096]{1,0:T(8,128)(2,1)S(1)}, u32[]{:S(2)}, u32[]{:S(2)}) collective-permute-start(bf16[96,4096]{1,0:T(8,128)(2,1)} %get-tuple-element.231.refs_1_), channel_id=1, source_target_pairs={{0,2},{1,3},{2,0},{3,1},{4,6},{5,7},{6,4},{7,5},{8,10},{9,11},{10,... | collective-permute-start | bytes 2359304 | tf_op jit(solution)/shard_map/ppermute | solution.py:37
  49.4 24.0 %copy-start.7 = (bf16[96,4096]{1,0:T(8,128)(2,1)S(1)}, bf16[96,4096]{1,0:T(8,128)(2,1)}, u32[]{:S(2)}) copy-start(bf16[96,4096]{1,0:T(8,128)(2,1)} %get-tuple-element.232.refs_2_) | copy-start | bytes 2359300
  49.4 24.2 %copy-start.20 = (bf16[512,256]{1,0:T(8,128)(2,1)S(1)}, bf16[512,256]{1,0:T(8,128)(2,1)}, u32[]{:S(2)}) copy-start(bf16[512,256]{1,0:T(8,128)(2,1)} %get-tuple-element.189) | copy-start | bytes 786436
  49.4 19.4 %collective-permute-start.13 = (bf16[1056,256]{1,0:T(8,128)(2,1)S(1)}, bf16[1056,256]{1,0:T(8,128)(2,1)S(1)}, u32[]{:S(2)}, u32[]{:S(2)}) collective-permute-start(bf16[1056,256]{1,0:T(8,128)(2,1)S(1)} %pad_maximum_fusion.2), channel_id=1, source_target_pairs={{0,16},{1,17},{2,18},{3,19},{4,20},{5,21},{6,22},{7,23},{8,24},{9,... | collective-permute-start | bytes 1622024 | tf_op jit(solution)/shard_map/ppermute | solution.py:37
  51.7 17.1 %collective-permute-start.11 = (bf16[1040,256]{1,0:T(8,128)(2,1)S(1)}, bf16[1040,256]{1,0:T(8,128)(2,1)S(1)}, u32[]{:S(2)}, u32[]{:S(2)}) collective-permute-start(bf16[1040,256]{1,0:T(8,128)(2,1)S(1)} %pad_maximum_fusion.3), channel_id=1, source_target_pairs={{0,4},{1,5},{2,6},{3,7},{4,0},{5,1},{6,2},{7,3},{8,12},{9,13},{10,... | collective-permute-start | bytes 1597448 | tf_op jit(solution)/shard_map/ppermute | solution.py:37
  51.9 14.6 %collective-permute-start.10 = (bf16[64,4096]{1,0:T(8,128)(2,1)S(1)}, bf16[64,4096]{1,0:T(8,128)(2,1)S(1)}, u32[]{:S(2)}, u32[]{:S(2)}) collective-permute-start(bf16[64,4096]{1,0:T(8,128)(2,1)S(1)} %collective-permute-done.9.refs_6_), channel_id=1, source_target_pairs={{0,1},{1,0},{2,3},{3,2},{4,5},{5,4},{6,7},{7,6},{8,9},{9,8},{10,11... | collective-permute-start | bytes 1572872 | tf_op jit(solution)/shard_map/ppermute | solution.py:37
  54.6 11.9 %collective-permute-start.12 = (bf16[512,256]{1,0:T(8,128)(2,1)S(1)}, bf16[512,256]{1,0:T(8,128)(2,1)S(1)}, u32[]{:S(2)}, u32[]{:S(2)}) collective-permute-start(bf16[512,256]{1,0:T(8,128)(2,1)S(1)} %copy-done.21), channel_id=1, source_target_pairs={{0,8},{1,9},{2,10},{3,11},{4,12},{5,13},{6,14},{7,15},{8,0},{9,1},... | collective-permute-start | bytes 786440 | tf_op jit(solution)/shard_map/ppermute | solution.py:37
  66.4 7.2 %copy-start.4 = (bf16[512,256]{1,0:T(8,128)(2,1)}, bf16[512,256]{1,0:T(8,128)(2,1)S(1)}, u32[]{:S(2)}) copy-start(bf16[512,256]{1,0:T(8,128)(2,1)S(1)} %collective-permute-done.12.refs_20_) | copy-start | bytes 786436
  66.4 2.4 %copy-start.14 = (bf16[64,4096]{1,0:T(8,128)(2,1)}, bf16[64,4096]{1,0:T(8,128)(2,1)S(1)}, u32[]{:S(2)}) copy-start(bf16[64,4096]{1,0:T(8,128)(2,1)S(1)} %collective-permute-done.10.refs_9_) | copy-start | bytes 1572868
  68.8 4.8 %copy-start.11 = (bf16[1040,256]{1,0:T(8,128)(2,1)}, bf16[1040,256]{1,0:T(8,128)(2,1)S(1)}, u32[]{:S(2)}) copy-start(bf16[1040,256]{1,0:T(8,128)(2,1)S(1)} %collective-permute-done.11.refs_19_) | copy-start | bytes 1597444
  68.8 0.8 copy-start.23
  69.7 28.9 %copy-start.8 = (bf16[96,4096]{1,0:T(8,128)(2,1)}, bf16[96,4096]{1,0:T(8,128)(2,1)S(1)}, u32[]{:S(2)}) copy-start(bf16[96,4096]{1,0:T(8,128)(2,1)S(1)} %collective-permute-done.14.refs_7_) | copy-start | bytes 2359300
  69.7 25.2 %collective-permute-start.18 = (bf16[1552,256]{1,0:T(8,128)(2,1)S(1)}, bf16[1552,256]{1,0:T(8,128)(2,1)S(1)}, u32[]{:S(2)}, u32[]{:S(2)}) collective-permute-start(bf16[1552,256]{1,0:T(8,128)(2,1)S(1)} %pad_maximum_fusion), channel_id=1, source_target_pairs={{0,16},{1,17},{2,18},{3,19},{4,20},{5,21},{6,22},{7,23},{8,24},{9,... | collective-permute-start | bytes 2383880 | tf_op jit(solution)/shard_map/ppermute | solution.py:37
  70.0 24.9 %collective-permute-start.15 = (bf16[96,4096]{1,0:T(8,128)(2,1)S(1)}, bf16[96,4096]{1,0:T(8,128)(2,1)S(1)}, u32[]{:S(2)}, u32[]{:S(2)}) collective-permute-start(bf16[96,4096]{1,0:T(8,128)(2,1)S(1)} %collective-permute-done.14.refs_7_), channel_id=1, source_target_pairs={{0,1},{1,0},{2,3},{3,2},{4,5},{5,4},{6,7},{7,6},{8,9},{9,8},{10,11... | collective-permute-start | bytes 2359304 | tf_op jit(solution)/shard_map/ppermute | solution.py:37
  73.4 21.5 %collective-permute-start.19 = (bf16[96,4096]{1,0:T(8,128)(2,1)S(1)}, bf16[96,4096]{1,0:T(8,128)(2,1)S(1)}, u32[]{:S(2)}, u32[]{:S(2)}) collective-permute-start(bf16[96,4096]{1,0:T(8,128)(2,1)S(1)} %copy-done.7), channel_id=1, source_target_pairs={{0,2},{1,3},{2,0},{3,1},{4,6},{5,7},{6,4},{7,5},{8,10},{9,11},{10,... | collective-permute-start | bytes 2359304 | tf_op jit(solution)/shard_map/ppermute | solution.py:37
  73.6 21.3 %collective-permute-start.16 = (bf16[1024,256]{1,0:T(8,128)(2,1)S(1)}, bf16[1024,256]{1,0:T(8,128)(2,1)S(1)}, u32[]{:S(2)}, u32[]{:S(2)}) collective-permute-start(bf16[1024,256]{1,0:T(8,128)(2,1)S(1)} %pad_maximum_fusion.4), channel_id=1, source_target_pairs={{0,4},{1,5},{2,6},{3,7},{4,0},{5,1},{6,2},{7,3},{8,12},{9,13},{10,... | collective-permute-start | bytes 1572872 | tf_op jit(solution)/shard_map/ppermute | solution.py:37
  77.2 16.7 %collective-permute-start.17 = (bf16[512,256]{1,0:T(8,128)(2,1)S(1)}, bf16[512,256]{1,0:T(8,128)(2,1)}, u32[]{:S(2)}, u32[]{:S(2)}) collective-permute-start(bf16[512,256]{1,0:T(8,128)(2,1)S(1)} %copy-done.20), channel_id=1, source_target_pairs={{0,8},{1,9},{2,10},{3,11},{4,12},{5,13},{6,14},{7,15},{8,0},{9,1},... | collective-permute-start | bytes 786440 | tf_op jit(solution)/shard_map/ppermute | solution.py:37
  94.9 1.7 %copy-start.1 = (bf16[1024,256]{1,0:T(8,128)(2,1)}, bf16[1024,256]{1,0:T(8,128)(2,1)S(1)}, u32[]{:S(2)}) copy-start(bf16[1024,256]{1,0:T(8,128)(2,1)S(1)} %collective-permute-done.16.refs_22_.refs_17_) | copy-start | bytes 1572868
  94.9 0.9 copy-start.9
  94.9 4.8 %copy-start.10 = (bf16[96,4096]{1,0:T(8,128)(2,1)}, bf16[96,4096]{1,0:T(8,128)(2,1)S(1)}, u32[]{:S(2)}) copy-start(bf16[96,4096]{1,0:T(8,128)(2,1)S(1)} %collective-permute-done.19.refs_8_) | copy-start | bytes 2359300
  95.8 2.7 %copy-start.22 = (bf16[1552,256]{1,0:T(8,128)(2,1)}, bf16[1552,256]{1,0:T(8,128)(2,1)S(1)}, u32[]{:S(2)}) copy-start(bf16[1552,256]{1,0:T(8,128)(2,1)S(1)} %collective-permute-done.18.refs_23_) | copy-start | bytes 2383876
  95.8 4.7 %collective-permute-start.20 = (bf16[96,4096]{1,0:T(8,128)(2,1)S(1)}, bf16[96,4096]{1,0:T(8,128)(2,1)}, u32[]{:S(2)}, u32[]{:S(2)}) collective-permute-start(bf16[96,4096]{1,0:T(8,128)(2,1)S(1)} %collective-permute-done.19.refs_8_), channel_id=1, source_target_pairs={{0,1},{1,0},{2,3},{3,2},{4,5},{5,4},{6,7},{7,6},{8,9},{9,8},{10,11... | collective-permute-start | bytes 2359304 | tf_op jit(solution)/shard_map/ppermute | solution.py:37
  98.5 19.1 %collective-permute-start.22 = (bf16[1536,256]{1,0:T(8,128)(2,1)}, bf16[1536,256]{1,0:T(8,128)(2,1)S(1)}, u32[]{:S(2)}, u32[]{:S(2)}) collective-permute-start(bf16[1536,256]{1,0:T(8,128)(2,1)} %pad_maximum_fusion.1), channel_id=1, source_target_pairs={{0,16},{1,17},{2,18},{3,19},{4,20},{5,21},{6,22},{7,23},{8,24},{9,... | collective-permute-start | bytes 2359304 | tf_op jit(solution)/shard_map/ppermute | solution.py:37
  99.8 16.3 %collective-permute-start.21 = (bf16[512,256]{1,0:T(8,128)(2,1)}, bf16[512,256]{1,0:T(8,128)(2,1)}, u32[]{:S(2)}, u32[]{:S(2)}) collective-permute-start(bf16[512,256]{1,0:T(8,128)(2,1)} %collective-permute-done.17.refs_18_), channel_id=1, source_target_pairs={{0,4},{1,5},{2,6},{3,7},{4,0},{5,1},{6,2},{7,3},{8,12},{9,13},{10,... | collective-permute-start | bytes 786440 | tf_op jit(solution)/shard_map/ppermute | solution.py:37
  117.6 8.4 %copy-start = (bf16[1536,256]{1,0:T(8,128)(2,1)}, bf16[1536,256]{1,0:T(8,128)(2,1)S(1)}, u32[]{:S(2)}) copy-start(bf16[1536,256]{1,0:T(8,128)(2,1)S(1)} %collective-permute-done.22.refs_20_.refs_3_) | copy-start | bytes 2359300
  119.1 17.6 %collective-permute-start.25 = (bf16[512,256]{1,0:T(8,128)(2,1)}, bf16[512,256]{1,0:T(8,128)(2,1)}, u32[]{:S(2)}, u32[]{:S(2)}) collective-permute-start(bf16[512,256]{1,0:T(8,128)(2,1)} %collective-permute-done.21.refs_19_), channel_id=1, source_target_pairs={{0,16},{1,17},{2,18},{3,19},{4,20},{5,21},{6,22},{7,23},{8,24},{9,... | collective-permute-start | bytes 786440 | tf_op jit(solution)/shard_map/ppermute | solution.py:37
  120.4 16.3 %collective-permute-start.23 = (bf16[768,256]{1,0:T(8,128)(2,1)}, bf16[768,256]{1,0:T(8,128)(2,1)}, u32[]{:S(2)}, u32[]{:S(2)}) collective-permute-start(bf16[768,256]{1,0:T(8,128)(2,1)} %get-tuple-element.226), channel_id=1, source_target_pairs={{0,4},{1,5},{2,6},{3,7},{4,8},{5,9},{6,10},{7,11},{8,12},{9,13},{1... | collective-permute-start | bytes 1179656 | tf_op jit(solution)/shard_map/ppermute | solution.py:48
  123.8 12.9 %collective-permute-start.24 = (bf16[768,256]{1,0:T(8,128)(2,1)}, bf16[768,256]{1,0:T(8,128)(2,1)}, u32[]{:S(2)}, u32[]{:S(2)}) collective-permute-start(bf16[768,256]{1,0:T(8,128)(2,1)} %get-tuple-element.228), channel_id=1, source_target_pairs={{4,0},{5,1},{6,2},{7,3},{8,4},{9,5},{10,6},{11,7},{12,8},{13,9},{1... | collective-permute-start | bytes 1179656 | tf_op jit(solution)/shard_map/ppermute | solution.py:48
  145.1 8.5 %collective-permute-start.26 = (bf16[256,512]{1,0:T(8,128)(2,1)}, bf16[256,512]{1,0:T(8,128)(2,1)S(1)}, u32[]{:S(2)}, u32[]{:S(2)}) collective-permute-start(bf16[256,512]{1,0:T(8,128)(2,1)} %get-tuple-element.252), channel_id=1, source_target_pairs={{0,1},{1,0},{2,3},{3,2},{4,5},{5,4},{6,7},{7,6},{8,9},{9,8},{10,11... | collective-permute-start | bytes 786440 | tf_op jit(solution)/shard_map/ppermute | solution.py:37
  146.8 8.1 %collective-permute-start.27 = (bf16[256,512]{1,0:T(8,128)(2,1)}, bf16[256,512]{1,0:T(8,128)(2,1)S(1)}, u32[]{:S(2)}, u32[]{:S(2)}) collective-permute-start(bf16[256,512]{1,0:T(8,128)(2,1)} %get-tuple-element.253), channel_id=1, source_target_pairs={{0,2},{1,3},{2,0},{3,1},{4,6},{5,7},{6,4},{7,5},{8,10},{9,11},{10,... | collective-permute-start | bytes 786440 | tf_op jit(solution)/shard_map/ppermute | solution.py:37
  148.1 12.6 %collective-permute-start.28 = (bf16[256,512]{1,0:T(8,128)(2,1)}, bf16[256,512]{1,0:T(8,128)(2,1)S(1)}, u32[]{:S(2)}, u32[]{:S(2)}) collective-permute-start(bf16[256,512]{1,0:T(8,128)(2,1)} %get-tuple-element.254), channel_id=1, source_target_pairs={{0,3},{1,2},{2,1},{3,0},{4,7},{5,6},{6,5},{7,4},{8,11},{9,10},{10,... | collective-permute-start | bytes 786440 | tf_op jit(solution)/shard_map/ppermute | solution.py:37
  153.7 7.0 %copy-start.17 = (bf16[256,512]{1,0:T(8,128)(2,1)}, bf16[256,512]{1,0:T(8,128)(2,1)S(1)}, u32[]{:S(2)}) copy-start(bf16[256,512]{1,0:T(8,128)(2,1)S(1)} %collective-permute-done.26.refs_1_) | copy-start | bytes 786436
  154.9 5.7 %copy-start.18 = (bf16[256,512]{1,0:T(8,128)(2,1)}, bf16[256,512]{1,0:T(8,128)(2,1)S(1)}, u32[]{:S(2)}) copy-start(bf16[256,512]{1,0:T(8,128)(2,1)S(1)} %collective-permute-done.27.refs_2_) | copy-start | bytes 786436
  160.7 0.7 copy-start.19

commit v3 on v2

--- a/solution.py
+++ b/solution.py
@@ -167,30 +167,38 @@
     outs, (tokens, weights, total, token_sems, sems) = refs[:-5], refs[-5:]
     part = depth // groups
     group, layer, member = place[0], place[1], place[2]
-    span = tokens.shape[0] // 2
-    token_copies, offset = ([], []), 0
-    for i, ref in enumerate(sources):
-        there = tokens.at[pl.ds(offset, ref.shape[0])]
-        copy = pltpu.make_async_copy(ref, there, token_sems.at[i])
-        token_copies[offset // span].append(copy)
-        offset += ref.shape[0]
-    for copy in token_copies[0]:
-        copy.start()
-    plan, offset, copies = [], 0, 0
-    for described, parts in items:
-        deep = sum(depth if bits[2] is None else part for bits in described)
-        loads = []
-        for c, (source, first, column) in enumerate(parts):
-            copy = pltpu.make_async_copy(
-                stored[source].at[pl.ds(first, deep), pl.ds(column, chunk)],
-                weights.at[pl.ds(offset, deep), pl.ds(c * chunk, chunk)],
-                sems.at[copies],
+    layer_wide = team * depth
+    layers = sorted({described[0][0] for described, _ in items})
+    plan, offset, copies, token_copies = [], 0, 0, 0
+    for layer_bits in layers:
+        loads, matched, row = [], [], 0
+        first = pl.multiple_of((layer ^ layer_bits) * layer_wide, LANES)
+        for ref in sources:
+            here = pl.ds(first, layer_wide)
+            there = tokens.at[pl.ds(row, ref.shape[0]), here]
+            loads.append(
+                pltpu.make_async_copy(ref.at[:, here], there, token_sems.at[token_copies])
             )
+            row += ref.shape[0]
+            token_copies += 1
+        for described, parts in items:
+            if described[0][0] != layer_bits:
+                continue
+            deep = sum(depth if bits[2] is None else part for bits in described)
+            for c, (source, first, column) in enumerate(parts):
+                loads.append(
+                    pltpu.make_async_copy(
+                        stored[source].at[pl.ds(first, deep), pl.ds(column, chunk)],
+                        weights.at[pl.ds(offset, deep), pl.ds(c * chunk, chunk)],
+                        sems.at[copies],
+                    )
+                )
+                copies += 1
+            matched.append((described, offset, deep, len(parts) * chunk))
+            offset += deep
+        for copy in loads:
             copy.start()
-            loads.append(copy)
-            copies += 1
-        plan.append((described, offset, deep, loads))
-        offset += deep
+        plan.append((loads, matched))
 
     def columns_of(own, described):
         lefts = []
@@ -202,30 +210,26 @@
             lefts.append(tokens[own, pl.ds(pl.multiple_of(first, LANES), wide)])
         return lefts[0] if len(lefts) == 1 else jnp.concatenate(lefts, axis=1)
 
-    for half in range(2):
-        own = pl.ds(half * span, span)
-        for copy in token_copies[half]:
+    span = tokens.shape[0] // 2
+    for step, (loads, matched) in enumerate(plan):
+        for copy in loads:
             copy.wait()
-        if half == 0:
-            for copy in token_copies[1]:
-                copy.start()
-        for i, (described, offset, deep, loads) in enumerate(plan):
-            if half == 0:
-                for copy in loads:
-                    copy.wait()
-            wide = len(loads) * chunk
-            right = weights[pl.ds(offset, deep), :wide]
-            term = jnp.dot(
-                columns_of(own, described), right, preferred_element_type=jnp.float32
-            )
-            if i == 0:
-                total[own, :wide] = term
-            else:
-                total[own, :wide] += term
+        for half in range(2):
+            own = pl.ds(half * span, span)
+            for i, (described, offset, deep, wide) in enumerate(matched):
+                right = weights[pl.ds(offset, deep), :wide]
+                term = jnp.dot(
+                    columns_of(own, described), right, preferred_element_type=jnp.float32
+                )
+                if i == 0 and step == 0:
+                    total[own, :wide] = term
+                else:
+                    total[own, :wide] += term
+    if wanted:
         column = 0
-        for described in rest if wanted else ():
-            left = columns_of(own, described)
-            outs[-1][own, column : column + left.shape[1]] = left
+        for described in rest:
+            left = columns_of(pl.ds(0, tokens.shape[0]), described)
+            outs[-1][:, column : column + left.shape[1]] = left
             column += left.shape[1]
     rows = total.shape[0] // team
     chunks = total.shape[1] // chunk
@@ -287,7 +291,7 @@
             pltpu.VMEM((count, width), jnp.bfloat16),
             pltpu.VMEM((deep, chunks * chunk), jnp.bfloat16),
             pltpu.VMEM((count, chunks * chunk), jnp.float32),
-            pltpu.SemaphoreType.DMA((len(tokens),)),
+            pltpu.SemaphoreType.DMA((len(tokens) * width // (team * depth),)),
             pltpu.SemaphoreType.DMA((copies,)),
         ],
         compiler_params=PARAMS,
@@ -435,8 +439,8 @@
         chunk = 2 * HD
         packed = pack(place, passage_blocks, [w_key, w_value, w_query], team, groups)
         moved = [swap(packed[r], team, 0, 0, r) for r in range(1, team)]
-        steps = range(1, 4)
-        lengths = [rows * n // 16 for n in (4, 6, 6)]
+        steps = range(1, 2)
+        lengths = [rows]
         normed = normalize(tie(tokens, packed[0]), norm_gain, lengths)
         *shards, far = make_shards(
             tie(place, normed[0]), packed[0], moved, widths, depth, groups, blocks
@@ -488,7 +492,11 @@
             return items, rest, late
 
         for phase in range(1, chunks + hops + 1):
-            arrays = lax.optimization_barrier(arrays)
+            long = arrays.pop("tokens1", None) if phase < chunks + hops - 1 else None
+            if phase < chunks + hops:
+                arrays = lax.optimization_barrier(arrays)
+            if long is not None:
+                arrays["tokens1"] = long
             sends = []
             ways = {}
             for c in range(chunks):
@@ -513,9 +521,8 @@
                     first += n
             if phase in steps:
                 sends.append((0, 0, 2, f"tokens{phase}", arrays[f"normed{phase}"]))
-            if phase - 1 in steps:
-                value = arrays[f"tokens{phase - 1}"]
-                sends.append((0, 0, 1, f"diagonal{phase - 1}", value))
+            if phase == chunks + hops - 1:
+                sends.append((0, 0, 1, "diagonal1", arrays["tokens1"]))
             if phase == 1:
                 for i in steps:
                     sends.append((0, 0, 1, f"near{i}", arrays[f"normed{i}"]))

time: 164 us -> 142 us (0.87)
  starting transfers between devices: 39.6 us -> 30.9 us
  Pallas kernels: 49.8 us -> 42.2 us
  waiting for transfers between devices: 62.2 us -> 56.1 us
    ppermute x27 -> x21, starting transfers between devices: 34.7 us -> 25.5 us  [swap(): return lax.ppermute(value, AXES, pairs)]
    pallas_call x2, Pallas kernels: 24.8 us -> 16.8 us  [project(): pl.pallas_call(functools.partial(project_kernel, items, (len(tokens), len...]
    ppermute x27 -> x21, waiting for transfers between devices: 62.2 us -> 54.5 us  [swap(): return lax.ppermute(value, AXES, pairs)]
    unnamed x48 -> x34, local copies, waits for them, and re-layouts: 4.6 us -> 4.76 us
  transfers between devices with their start and end apart: 29 -> 23, of which waited for: 11 -> 11; matrix products, arithmetic and copies ran while one was open for 3% -> 5% of each run, Pallas kernels for 21% -> 18%
where the time goes in v3:
time: 142 us
  waiting for transfers between devices  56.1 us (40%)
  Pallas kernels  42.2 us (30%)
  starting transfers between devices  30.9 us (22%)
  local copies, waits for them, and re-layouts  6.43 us (5%)
  other arithmetic  5.81 us (4%)
    ppermute x21, waiting for transfers between devices, swap(): return lax.ppermute(value, AXES, pairs)  54.5 us
    ppermute x21, starting transfers between devices, swap(): return lax.ppermute(value, AXES, pairs)  25.5 us
    pallas_call x2, Pallas kernels, project(): pl.pallas_call(functools.partial(project_kernel, items, (len(tokens), len...  16.8 us
    pallas_call x2, Pallas kernels, attend(): pl.pallas_call(functools.partial(attend_kernel, base, block, deep, firsts...  13.6 us
    ppermute x2, starting transfers between devices, from_layer(): return lax.ppermute(value, AXES, pairs)  5.39 us
    unnamed x34, local copies, waits for them, and re-layouts  4.76 us
    pallas_call x1, Pallas kernels, normalize(): pl.pallas_call(norm_kernel, out_shape=[jax.ShapeDtypeStruct((n, width), j...  4.07 us
    pallas_call x1, Pallas kernels, pack(): pl.pallas_call(functools.partial(pack_kernel, team, depth // groups, len(...  3.18 us
  transfers between devices with their start and end apart: 23, of which 11 were waited for; matrix products, arithmetic and copies ran while one was open for 5% of the time, Pallas kernels for 18%

profile of v3, /device:TPU:1, one launch (start us, length us, event | category | flops | bytes accessed | tf_op | source)
XLA Modules:
  0.0 141.6 jit_solution(881572195341552835)
XLA Ops:
  0.0 0.7 pad_add_fusion.place
  0.7 3.2 %pack.1 = (bf16[272,768]{1,0:T(8,128)(2,1)}, bf16[272,768]{1,0:T(8,128)(2,1)}, bf16[144,768]{1,0:T(8,128)(2,1)}, bf16[144,768]{1,0:T(8,128)(2,1)}) custom-call(s32[3]{0:T(128)} %pad_add_fusion.place, s32[2]{0:T(128)} %numbers.1, bf16[256,512]{1,0:T(8,128)(2,1)} %refs_0_.1, bf16[256,512]{1,0:T(8,128)(2,1)} %refs_1_.1, bf16[256,2048]{1,0:T(8,128)(2,1)} %refs_2_.1), custom_call_target="tpu_custom_call" | custom-call | bytes 3145728 | tf_op jit(solution)/shard_map/pack/pallas_call | solution.py:109
  3.8 0.1 collective-permute-start
  4.0 2.7 %collective-permute-start.1 = (bf16[144,768]{1,0:T(8,128)(2,1)}, bf16[144,768]{1,0:T(8,128)(2,1)S(1)}, u32[]{:S(2)}, u32[]{:S(2)}) collective-permute-start(bf16[144,768]{1,0:T(8,128)(2,1)} %get-tuple-element.79), channel_id=1, source_target_pairs={{0,2},{1,3},{2,0},{3,1},{4,6},{5,7},{6,4},{7,5},{8,10},{9,11},{10,... | collective-permute-start | bytes 663560 | tf_op jit(solution)/shard_map/ppermute | solution.py:37
  6.7 0.0 collective-permute-start.2
  6.7 4.1 %normalize.1.refs_0_ = bf16[256,4096]{1,0:T(8,128)(2,1)} custom-call(bf16[256,4096]{1,0:T(8,128)(2,1)} %tokens_ref, f32[1,4096]{1,0:T(1,128)} %bitcast.8), custom_call_target="tpu_custom_call" | custom-call | flops 6291456 | bytes 4194304 | tf_op jit(solution)/shard_map/normalize/pallas_call | solution.py:66
  10.8 1.8 %collective-permute-done.1.refs_2_.refs_6_ = bf16[144,768]{1,0:T(8,128)(2,1)S(1)} collective-permute-done((bf16[144,768]{1,0:T(8,128)(2,1)}, bf16[144,768]{1,0:T(8,128)(2,1)S(1)}, u32[]{:S(2)}, u32[]{:S(2)}) %collective-permute-start.1) | collective-permute-done | bytes 221216 | tf_op jit(solution)/shard_map/ppermute | solution.py:37
  12.6 4.7 %collective-permute-done.2.refs_3_.refs_7_ = bf16[144,768]{1,0:T(8,128)(2,1)S(1)} collective-permute-done((bf16[144,768]{1,0:T(8,128)(2,1)}, bf16[144,768]{1,0:T(8,128)(2,1)S(1)}, u32[]{:S(2)}, u32[]{:S(2)}) %collective-permute-start.2) | collective-permute-done | bytes 221216 | tf_op jit(solution)/shard_map/ppermute | solution.py:37
  17.3 0.0 collective-permute-done.refs_1_.refs_5_
  17.3 0.7 copy-done.7
  18.0 0.8 copy-done.3
  18.8 2.3 %shards.1 = (bf16[528,256]{1,0:T(8,128)(2,1)}, bf16[512,256]{1,0:T(8,128)(2,1)}, bf16[512,256]{1,0:T(8,128)(2,1)}, bf16[256,768]{1,0:T(8,128)(2,1)}) custom-call(s32[3]{0:T(128)} %pad_add_fusion.place, bf16[272,768]{1,0:T(8,128)(2,1)} %get-tuple-element.131.refs_0_.refs_8_, bf16[272,768]{1,0:T(8,128)(2,1)} %copy-done.3, bf16[144,768]{1,0:T(8,128)(2,1)} %copy-done.6, ...), custom_call_target="tpu_custom_call" | custom-call | bytes 2359296 | tf_op jit(solution)/shard_map/shards/pallas_call | solution.py:152
  21.1 0.4 collective-permute-start.4
  21.5 1.3 collective-permute-start.3
  22.8 1.3 collective-permute-start.5
  24.0 2.3 %collective-permute-start.6 = (bf16[528,256]{1,0:T(8,128)(2,1)}, bf16[528,256]{1,0:T(8,128)(2,1)S(1)}, u32[]{:S(2)}, u32[]{:S(2)}) collective-permute-start(bf16[528,256]{1,0:T(8,128)(2,1)} %get-tuple-element.120), channel_id=1, source_target_pairs={{0,8},{1,9},{2,10},{3,11},{4,12},{5,13},{6,14},{7,15},{8,0},{9,1},... | collective-permute-start | bytes 811016 | tf_op jit(solution)/shard_map/ppermute | solution.py:37
  26.4 1.2 collective-permute-start.13
  27.6 8.5 %collective-permute-done.5.refs_9_ = bf16[528,256]{1,0:T(8,128)(2,1)S(1)} collective-permute-done((bf16[528,256]{1,0:T(8,128)(2,1)}, bf16[528,256]{1,0:T(8,128)(2,1)S(1)}, u32[]{:S(2)}, u32[]{:S(2)}) %collective-permute-start.5) | collective-permute-done | bytes 270368 | tf_op jit(solution)/shard_map/ppermute | solution.py:37
  36.1 0.0 collective-permute-done.6.refs_10_
  36.1 0.7 copy-done.9
  36.9 0.0 collective-permute-done.4.refs_1_
  36.9 0.0 copy-done.10
  37.0 0.4 collective-permute-start.9
  37.4 1.0 pad_maximum_fusion.3
  38.4 2.4 %collective-permute-start.7 = (bf16[1040,256]{1,0:T(8,128)(2,1)S(1)}, bf16[1040,256]{1,0:T(8,128)(2,1)S(1)}, u32[]{:S(2)}, u32[]{:S(2)}) collective-permute-start(bf16[1040,256]{1,0:T(8,128)(2,1)S(1)} %pad_maximum_fusion.3), channel_id=1, source_target_pairs={{0,4},{1,5},{2,6},{3,7},{4,0},{5,1},{6,2},{7,3},{8,12},{9,13},{10,... | collective-permute-start | bytes 1597448 | tf_op jit(solution)/shard_map/ppermute | solution.py:37
  40.8 0.0 collective-permute-start.8
  40.8 15.2 %collective-permute-done.8.refs_12_ = bf16[512,256]{1,0:T(8,128)(2,1)S(1)} collective-permute-done((bf16[512,256]{1,0:T(8,128)(2,1)S(1)}, bf16[512,256]{1,0:T(8,128)(2,1)S(1)}, u32[]{:S(2)}, u32[]{:S(2)}) %collective-permute-start.8) | collective-permute-done | bytes 262176 | tf_op jit(solution)/shard_map/ppermute | solution.py:37
  56.1 0.5 collective-permute-done.7.refs_11_
  56.6 0.0 collective-permute-done.9.refs_13_
  56.6 0.1 pad_maximum_fusion
  56.6 1.3 collective-permute-start.12
  57.9 0.7 collective-permute-start.10
  58.6 2.1 %collective-permute-start.11 = (bf16[512,256]{1,0:T(8,128)(2,1)S(1)}, bf16[512,256]{1,0:T(8,128)(2,1)}, u32[]{:S(2)}, u32[]{:S(2)}) collective-permute-start(bf16[512,256]{1,0:T(8,128)(2,1)S(1)} %copy-done.14), channel_id=1, source_target_pairs={{0,8},{1,9},{2,10},{3,11},{4,12},{5,13},{6,14},{7,15},{8,0},{9,1},... | collective-permute-start | bytes 786440 | tf_op jit(solution)/shard_map/ppermute | solution.py:37
  60.7 11.9 %collective-permute-done.13.refs_2_ = bf16[256,4096]{1,0:T(8,128)(2,1)S(1)} collective-permute-done((bf16[256,4096]{1,0:T(8,128)(2,1)}, bf16[256,4096]{1,0:T(8,128)(2,1)S(1)}, u32[]{:S(2)}, u32[]{:S(2)}) %collective-permute-start.13) | collective-permute-done | bytes 2097184 | tf_op jit(solution)/shard_map/ppermute | solution.py:37
  72.6 3.3 %collective-permute-done.10.refs_14_.refs_9_ = bf16[1024,256]{1,0:T(8,128)(2,1)S(1)} collective-permute-done((bf16[1024,256]{1,0:T(8,128)(2,1)S(1)}, bf16[1024,256]{1,0:T(8,128)(2,1)S(1)}, u32[]{:S(2)}, u32[]{:S(2)}) %collective-permute-start.10) | collective-permute-done | bytes 524320 | tf_op jit(solution)/shard_map/ppermute | solution.py:37
  75.9 0.9 copy-done.16
  76.8 2.1 %collective-permute-start.14 = (bf16[256,4096]{1,0:T(8,128)(2,1)S(1)}, bf16[256,4096]{1,0:T(8,128)(2,1)}, u32[]{:S(2)}, u32[]{:S(2)}) collective-permute-start(bf16[256,4096]{1,0:T(8,128)(2,1)S(1)} %collective-permute-done.13.refs_2_), channel_id=1, source_target_pairs={{0,1},{1,0},{2,3},{3,2},{4,5},{5,4},{6,7},{7,6},{8,9},{9,8},{10,11... | collective-permute-start | bytes 6291464 | tf_op jit(solution)/shard_map/ppermute | solution.py:37
  78.9 2.7 %collective-permute-start.17 = (bf16[512,256]{1,0:T(8,128)(2,1)}, bf16[512,256]{1,0:T(8,128)(2,1)}, u32[]{:S(2)}, u32[]{:S(2)}) collective-permute-start(bf16[512,256]{1,0:T(8,128)(2,1)} %collective-permute-done.11.refs_10_), channel_id=1, source_target_pairs={{0,4},{1,5},{2,6},{3,7},{4,0},{5,1},{6,2},{7,3},{8,12},{9,13},{10,... | collective-permute-start | bytes 786440 | tf_op jit(solution)/shard_map/ppermute | solution.py:37
  81.6 1.9 %pad_maximum_fusion.1 = bf16[1536,256]{1,0:T(8,128)(2,1)} fusion(bf16[512,256]{1,0:T(8,128)(2,1)} %collective-permute-done.11.refs_10_, bf16[1024,256]{1,0:T(8,128)(2,1)S(1)} %collective-permute-done.10.refs_14_.refs_9_), kind=kLoop, calls=%fused_computation.1 | loop fusion | flops 1572864 | bytes 1572864 | tf_op jit(solution)/shard_map/concatenate | solution.py:461
  83.6 0.3 collective-permute-start.18
  83.8 0.8 convert_reduce_fusion
  84.6 0.8 slice_reduce_fusion.2
  85.4 0.8 slice_reduce_fusion
  86.2 0.1 reshape.13
  86.3 0.8 convert_reduce_fusion.1
  87.1 1.5 %collective-permute-done.17.refs_11_ = bf16[512,256]{1,0:T(8,128)(2,1)} collective-permute-done((bf16[512,256]{1,0:T(8,128)(2,1)}, bf16[512,256]{1,0:T(8,128)(2,1)}, u32[]{:S(2)}, u32[]{:S(2)}) %collective-permute-start.17) | collective-permute-done | bytes 262176 | tf_op jit(solution)/shard_map/ppermute | solution.py:37
  88.6 0.3 collective-permute-start.19
  88.9 9.8 %project.2 = (bf16[1024,256]{1,0:T(8,128)(2,1)}, f32[1024,256]{1,0:T(8,128)}, bf16[768,256]{1,0:T(8,128)(2,1)}, bf16[768,256]{1,0:T(8,128)(2,1)}, bf16[1024,512]{1,0:T(8,128)(2,1)}) custom-call(s32[3]{0:T(128)} %pad_add_fusion.place, bf16[256,4096]{1,0:T(8,128)(2,1)} %normalize.1.refs_0_, bf16[256,4096]{1,0:T(8,128)(2,1)} %collective-permute-done.4.refs_1_, ...), custom_call_target="tpu_custom_call" | custom-call | flops 4294967296 | bytes 13631488 | tf_op jit(solution)/shard_map/project/pallas_call | solution.py:275
  98.7 3.9 %collective-permute-start.15 = (bf16[768,256]{1,0:T(8,128)(2,1)}, bf16[768,256]{1,0:T(8,128)(2,1)}, u32[]{:S(2)}, u32[]{:S(2)}) collective-permute-start(bf16[768,256]{1,0:T(8,128)(2,1)} %get-tuple-element.136), channel_id=1, source_target_pairs={{0,4},{1,5},{2,6},{3,7},{4,8},{5,9},{6,10},{7,11},{8,12},{9,13},{1... | collective-permute-start | bytes 1179656 | tf_op jit(solution)/shard_map/ppermute | solution.py:48
  102.6 1.5 %collective-permute-start.16 = (bf16[768,256]{1,0:T(8,128)(2,1)}, bf16[768,256]{1,0:T(8,128)(2,1)}, u32[]{:S(2)}, u32[]{:S(2)}) collective-permute-start(bf16[768,256]{1,0:T(8,128)(2,1)} %get-tuple-element.138), channel_id=1, source_target_pairs={{4,0},{5,1},{6,2},{7,3},{8,4},{9,5},{10,6},{11,7},{12,8},{13,9},{1... | collective-permute-start | bytes 1179656 | tf_op jit(solution)/shard_map/ppermute | solution.py:48
  104.1 0.5 subtract_add_fusion.first_ref
  104.6 0.0 collective-permute-done.18.refs_12_.refs_3_
  104.7 0.9 copy-done
  105.5 6.9 %project.3.refs_1_ = f32[1024,256]{1,0:T(8,128)} custom-call(s32[3]{0:T(128)} %pad_add_fusion.place, bf16[256,4096]{1,0:T(8,128)(2,1)} %normalize.1.refs_0_, bf16[256,4096]{1,0:T(8,128)(2,1)} %collective-permute-done.4.refs_1_, bf16[256,4096]{1,0:T(8,128)(2,1)} %copy-done.1, bf16[256,4096]{1,0:T(8,128)(2,1)} %collective-permute-done.14.refs_3_, ...), custom_call_target="tpu_custom_call" | custom-call | flops 1879048192 | bytes 10747904 | tf_op jit(solution)/shard_map/project/pallas_call | solution.py:275
  112.5 1.6 %collective-permute-done.16.after = bf16[768,256]{1,0:T(8,128)(2,1)} collective-permute-done((bf16[768,256]{1,0:T(8,128)(2,1)}, bf16[768,256]{1,0:T(8,128)(2,1)}, u32[]{:S(2)}, u32[]{:S(2)}) %collective-permute-start.16) | collective-permute-done | bytes 393248 | tf_op jit(solution)/shard_map/ppermute | solution.py:48
  114.1 8.4 %attend.3 = (bf16[256,512]{1,0:T(8,128)(2,1)}, bf16[256,512]{1,0:T(8,128)(2,1)}, bf16[256,512]{1,0:T(8,128)(2,1)}) custom-call(s32[8]{0:T(128)} %subtract_add_fusion.first_ref, s32[8]{0:T(128)} %get-tuple-element.145.count_ref, bf16[768,256]{1,0:T(8,128)(2,1)} %collective-permute-done.15.before, bf16[1024,256]{1,0:T(8,128)(2,1)} %get-tuple-element.137.own, ...), custom_call_target="tpu_custom_call" | custom-call | flops 1409286144 | bytes 1835008 | tf_op jit(solution)/shard_map/attend/pallas_call | solution.py:384
  122.5 2.3 %collective-permute-start.20 = (bf16[256,512]{1,0:T(8,128)(2,1)}, bf16[256,512]{1,0:T(8,128)(2,1)S(1)}, u32[]{:S(2)}, u32[]{:S(2)}) collective-permute-start(bf16[256,512]{1,0:T(8,128)(2,1)} %get-tuple-element.142), channel_id=1, source_target_pairs={{0,1},{1,0},{2,3},{3,2},{4,5},{5,4},{6,7},{7,6},{8,9},{9,8},{10,11... | collective-permute-start | bytes 786440 | tf_op jit(solution)/shard_map/ppermute | solution.py:37
  124.8 1.2 collective-permute-start.21
  126.0 0.4 collective-permute-start.22
  126.4 5.2 %attend.2.refs_0_ = bf16[256,512]{1,0:T(8,128)(2,1)} custom-call(s32[8]{0:T(128)} %subtract_add_fusion.first_ref, s32[8]{0:T(128)} %get-tuple-element.145.count_ref, bf16[768,256]{1,0:T(8,128)(2,1)} %collective-permute-done.15.before, bf16[1024,256]{1,0:T(8,128)(2,1)} %get-tuple-element.137.own, bf16[768,256]{1,0:T(8,128)(2,1)} %collective-permute-done.16.after, ...), custom_call_target="tpu_custom_call" | custom-call | flops 469762048 | bytes 1835008 | tf_op jit(solution)/shard_map/attend/pallas_call | solution.py:384
  131.6 1.3 collective-permute-done.21.refs_2_
  132.9 5.7 %collective-permute-done.22.refs_3_ = bf16[256,512]{1,0:T(8,128)(2,1)S(1)} collective-permute-done((bf16[256,512]{1,0:T(8,128)(2,1)}, bf16[256,512]{1,0:T(8,128)(2,1)S(1)}, u32[]{:S(2)}, u32[]{:S(2)}) %collective-permute-start.22) | collective-permute-done | bytes 262176 | tf_op jit(solution)/shard_map/ppermute | solution.py:37
  138.6 0.7 copy-done.13
  139.3 2.2 %assemble.1 = bf16[256,2048]{1,0:T(8,128)(2,1)} custom-call(s32[3]{0:T(128)} %pad_add_fusion.place, bf16[256,512]{1,0:T(8,128)(2,1)} %attend.2.refs_0_, bf16[256,512]{1,0:T(8,128)(2,1)} %copy-done.11, bf16[256,512]{1,0:T(8,128)(2,1)} %copy-done.12, bf16[256,512]{1,0:T(8,128)(2,1)} %copy-done.13), custom_call_target="tpu_custom_call" | custom-call | bytes 2097152 | tf_op jit(solution)/shard_map/assemble/pallas_call | solution.py:413
  (37 shorter events, 0.2 us)
Async XLA Ops:
  3.8 13.5 %collective-permute-start = (bf16[272,768]{1,0:T(8,128)(2,1)}, bf16[272,768]{1,0:T(8,128)(2,1)S(1)}, u32[]{:S(2)}, u32[]{:S(2)}) collective-permute-start(bf16[272,768]{1,0:T(8,128)(2,1)} %get-tuple-element.78), channel_id=1, source_target_pairs={{0,1},{1,0},{2,3},{3,2},{4,5},{5,4},{6,7},{7,6},{8,9},{9,8},{10,11... | collective-permute-start | bytes 1253384 | tf_op jit(solution)/shard_map/ppermute | solution.py:37
  4.0 8.6 %collective-permute-start.1 = (bf16[144,768]{1,0:T(8,128)(2,1)}, bf16[144,768]{1,0:T(8,128)(2,1)S(1)}, u32[]{:S(2)}, u32[]{:S(2)}) collective-permute-start(bf16[144,768]{1,0:T(8,128)(2,1)} %get-tuple-element.79), channel_id=1, source_target_pairs={{0,2},{1,3},{2,0},{3,1},{4,6},{5,7},{6,4},{7,5},{8,10},{9,11},{10,... | collective-permute-start | bytes 663560 | tf_op jit(solution)/shard_map/ppermute | solution.py:37
  6.7 10.7 %collective-permute-start.2 = (bf16[144,768]{1,0:T(8,128)(2,1)}, bf16[144,768]{1,0:T(8,128)(2,1)S(1)}, u32[]{:S(2)}, u32[]{:S(2)}) collective-permute-start(bf16[144,768]{1,0:T(8,128)(2,1)} %get-tuple-element.80), channel_id=1, source_target_pairs={{0,3},{1,2},{2,1},{3,0},{4,7},{5,6},{6,5},{7,4},{8,11},{9,10},{10,... | collective-permute-start | bytes 663560 | tf_op jit(solution)/shard_map/ppermute | solution.py:37
  12.6 4.7 %copy-start.6 = (bf16[144,768]{1,0:T(8,128)(2,1)}, bf16[144,768]{1,0:T(8,128)(2,1)S(1)}, u32[]{:S(2)}) copy-start(bf16[144,768]{1,0:T(8,128)(2,1)S(1)} %collective-permute-done.1.refs_2_.refs_6_) | copy-start | bytes 663556
  17.3 0.7 copy-start.7
  18.0 0.8 copy-start.3
  21.1 19.7 %copy-start.15 = (bf16[512,256]{1,0:T(8,128)(2,1)S(1)}, bf16[512,256]{1,0:T(8,128)(2,1)}, u32[]{:S(2)}) copy-start(bf16[512,256]{1,0:T(8,128)(2,1)} %get-tuple-element.103) | copy-start | bytes 786436
  21.1 15.8 %collective-permute-start.4 = (bf16[256,4096]{1,0:T(8,128)(2,1)}, bf16[256,4096]{1,0:T(8,128)(2,1)}, u32[]{:S(2)}, u32[]{:S(2)}) collective-permute-start(bf16[256,4096]{1,0:T(8,128)(2,1)} %normalize.1.refs_0_), channel_id=1, source_target_pairs={{0,1},{1,0},{2,3},{3,2},{4,5},{5,4},{6,7},{7,6},{8,9},{9,8},{10,11... | collective-permute-start | bytes 6291464 | tf_op jit(solution)/shard_map/ppermute | solution.py:37
  21.5 14.6 %collective-permute-start.3 = (bf16[256,768]{1,0:T(8,128)(2,1)}, bf16[256,768]{1,0:T(8,128)(2,1)S(1)}, u32[]{:S(2)}, u32[]{:S(2)}) collective-permute-start(bf16[256,768]{1,0:T(8,128)(2,1)} %get-tuple-element.85), channel_id=1, source_target_pairs={{0,16},{1,17},{2,18},{3,19},{4,20},{5,21},{6,22},{7,23},{8,24},{9,... | collective-permute-start | bytes 1179656 | tf_op jit(solution)/shard_map/ppermute | solution.py:37
  22.8 13.4 %collective-permute-start.5 = (bf16[528,256]{1,0:T(8,128)(2,1)}, bf16[528,256]{1,0:T(8,128)(2,1)S(1)}, u32[]{:S(2)}, u32[]{:S(2)}) collective-permute-start(bf16[528,256]{1,0:T(8,128)(2,1)} %get-tuple-element.120), channel_id=1, source_target_pairs={{0,4},{1,5},{2,6},{3,7},{4,0},{5,1},{6,2},{7,3},{8,12},{9,13},{10,... | collective-permute-start | bytes 811016 | tf_op jit(solution)/shard_map/ppermute | solution.py:37
  24.0 12.1 %collective-permute-start.6 = (bf16[528,256]{1,0:T(8,128)(2,1)}, bf16[528,256]{1,0:T(8,128)(2,1)S(1)}, u32[]{:S(2)}, u32[]{:S(2)}) collective-permute-start(bf16[528,256]{1,0:T(8,128)(2,1)} %get-tuple-element.120), channel_id=1, source_target_pairs={{0,8},{1,9},{2,10},{3,11},{4,12},{5,13},{6,14},{7,15},{8,0},{9,1},... | collective-permute-start | bytes 811016 | tf_op jit(solution)/shard_map/ppermute | solution.py:37
  26.4 46.2 %collective-permute-start.13 = (bf16[256,4096]{1,0:T(8,128)(2,1)}, bf16[256,4096]{1,0:T(8,128)(2,1)S(1)}, u32[]{:S(2)}, u32[]{:S(2)}) collective-permute-start(bf16[256,4096]{1,0:T(8,128)(2,1)} %normalize.1.refs_0_), channel_id=1, source_target_pairs={{0,2},{1,3},{2,0},{3,1},{4,6},{5,7},{6,4},{7,5},{8,10},{9,11},{10,... | collective-permute-start | bytes 6291464 | tf_op jit(solution)/shard_map/ppermute | solution.py:37
  36.1 0.8 copy-start.10
  36.1 1.3 copy-start.4
  36.1 0.8 copy-start.9
  37.0 20.9 %copy-start.14 = (bf16[512,256]{1,0:T(8,128)(2,1)S(1)}, bf16[512,256]{1,0:T(8,128)(2,1)}, u32[]{:S(2)}) copy-start(bf16[512,256]{1,0:T(8,128)(2,1)} %get-tuple-element.118) | copy-start | bytes 786436
  37.0 19.6 %collective-permute-start.9 = (bf16[1056,256]{1,0:T(8,128)(2,1)S(1)}, bf16[1056,256]{1,0:T(8,128)(2,1)}, u32[]{:S(2)}, u32[]{:S(2)}) collective-permute-start(bf16[1056,256]{1,0:T(8,128)(2,1)S(1)} %pad_maximum_fusion.2), channel_id=1, source_target_pairs={{0,16},{1,17},{2,18},{3,19},{4,20},{5,21},{6,22},{7,23},{8,24},{9,... | collective-permute-start | bytes 1622024 | tf_op jit(solution)/shard_map/ppermute | solution.py:37
  38.4 18.2 %collective-permute-start.7 = (bf16[1040,256]{1,0:T(8,128)(2,1)S(1)}, bf16[1040,256]{1,0:T(8,128)(2,1)S(1)}, u32[]{:S(2)}, u32[]{:S(2)}) collective-permute-start(bf16[1040,256]{1,0:T(8,128)(2,1)S(1)} %pad_maximum_fusion.3), channel_id=1, source_target_pairs={{0,4},{1,5},{2,6},{3,7},{4,0},{5,1},{6,2},{7,3},{8,12},{9,13},{10,... | collective-permute-start | bytes 1597448 | tf_op jit(solution)/shard_map/ppermute | solution.py:37
  40.8 15.3 %collective-permute-start.8 = (bf16[512,256]{1,0:T(8,128)(2,1)S(1)}, bf16[512,256]{1,0:T(8,128)(2,1)S(1)}, u32[]{:S(2)}, u32[]{:S(2)}) collective-permute-start(bf16[512,256]{1,0:T(8,128)(2,1)S(1)} %copy-done.15), channel_id=1, source_target_pairs={{0,8},{1,9},{2,10},{3,11},{4,12},{5,13},{6,14},{7,15},{8,0},{9,1},... | collective-permute-start | bytes 786440 | tf_op jit(solution)/shard_map/ppermute | solution.py:37
  56.1 19.8 %copy-start.5 = (bf16[512,256]{1,0:T(8,128)(2,1)}, bf16[512,256]{1,0:T(8,128)(2,1)S(1)}, u32[]{:S(2)}) copy-start(bf16[512,256]{1,0:T(8,128)(2,1)S(1)} %collective-permute-done.8.refs_12_) | copy-start | bytes 786436
  56.6 19.3 %copy-start.8 = (bf16[1040,256]{1,0:T(8,128)(2,1)}, bf16[1040,256]{1,0:T(8,128)(2,1)S(1)}, u32[]{:S(2)}) copy-start(bf16[1040,256]{1,0:T(8,128)(2,1)S(1)} %collective-permute-done.7.refs_11_) | copy-start | bytes 1597444
  56.6 19.3 %collective-permute-start.12 = (bf16[1552,256]{1,0:T(8,128)(2,1)S(1)}, bf16[1552,256]{1,0:T(8,128)(2,1)S(1)}, u32[]{:S(2)}, u32[]{:S(2)}) collective-permute-start(bf16[1552,256]{1,0:T(8,128)(2,1)S(1)} %pad_maximum_fusion), channel_id=1, source_target_pairs={{0,16},{1,17},{2,18},{3,19},{4,20},{5,21},{6,22},{7,23},{8,24},{9,... | collective-permute-start | bytes 2383880 | tf_op jit(solution)/shard_map/ppermute | solution.py:37
  57.9 17.9 %collective-permute-start.10 = (bf16[1024,256]{1,0:T(8,128)(2,1)S(1)}, bf16[1024,256]{1,0:T(8,128)(2,1)S(1)}, u32[]{:S(2)}, u32[]{:S(2)}) collective-permute-start(bf16[1024,256]{1,0:T(8,128)(2,1)S(1)} %pad_maximum_fusion.4), channel_id=1, source_target_pairs={{0,4},{1,5},{2,6},{3,7},{4,0},{5,1},{6,2},{7,3},{8,12},{9,13},{10,... | collective-permute-start | bytes 1572872 | tf_op jit(solution)/shard_map/ppermute | solution.py:37
  58.6 13.9 %collective-permute-start.11 = (bf16[512,256]{1,0:T(8,128)(2,1)S(1)}, bf16[512,256]{1,0:T(8,128)(2,1)}, u32[]{:S(2)}, u32[]{:S(2)}) collective-permute-start(bf16[512,256]{1,0:T(8,128)(2,1)S(1)} %copy-done.14), channel_id=1, source_target_pairs={{0,8},{1,9},{2,10},{3,11},{4,12},{5,13},{6,14},{7,15},{8,0},{9,1},... | collective-permute-start | bytes 786440 | tf_op jit(solution)/shard_map/ppermute | solution.py:37
  72.6 9.1 %copy-start.1 = (bf16[256,4096]{1,0:T(8,128)(2,1)}, bf16[256,4096]{1,0:T(8,128)(2,1)S(1)}, u32[]{:S(2)}) copy-start(bf16[256,4096]{1,0:T(8,128)(2,1)S(1)} %collective-permute-done.13.refs_2_) | copy-start | bytes 6291460
  75.9 5.8 %copy-start.2 = (bf16[1024,256]{1,0:T(8,128)(2,1)}, bf16[1024,256]{1,0:T(8,128)(2,1)S(1)}, u32[]{:S(2)}) copy-start(bf16[1024,256]{1,0:T(8,128)(2,1)S(1)} %collective-permute-done.10.refs_14_.refs_9_) | copy-start | bytes 1572868
  75.9 0.9 copy-start.16
  76.8 12.1 %collective-permute-start.14 = (bf16[256,4096]{1,0:T(8,128)(2,1)S(1)}, bf16[256,4096]{1,0:T(8,128)(2,1)}, u32[]{:S(2)}, u32[]{:S(2)}) collective-permute-start(bf16[256,4096]{1,0:T(8,128)(2,1)S(1)} %collective-permute-done.13.refs_2_), channel_id=1, source_target_pairs={{0,1},{1,0},{2,3},{3,2},{4,5},{5,4},{6,7},{7,6},{8,9},{9,8},{10,11... | collective-permute-start | bytes 6291464 | tf_op jit(solution)/shard_map/ppermute | solution.py:37
  78.9 9.7 %collective-permute-start.17 = (bf16[512,256]{1,0:T(8,128)(2,1)}, bf16[512,256]{1,0:T(8,128)(2,1)}, u32[]{:S(2)}, u32[]{:S(2)}) collective-permute-start(bf16[512,256]{1,0:T(8,128)(2,1)} %collective-permute-done.11.refs_10_), channel_id=1, source_target_pairs={{0,4},{1,5},{2,6},{3,7},{4,0},{5,1},{6,2},{7,3},{8,12},{9,13},{10,... | collective-permute-start | bytes 786440 | tf_op jit(solution)/shard_map/ppermute | solution.py:37
  83.6 21.1 %collective-permute-start.18 = (bf16[1536,256]{1,0:T(8,128)(2,1)}, bf16[1536,256]{1,0:T(8,128)(2,1)S(1)}, u32[]{:S(2)}, u32[]{:S(2)}) collective-permute-start(bf16[1536,256]{1,0:T(8,128)(2,1)} %pad_maximum_fusion.1), channel_id=1, source_target_pairs={{0,16},{1,17},{2,18},{3,19},{4,20},{5,21},{6,22},{7,23},{8,24},{9,... | collective-permute-start | bytes 2359304 | tf_op jit(solution)/shard_map/ppermute | solution.py:37
  88.6 23.9 %collective-permute-start.19 = (bf16[512,256]{1,0:T(8,128)(2,1)}, bf16[512,256]{1,0:T(8,128)(2,1)}, u32[]{:S(2)}, u32[]{:S(2)}) collective-permute-start(bf16[512,256]{1,0:T(8,128)(2,1)} %collective-permute-done.17.refs_11_), channel_id=1, source_target_pairs={{0,16},{1,17},{2,18},{3,19},{4,20},{5,21},{6,22},{7,23},{8,24},{9,... | collective-permute-start | bytes 786440 | tf_op jit(solution)/shard_map/ppermute | solution.py:37
  98.7 13.8 %collective-permute-start.15 = (bf16[768,256]{1,0:T(8,128)(2,1)}, bf16[768,256]{1,0:T(8,128)(2,1)}, u32[]{:S(2)}, u32[]{:S(2)}) collective-permute-start(bf16[768,256]{1,0:T(8,128)(2,1)} %get-tuple-element.136), channel_id=1, source_target_pairs={{0,4},{1,5},{2,6},{3,7},{4,8},{5,9},{6,10},{7,11},{8,12},{9,13},{1... | collective-permute-start | bytes 1179656 | tf_op jit(solution)/shard_map/ppermute | solution.py:48
  102.6 11.5 %collective-permute-start.16 = (bf16[768,256]{1,0:T(8,128)(2,1)}, bf16[768,256]{1,0:T(8,128)(2,1)}, u32[]{:S(2)}, u32[]{:S(2)}) collective-permute-start(bf16[768,256]{1,0:T(8,128)(2,1)} %get-tuple-element.138), channel_id=1, source_target_pairs={{4,0},{5,1},{6,2},{7,3},{8,4},{9,5},{10,6},{11,7},{12,8},{13,9},{1... | collective-permute-start | bytes 1179656 | tf_op jit(solution)/shard_map/ppermute | solution.py:48
  104.7 0.9 copy-start
  122.5 9.1 %collective-permute-start.20 = (bf16[256,512]{1,0:T(8,128)(2,1)}, bf16[256,512]{1,0:T(8,128)(2,1)S(1)}, u32[]{:S(2)}, u32[]{:S(2)}) collective-permute-start(bf16[256,512]{1,0:T(8,128)(2,1)} %get-tuple-element.142), channel_id=1, source_target_pairs={{0,1},{1,0},{2,3},{3,2},{4,5},{5,4},{6,7},{7,6},{8,9},{9,8},{10,11... | collective-permute-start | bytes 786440 | tf_op jit(solution)/shard_map/ppermute | solution.py:37
  124.8 8.1 %collective-permute-start.21 = (bf16[256,512]{1,0:T(8,128)(2,1)}, bf16[256,512]{1,0:T(8,128)(2,1)S(1)}, u32[]{:S(2)}, u32[]{:S(2)}) collective-permute-start(bf16[256,512]{1,0:T(8,128)(2,1)} %get-tuple-element.143), channel_id=1, source_target_pairs={{0,2},{1,3},{2,0},{3,1},{4,6},{5,7},{6,4},{7,5},{8,10},{9,11},{10,... | collective-permute-start | bytes 786440 | tf_op jit(solution)/shard_map/ppermute | solution.py:37
  126.0 12.6 %collective-permute-start.22 = (bf16[256,512]{1,0:T(8,128)(2,1)}, bf16[256,512]{1,0:T(8,128)(2,1)S(1)}, u32[]{:S(2)}, u32[]{:S(2)}) collective-permute-start(bf16[256,512]{1,0:T(8,128)(2,1)} %get-tuple-element.144), channel_id=1, source_target_pairs={{0,3},{1,2},{2,1},{3,0},{4,7},{5,6},{6,5},{7,4},{8,11},{9,10},{10,... | collective-permute-start | bytes 786440 | tf_op jit(solution)/shard_map/ppermute | solution.py:37
  131.6 7.0 %copy-start.11 = (bf16[256,512]{1,0:T(8,128)(2,1)}, bf16[256,512]{1,0:T(8,128)(2,1)S(1)}, u32[]{:S(2)}) copy-start(bf16[256,512]{1,0:T(8,128)(2,1)S(1)} %collective-permute-done.20.refs_1_) | copy-start | bytes 786436
  132.9 5.7 %copy-start.12 = (bf16[256,512]{1,0:T(8,128)(2,1)}, bf16[256,512]{1,0:T(8,128)(2,1)S(1)}, u32[]{:S(2)}) copy-start(bf16[256,512]{1,0:T(8,128)(2,1)S(1)} %collective-permute-done.21.refs_2_) | copy-start | bytes 786436
  138.6 0.7 copy-start.13

commit v4 on v3

--- a/solution.py
+++ b/solution.py
@@ -11,9 +11,10 @@
 MOST_BLK = 7
 LANES = 128
 NOTES = 16
+LONG = ("normed", "far_tokens")
 AXES = ("groups", "seq")
 LOG2_E = 1.4426950408889634
-VMEM_LIMIT = 63 * 1024 * 1024
+VMEM_LIMIT = 64 * 1024 * 1024
 IN_VMEM = pl.BlockSpec(memory_space=pltpu.VMEM)
 IN_SMEM = pl.BlockSpec(memory_space=pltpu.SMEM)
 IN_HBM = pl.BlockSpec(memory_space=pltpu.HBM)
@@ -74,7 +75,7 @@
     )(tokens, norm_gain.reshape(1, width))
 
 
-def pack_kernel(team, part, count, place, numbers, *refs):
+def pack_kernel(team, part, notes, count, place, numbers, *refs):
     weights, outs = refs[:count], refs[count : count + team]
     loaded, sems = refs[count + team : -1], refs[-1]
     copies = [
@@ -83,33 +84,34 @@
     ]
     for copy in copies:
         copy.start()
-    row = lax.broadcasted_iota(jnp.int32, (NOTES, outs[0].shape[1]), 0)
-    noted = jnp.zeros((NOTES, outs[0].shape[1]), jnp.float32)
-    for i in range(numbers.shape[0]):
-        noted = jnp.where(row == i, numbers[i].astype(jnp.float32), noted)
-    noted = noted.astype(jnp.bfloat16)
-    for out in outs:
-        out[out.shape[0] - NOTES :, :] = noted
+    if notes:
+        row = lax.broadcasted_iota(jnp.int32, (notes, outs[0].shape[1]), 0)
+        noted = jnp.zeros((notes, outs[0].shape[1]), jnp.float32)
+        for i in range(numbers.shape[0]):
+            noted = jnp.where(row == i, numbers[i].astype(jnp.float32), noted)
+        noted = noted.astype(jnp.bfloat16)
+        for out in outs:
+            out[out.shape[0] - notes :, :] = noted
     column = 0
     for copy, weight in zip(copies, loaded):
         copy.wait()
         width = weight.shape[1] // team
         for r, out in enumerate(outs):
-            length = out.shape[0] - NOTES
+            length = out.shape[0] - notes
             first = 0 if r < 2 else pl.multiple_of(place[0] * part, part)
             columns = pl.ds(pl.multiple_of((place[2] ^ r) * width, width), width)
             out[:length, column : column + width] = weight[pl.ds(first, length), columns]
         column += width
 
 
-def pack(place, numbers, weights, team, groups):
+def pack(place, numbers, weights, team, groups, notes=0):
     depth = weights[0].shape[0]
     width = sum(weight.shape[1] for weight in weights) // team
     lengths = [depth if r < 2 else depth // groups for r in range(team)]
     return pl.pallas_call(
-        functools.partial(pack_kernel, team, depth // groups, len(weights)),
+        functools.partial(pack_kernel, team, depth // groups, notes, len(weights)),
         out_shape=[
-            jax.ShapeDtypeStruct((length + NOTES, width), jnp.bfloat16)
+            jax.ShapeDtypeStruct((length + notes, width), jnp.bfloat16)
             for length in lengths
         ],
         in_specs=[IN_SMEM] * 2 + [IN_HBM] * len(weights),
@@ -134,6 +136,8 @@
             column += width
         if r >= 2:
             far[(r - 2) * part : (r - 1) * part, :] = ref[rows, :]
+    if not blocks:
+        return
     noted_in = shards[0]
     row = lax.broadcasted_iota(jnp.int32, (NOTES, noted_in.shape[1]), 0)
     noted = jnp.zeros((NOTES, noted_in.shape[1]), jnp.float32)
@@ -144,10 +148,10 @@
     noted_in[team * part :, :] = noted.astype(jnp.bfloat16)
 
 
-def make_shards(place, packed, moved, widths, depth, groups, blocks):
+def make_shards(place, packed, moved, widths, depth, groups, blocks=0):
     part, width = depth // groups, packed.shape[1]
     team = 1 + len(moved)
-    shapes = [(team * part + (0 if i else NOTES), w) for i, w in enumerate(widths)]
+    shapes = [(team * part + (NOTES if blocks and not i else 0), w) for i, w in enumerate(widths)]
     shapes.append(((team - 2) * part, width))
     return pl.pallas_call(
         functools.partial(shards_kernel, team, part, blocks),
@@ -303,6 +307,46 @@
     )(place, *tokens, *[arrays[name] for name in names])
 
 
+def places_kernel(blocks, firsts, place, *refs):
+    ins, (first, count), (held, sems) = refs[:-4], refs[-4:-2], refs[-2:]
+    copies = []
+    for i, (ref, start) in enumerate(zip(ins, firsts)):
+        there = held.at[pl.ds(i * NOTES, NOTES)]
+        copies.append(pltpu.make_async_copy(ref.at[pl.ds(start, NOTES)], there, sems.at[i]))
+        copies[-1].start()
+    for copy in copies:
+        copy.wait()
+    ids = held[:, :LANES].astype(jnp.float32)
+    mine = ids[:NOTES]
+    same, less = jnp.zeros_like(mine), jnp.zeros_like(mine)
+    for i in range(len(ins)):
+        for k in range(blocks):
+            other = ids[i * NOTES + k : i * NOTES + k + 1]
+            same += (other == mine).astype(jnp.float32)
+            less += (other < mine).astype(jnp.float32)
+    count[...] = same.astype(jnp.int32)
+    first[...] = less.astype(jnp.int32) - place[1] * blocks + (MOST_BLK - 1)
+
+
+def places(place, noted, blocks):
+    shape = jax.ShapeDtypeStruct((NOTES, LANES), jnp.int32)
+    width = noted[0][0].shape[1]
+    first, count = pl.pallas_call(
+        functools.partial(places_kernel, blocks, [start for _, start in noted]),
+        out_shape=[shape] * 2,
+        in_specs=[IN_SMEM] + [IN_HBM] * len(noted),
+        out_specs=[IN_VMEM] * 2,
+        scratch_shapes=[
+            pltpu.VMEM((len(noted) * NOTES, width), jnp.bfloat16),
+            pltpu.SemaphoreType.DMA((len(noted),)),
+        ],
+        compiler_params=PARAMS,
+        cost_estimate=cost(0, 4 * NOTES * width * len(noted)),
+        name="places",
+    )(place, *[array for array, _ in noted])
+    return first, count
+
+
 def attend_kernel(
     base, block, deep, firsts, first_ref, count_ref, before, own, after, *refs
 ):
@@ -311,21 +355,20 @@
     per_out = outs[0].shape[0] // block
     total_blocks = per_out * len(outs)
     mine = pl.ds(base * block, total_blocks * block)
+    column = 0
+    for ref in ins[: firsts[0] - (2 + len(firsts[1]) if deep else 0)]:
+        query[:, column : column + ref.shape[1]] = ref[mine, :]
+        column += ref.shape[1]
     if deep:
-        *sums, left = ins[: len(firsts[1]) + 1]
-        weights = iter(ins[len(firsts[1]) + 1 :])
-        for c, (begun, starts) in enumerate(zip(sums, firsts[1])):
-            total = begun[mine, :]
-            for i, start in enumerate(starts):
-                total += jnp.dot(
-                    left[mine, i * deep : (i + 1) * deep],
-                    next(weights)[start : start + deep, :],
-                    preferred_element_type=jnp.float32,
-                )
-            wide = total.shape[1]
-            query[:, c * wide : (c + 1) * wide] = total.astype(jnp.bfloat16)
-    else:
-        query[...] = ins[0][mine, :]
+        begun, left, *weights = ins[firsts[0] - 2 - len(firsts[1]) :]
+        total = begun[mine, :]
+        for i, (weight, start) in enumerate(zip(weights, firsts[1])):
+            total += jnp.dot(
+                left[mine, i * deep : (i + 1) * deep],
+                weight[start : start + deep, :],
+                preferred_element_type=jnp.float32,
+            )
+        query[:, column:] = total.astype(jnp.bfloat16)
     offset = 0
     for ref in (before, own, after):
         window[offset : offset + ref.shape[0], :] = ref[...]
@@ -335,7 +378,7 @@
     row = lax.broadcasted_iota(jnp.int32, (span, 1), 0)
 
     def place_of(b):
-        return pl.ds(pl.multiple_of(first_ref[base + b] * block, block), span)
+        return pl.ds(pl.multiple_of(first_ref[base + b, 0] * block, block), span)
 
     def score(b):
         rows = pl.ds(b * block, block)
@@ -352,7 +395,7 @@
     scores = score(0)
     for b in range(total_blocks):
         upcoming = score(b + 1) if b + 1 < total_blocks else None
-        scores = jnp.where(row < count_ref[base + b] * block, scores, -1e30)
+        scores = jnp.where(row < count_ref[base + b, 0] * block, scores, -1e30)
         row_max = jnp.max(scores, axis=0, keepdims=True)
         weights = jnp.exp2((scores - row_max) * (HD ** (-0.5) * LOG2_E))
         row_total = jnp.sum(weights, axis=0, keepdims=True)
@@ -373,11 +416,11 @@
 
 def attend(first, count, query, before, own, after, block, base, rows, parts):
     if isinstance(query, tuple):
-        *sums, left, lates = query
-        ins = [*sums, left] + [array for late in lates for array, _ in late]
-        firsts = (len(ins), [[start for _, start in late] for late in lates])
-        deep = left.shape[1] // len(lates[0])
-        columns = sum(value.shape[1] for value in sums)
+        done, begun, left, late = query
+        ins = [*done, begun, left] + [array for array, _ in late]
+        firsts = (len(ins), [start for _, start in late])
+        deep = left.shape[1] // len(late)
+        columns = sum(value.shape[1] for value in done) + begun.shape[1]
     else:
         ins, firsts, deep, columns = [query], (1, []), 0, query.shape[1]
     span = before.shape[0] + own.shape[0] + after.shape[0]
@@ -400,27 +443,6 @@
     )(first, count, before, own, after, *ins)
 
 
-def assemble_kernel(place, *refs):
-    pieces, out = refs[:-1], refs[-1]
-    for r, piece in enumerate(pieces):
-        width = piece.shape[1]
-        first = pl.multiple_of((place[2] ^ r) * width, width)
-        out[:, pl.ds(first, width)] = piece[...]
-
-
-def assemble(place, pieces):
-    rows, width = pieces[0].shape
-    return pl.pallas_call(
-        assemble_kernel,
-        out_shape=jax.ShapeDtypeStruct((rows, width * len(pieces)), jnp.bfloat16),
-        in_specs=[IN_SMEM] + [IN_VMEM] * len(pieces),
-        out_specs=IN_VMEM,
-        compiler_params=PARAMS,
-        cost_estimate=cost(0, 4 * rows * width * len(pieces)),
-        name="assemble",
-    )(place, *pieces)
-
-
 def on_device(tokens, norm_gain, w_query, w_key, w_value, passage_blocks):
     groups, peers = lax.axis_size("groups"), lax.axis_size("seq")
     team = w_key.shape[1] // HD
@@ -437,23 +459,22 @@
 
     if depth // groups % LANES == 0 and team * blocks <= NOTES:
         chunk = 2 * HD
-        packed = pack(place, passage_blocks, [w_key, w_value, w_query], team, groups)
+        weights = [w_key, w_value, w_query]
+        packed = pack(place, passage_blocks, weights, team, groups, NOTES)
         moved = [swap(packed[r], team, 0, 0, r) for r in range(1, team)]
-        steps = range(1, 2)
-        lengths = [rows]
-        normed = normalize(tie(tokens, packed[0]), norm_gain, lengths)
+        (normed,) = normalize(tie(tokens, packed[0]), norm_gain, [rows])
         *shards, far = make_shards(
-            tie(place, normed[0]), packed[0], moved, widths, depth, groups, blocks
+            tie(place, normed), packed[0], moved, widths, depth, groups, blocks
         )
 
         chunks = len(shards)
         hops = max(bits.bit_count() for bits in range(layers))
-        arrays = {"own": packed[0], "far": far}
-        arrays.update({f"normed{i}": value for i, value in zip(steps, normed)})
-        arrays.update({f"moved{r}": value for r, value in enumerate(moved, 1)})
+        arrays = {"layer0": packed[0], "far": far, "normed": normed}
+        arrays["far_tokens"] = swap(tie(normed, *moved[1:]), team, 0, 0, 2)
+        arrays.update({f"layer{r}": value for r, value in enumerate(moved, 1)})
         arrays.update({f"shard{c}": shard for c, shard in enumerate(shards)})
         held = {(c, 0): (f"shard{c}", 0, shard.shape[0]) for c, shard in enumerate(shards)}
-        crossed, far_tokens, diagonal = {}, [], []
+        crossed, received = {}, {}
         part = depth // groups
 
         def join(parts):
@@ -463,9 +484,9 @@
         def items_of(cs, layer_bits=range(layers), others=range(groups)):
             items = []
             if 0 in layer_bits:
-                for r, name in enumerate(["own"] + [f"moved{r}" for r in range(1, team)]):
+                for r in range(team):
                     described = [(0, r, None if r < 2 else 0)]
-                    items.append((described, [(name, 0, c * chunk) for c in cs]))
+                    items.append((described, [(f"layer{r}", 0, c * chunk) for c in cs]))
                 for other in range(1, groups):
                     described = [(0, r, other) for r in range(2, team)]
                     items.append((described, [(f"far{other}", 0, c * chunk) for c in cs]))
@@ -492,11 +513,11 @@
             return items, rest, late
 
         for phase in range(1, chunks + hops + 1):
-            long = arrays.pop("tokens1", None) if phase < chunks + hops - 1 else None
+            waited = phase == chunks + hops - 1
+            long = {} if waited else {n: arrays.pop(n) for n in LONG if n in arrays}
             if phase < chunks + hops:
                 arrays = lax.optimization_barrier(arrays)
-            if long is not None:
-                arrays["tokens1"] = long
+            arrays.update(long)
             sends = []
             ways = {}
             for c in range(chunks):
@@ -504,75 +525,62 @@
                     low = bits & -bits
                     if c + bits.bit_count() == phase:
                         ways.setdefault((0, low), []).append((c, bits, held[c, bits ^ low]))
-                    elif c + bits.bit_count() + 1 == phase:
-                        for other in range(1, groups):
-                            way = ways.setdefault((other, 0), [])
-                            way.append((c, bits, held[c, bits]))
+            if waited:
+                sends.append((0, 0, 1, "diagonal", arrays["far_tokens"]))
+            for name, listed in received.items():
+                for other in range(1, groups):
+                    value = tie(arrays[name], *[arrays[n] for n in ("tail",) if n in arrays])
+                    sends.append((other, 0, 0, f"{name}_{other}", value))
+                    for c, bits in listed:
+                        _, first, n = held[c, bits]
+                        crossed[c, bits, other] = (f"{name}_{other}", first, n)
+            received = {}
             for (other, low), listed in ways.items():
-                name = f"phase{phase}from{other}{low}"
+                name = f"phase{phase}from{low}"
                 value = join([p for _, _, p in listed])
                 sends.append((other, low, 0, name, value))
+                received[name] = [(c, bits) for c, bits, _ in listed]
                 first = 0
                 for c, bits, (_, _, n) in listed:
-                    if other:
-                        crossed[c, bits, other] = (name, first, n)
-                    else:
-                        held[c, bits] = (name, first, n)
+                    held[c, bits] = (name, first, n)
                     first += n
-            if phase in steps:
-                sends.append((0, 0, 2, f"tokens{phase}", arrays[f"normed{phase}"]))
-            if phase == chunks + hops - 1:
-                sends.append((0, 0, 1, "diagonal1", arrays["tokens1"]))
             if phase == 1:
-                for i in steps:
-                    sends.append((0, 0, 1, f"near{i}", arrays[f"normed{i}"]))
+                sends.append((0, 0, 1, "near", tie(normed, arrays["layer0"])))
                 for other in range(1, groups):
                     sends.append((other, 0, 0, f"far{other}", arrays["far"]))
+            if phase == hops + 1:
+                noted = []
+                for bits in range(layers):
+                    name, start, _ = held[0, bits]
+                    noted.append((arrays[name], start + team * part))
+                arrays["first"], arrays["count"] = places(place, noted, team * blocks)
             new = {}
             for group_bits, layer_bits, member_bits, name, value in sends:
                 new[name] = swap(value, team, group_bits, layer_bits, member_bits)
             arrays.update(new)
             if phase == chunks + hops - 1:
-                team_tokens = [arrays[f"normed{i}"] for i in steps]
-                team_tokens += [arrays[f"near{i}"] for i in steps]
-                team_tokens += [arrays[f"tokens{i}"] for i in steps]
-                team_tokens += [arrays[f"diagonal{i}"] for i in steps]
-                items, rest, _ = without_last(range(chunks - 1))
+                names = ("normed", "near", "far_tokens", "diagonal")
+                team_tokens = [arrays[n] for n in names]
                 made = project(
-                    place,
-                    team,
-                    team_tokens,
-                    arrays,
-                    items,
-                    chunk,
-                    groups,
-                    depth,
-                    margin,
-                    rest,
-                    True,
+                    place, team, team_tokens, arrays, items_of([0]), chunk, groups, depth, margin
                 )
-                names = ["keys_values"] + [f"sum{c}" for c in range(1, chunks - 1)]
-                arrays.update(zip(names + ["tail", "head", "left"], made))
-        team_tokens = [arrays[f"normed{i}"] for i in steps]
-        team_tokens += [arrays[f"near{i}"] for i in steps]
-        team_tokens += [arrays[f"tokens{i}"] for i in steps]
-        team_tokens += [arrays[f"diagonal{i}"] for i in steps]
+                arrays.update(zip(("keys_values", "tail", "head"), made))
         keys_values, tail, head = (arrays[n] for n in ("keys_values", "tail", "head"))
-        items, rest, late = without_last([chunks - 1])
-        (begun,) = project(
-            place, team, team_tokens, arrays, items, chunk, groups, depth, rest=rest
-        )
-        lates = [without_last([chunks - 2])[2], late]
-        query = (arrays[f"sum{chunks - 2}"], begun, arrays["left"], lates)
-        assert chunks == 3
-        ids = []
-        for s in range(layers):
-            name, first, n = held[0, s]
-            noted = arrays[name][first + team * part : first + n]
-            ids.append(noted[: team * blocks, 0])
-        ids = jnp.stack(ids).astype(jnp.int32)
-        mine = ids[0]
-        ids = ids.reshape(-1)
+        items, rest, late = without_last(range(1, chunks))
+        *query, begun, left = project(
+            place,
+            team,
+            team_tokens,
+            arrays,
+            items,
+            chunk,
+            groups,
+            depth,
+            rest=rest,
+            wanted=True,
+        )
+        query = (query, begun, left, late)
+        first, count = arrays["first"], arrays["count"]
     else:
         (normed,) = normalize(tokens, norm_gain, [rows])
         team_tokens = [normed] + [swap(normed, team, 0, 0, r) for r in range(1, team)]
@@ -601,15 +609,16 @@
             ]
         )
 
+        count = jnp.sum((mine[:, None] == ids[None, :]).astype(jnp.int32), axis=1)
+        first = jnp.sum((ids[None, :] < mine[:, None]).astype(jnp.int32), axis=1)
+        first = first - layer * team * blocks + (MOST_BLK - 1)
+        first, count = first[:, None], count[:, None]
+
     before = from_layer(tail, team, -1)
     after = from_layer(head, team, 1)
 
-    count = jnp.sum((mine[:, None] == ids[None, :]).astype(jnp.int32), axis=1)
-    first = jnp.sum((ids[None, :] < mine[:, None]).astype(jnp.int32), axis=1)
-    first = first - layer * team * blocks + (MOST_BLK - 1)
-
     pieces = [None] * team
-    for start, end in ((1, team), (0, 1)):
+    for start, end in ((2, team), (0, 2)):
         made = attend(
             first,
             count,
@@ -624,7 +633,11 @@
         )
         for r, piece in enumerate(made, start):
             pieces[r] = swap(piece, team, 0, 0, r) if r else piece
-    return assemble(place, pieces)
+    out = jnp.zeros((rows, w_query.shape[1]), jnp.bfloat16)
+    for r in [0, *range(2, team), 1]:
+        piece = pieces[r]
+        out = lax.dynamic_update_slice(out, piece, (0, (member ^ r) * piece.shape[1]))
+    return out
 
 
 def solution(mesh):

time: 142 us -> 132 us (0.930)
  waiting for transfers between devices: 56.1 us -> 43.1 us
  starting transfers between devices: 30.9 us -> 37.9 us
  other arithmetic: 5.81 us -> 3.5 us
  Pallas kernels: 42.2 us -> 40.4 us
    ppermute x21 -> x24, waiting for transfers between devices: 54.5 us -> 42.2 us  [swap(): return lax.ppermute(value, AXES, pairs)]
    ppermute x21 -> x24, starting transfers between devices: 25.5 us -> 31.2 us  [swap(): return lax.ppermute(value, AXES, pairs)]
    dynamic_update_slice x0 -> x4, local copies, waits for them, and re-layouts: none -> 3.65 us  [on_device(): lax.dynamic_update_slice(out, piece, (0, (member ^ r) * piece.shape[1]))]
    unnamed x34 -> x12, local copies, waits for them, and re-layouts: 4.76 us -> 2.53 us
    slice x2 -> x0, local copies, waits for them, and re-layouts: 1.59 us -> none  [on_device(): ids.append(noted[:team * blocks, 0])]
    pallas_call x2, Pallas kernels: 13.6 us -> 12 us  [attend(): pl.pallas_call(functools.partial(attend_kernel, base, block, deep, firsts...]
    concatenate x5 -> x2, other arithmetic: 3.03 us -> 2.84 us  [join(): return views[0] if len(views) == 1 else jnp.concatenate(views, axis=0)]
  transfers between devices with their start and end apart: 23 -> 26, of which waited for: 11 -> 9; matrix products, arithmetic and copies ran while one was open for 5% -> 4% of each run, Pallas kernels for 18% -> 22%
where the time goes in v4:
time: 132 us; the launch traced here: 131 us
  waiting for transfers between devices  43.1 us (33%)
  Pallas kernels  40.4 us (31%)
  starting transfers between devices  37.9 us (29%)
  local copies, waits for them, and re-layouts  6.29 us (5%)
  other arithmetic  3.5 us (3%)
    ppermute x24, waiting for transfers between devices, swap(): return lax.ppermute(value, AXES, pairs)  42.2 us
    ppermute x24, starting transfers between devices, swap(): return lax.ppermute(value, AXES, pairs)  31.2 us
    pallas_call x2, Pallas kernels, project(): pl.pallas_call(functools.partial(project_kernel, items, (len(tokens), len...  16.7 us
    pallas_call x2, Pallas kernels, attend(): pl.pallas_call(functools.partial(attend_kernel, base, block, deep, firsts...  12 us
    ppermute x2, starting transfers between devices, from_layer(): return lax.ppermute(value, AXES, pairs)  6.78 us
    pallas_call x1, Pallas kernels, normalize(): pl.pallas_call(norm_kernel, out_shape=[jax.ShapeDtypeStruct((n, width), j...  4.11 us
    dynamic_update_slice x4, local copies, waits for them, and re-layouts, on_device(): lax.dynamic_update_slice(out, piece, (0, (member ^ r) * piece.shape[1]))  3.65 us
    pallas_call x1, Pallas kernels, pack(): pl.pallas_call(functools.partial(pack_kernel, team, depth // groups, note...  3.17 us
  transfers between devices with their start and end apart: 26, of which 9 were waited for; matrix products, arithmetic and copies ran while one was open for 4% of the time, Pallas kernels for 22%

profile of v4, /device:TPU:1, one launch (start us, length us, event | category | flops | bytes accessed | tf_op | source)
XLA Modules:
  0.0 131.4 jit_solution(12581783592192204309)
XLA Ops:
  0.0 0.7 pad_add_fusion.place
  0.7 3.2 %pack.1 = (bf16[272,768]{1,0:T(8,128)(2,1)}, bf16[272,768]{1,0:T(8,128)(2,1)}, bf16[144,768]{1,0:T(8,128)(2,1)}, bf16[144,768]{1,0:T(8,128)(2,1)}) custom-call(s32[3]{0:T(128)} %pad_add_fusion.place, s32[2]{0:T(128)} %numbers.1, bf16[256,512]{1,0:T(8,128)(2,1)} %refs_0_.1, bf16[256,512]{1,0:T(8,128)(2,1)} %refs_1_.1, bf16[256,2048]{1,0:T(8,128)(2,1)} %refs_2_.1), custom_call_target="tpu_custom_call" | custom-call | bytes 3145728 | tf_op jit(solution)/shard_map/pack/pallas_call | solution.py:111
  3.8 0.1 collective-permute-start
  4.0 2.7 %collective-permute-start.1 = (bf16[144,768]{1,0:T(8,128)(2,1)}, bf16[144,768]{1,0:T(8,128)(2,1)}, u32[]{:S(2)}, u32[]{:S(2)}) collective-permute-start(bf16[144,768]{1,0:T(8,128)(2,1)} %get-tuple-element.87), channel_id=1, source_target_pairs={{0,2},{1,3},{2,0},{3,1},{4,6},{5,7},{6,4},{7,5},{8,10},{9,11},{10,... | collective-permute-start | bytes 663560 | tf_op jit(solution)/shard_map/ppermute | solution.py:38
  6.7 0.0 collective-permute-start.2
  6.7 4.1 %normalize.1.refs_0_ = bf16[256,4096]{1,0:T(8,128)(2,1)} custom-call(bf16[256,4096]{1,0:T(8,128)(2,1)} %tokens_ref, f32[1,4096]{1,0:T(1,128)} %bitcast.4), custom_call_target="tpu_custom_call" | custom-call | flops 6291456 | bytes 4194304 | tf_op jit(solution)/shard_map/normalize/pallas_call | solution.py:67
  10.8 1.9 %collective-permute-done.1.refs_2_.refs_7_ = bf16[144,768]{1,0:T(8,128)(2,1)} collective-permute-done((bf16[144,768]{1,0:T(8,128)(2,1)}, bf16[144,768]{1,0:T(8,128)(2,1)}, u32[]{:S(2)}, u32[]{:S(2)}) %collective-permute-start.1) | collective-permute-done | bytes 221216 | tf_op jit(solution)/shard_map/ppermute | solution.py:38
  12.7 4.7 %collective-permute-done.2.refs_3_.refs_8_ = bf16[144,768]{1,0:T(8,128)(2,1)} collective-permute-done((bf16[144,768]{1,0:T(8,128)(2,1)}, bf16[144,768]{1,0:T(8,128)(2,1)}, u32[]{:S(2)}, u32[]{:S(2)}) %collective-permute-start.2) | collective-permute-done | bytes 221216 | tf_op jit(solution)/shard_map/ppermute | solution.py:38
  17.4 2.3 %shards.1 = (bf16[528,256]{1,0:T(8,128)(2,1)}, bf16[512,256]{1,0:T(8,128)(2,1)}, bf16[512,256]{1,0:T(8,128)(2,1)}, bf16[256,768]{1,0:T(8,128)(2,1)}) custom-call(s32[3]{0:T(128)} %pad_add_fusion.place, bf16[272,768]{1,0:T(8,128)(2,1)} %get-tuple-element.136.refs_0_.refs_5_, bf16[272,768]{1,0:T(8,128)(2,1)} %collective-permute-done.refs_1_.refs_6_, ...), custom_call_target="tpu_custom_call" | custom-call | bytes 2359296 | tf_op jit(solution)/shard_map/shards/pallas_call | solution.py:156
  19.7 0.4 collective-permute-start.4
  20.1 1.3 collective-permute-start.11
  21.4 1.2 collective-permute-start.3
  22.6 1.3 collective-permute-start.5
  23.9 2.3 %collective-permute-start.6 = (bf16[528,256]{1,0:T(8,128)(2,1)}, bf16[528,256]{1,0:T(8,128)(2,1)S(1)}, u32[]{:S(2)}, u32[]{:S(2)}) collective-permute-start(bf16[528,256]{1,0:T(8,128)(2,1)} %get-tuple-element.113.refs_0_), channel_id=1, source_target_pairs={{0,8},{1,9},{2,10},{3,11},{4,12},{5,13},{6,14},{7,15},{8,0},{9,1},... | collective-permute-start | bytes 811016 | tf_op jit(solution)/shard_map/ppermute | solution.py:38
  26.2 9.5 %collective-permute-done.5.refs_1_.refs_9_ = bf16[528,256]{1,0:T(8,128)(2,1)S(1)} collective-permute-done((bf16[528,256]{1,0:T(8,128)(2,1)}, bf16[528,256]{1,0:T(8,128)(2,1)S(1)}, u32[]{:S(2)}, u32[]{:S(2)}) %collective-permute-start.5) | collective-permute-done | bytes 270368 | tf_op jit(solution)/shard_map/ppermute | solution.py:38
  35.8 0.0 collective-permute-done.6.refs_2_.refs_11_
  35.8 0.8 copy-done.3
  36.6 0.0 collective-permute-done.4.refs_1_
  36.6 1.0 pad_maximum_fusion
  37.6 2.4 %collective-permute-start.9 = (bf16[1040,256]{1,0:T(8,128)(2,1)S(1)}, bf16[1040,256]{1,0:T(8,128)(2,1)}, u32[]{:S(2)}, u32[]{:S(2)}) collective-permute-start(bf16[1040,256]{1,0:T(8,128)(2,1)S(1)} %pad_maximum_fusion), channel_id=1, source_target_pairs={{0,4},{1,5},{2,6},{3,7},{4,0},{5,1},{6,2},{7,3},{8,12},{9,13},{10,... | collective-permute-start | bytes 1597448 | tf_op jit(solution)/shard_map/ppermute | solution.py:38
  40.0 0.3 collective-permute-start.7
  40.2 1.2 collective-permute-start.8
  41.4 0.3 collective-permute-start.10
  41.7 13.6 %collective-permute-done.10.refs_11_ = bf16[512,256]{1,0:T(8,128)(2,1)} collective-permute-done((bf16[512,256]{1,0:T(8,128)(2,1)}, bf16[512,256]{1,0:T(8,128)(2,1)}, u32[]{:S(2)}, u32[]{:S(2)}) %collective-permute-start.10) | collective-permute-done | bytes 262176 | tf_op jit(solution)/shard_map/ppermute | solution.py:38
  55.3 0.0 collective-permute-done.7.refs_10_
  55.3 0.0 collective-permute-done.8.refs_12_
  55.3 0.7 copy-done.4
  56.0 0.1 copy-done.5
  56.1 0.3 collective-permute-start.12
  56.4 1.9 %pad_maximum_fusion.1 = bf16[1024,256]{1,0:T(8,128)(2,1)} fusion(bf16[512,256]{1,0:T(8,128)(2,1)} %get-tuple-element.129, bf16[512,256]{1,0:T(8,128)(2,1)} %collective-permute-done.10.refs_11_), kind=kLoop, calls=%fused_computation.1 | loop fusion | flops 1048576 | bytes 1048576 | tf_op jit(solution)/shard_map/concatenate | solution.py:482
  58.2 1.1 collective-permute-start.14
  59.3 1.2 collective-permute-start.13
  60.6 2.0 %collective-permute-start.15 = (bf16[512,256]{1,0:T(8,128)(2,1)}, bf16[512,256]{1,0:T(8,128)(2,1)}, u32[]{:S(2)}, u32[]{:S(2)}) collective-permute-start(bf16[512,256]{1,0:T(8,128)(2,1)} %get-tuple-element.129), channel_id=1, source_target_pairs={{0,8},{1,9},{2,10},{3,11},{4,12},{5,13},{6,14},{7,15},{8,0},{9,1},... | collective-permute-start | bytes 786440 | tf_op jit(solution)/shard_map/ppermute | solution.py:38
  62.6 2.1 %places.1 = (s32[16,128]{1,0:T(8,128)}, s32[16,128]{1,0:T(8,128)}) custom-call(s32[3]{0:T(128)} %pad_add_fusion.place, bf16[528,256]{1,0:T(8,128)(2,1)} %get-tuple-element.113.refs_0_, bf16[528,256]{1,0:T(8,128)(2,1)} %copy-done.1, bf16[528,256]{1,0:T(8,128)(2,1)} %copy-done, bf16[1040,256]{1,0:T(8,128)(2,1)} %collective-permute-done.9.refs_3_.refs_13_.refs_9_), custom_call_target="tpu_custom_call" | custom-call | bytes 65536 | tf_op jit(solution)/shard_map/places/pallas_call | solution.py:334
  64.7 2.9 %collective-permute-done.11.refs_2_ = bf16[256,4096]{1,0:T(8,128)(2,1)} collective-permute-done((bf16[256,4096]{1,0:T(8,128)(2,1)}, bf16[256,4096]{1,0:T(8,128)(2,1)}, u32[]{:S(2)}, u32[]{:S(2)}) %collective-permute-start.11) | collective-permute-done | bytes 2097184 | tf_op jit(solution)/shard_map/ppermute | solution.py:38
  67.5 5.4 %collective-permute-done.13.refs_12_ = bf16[512,256]{1,0:T(8,128)(2,1)} collective-permute-done((bf16[512,256]{1,0:T(8,128)(2,1)}, bf16[512,256]{1,0:T(8,128)(2,1)}, u32[]{:S(2)}, u32[]{:S(2)}) %collective-permute-start.13) | collective-permute-done | bytes 262176 | tf_op jit(solution)/shard_map/ppermute | solution.py:38
  72.9 1.8 %collective-permute-done.14.refs_13_ = bf16[1024,256]{1,0:T(8,128)(2,1)} collective-permute-done((bf16[1024,256]{1,0:T(8,128)(2,1)}, bf16[1024,256]{1,0:T(8,128)(2,1)}, u32[]{:S(2)}, u32[]{:S(2)}) %collective-permute-start.14) | collective-permute-done | bytes 524320 | tf_op jit(solution)/shard_map/ppermute | solution.py:38
  74.7 0.0 collective-permute-done.12.refs_14_.refs_10_
  74.7 3.8 %collective-permute-start.16 = (bf16[256,4096]{1,0:T(8,128)(2,1)}, bf16[256,4096]{1,0:T(8,128)(2,1)}, u32[]{:S(2)}, u32[]{:S(2)}) collective-permute-start(bf16[256,4096]{1,0:T(8,128)(2,1)} %collective-permute-done.11.refs_2_), channel_id=1, source_target_pairs={{0,1},{1,0},{2,3},{3,2},{4,5},{5,4},{6,7},{7,6},{8,9},{9,8},{10,11... | collective-permute-start | bytes 6291464 | tf_op jit(solution)/shard_map/ppermute | solution.py:38
  78.5 1.2 collective-permute-start.19
  79.7 3.1 %collective-permute-start.21 = (bf16[512,256]{1,0:T(8,128)(2,1)}, bf16[512,256]{1,0:T(8,128)(2,1)}, u32[]{:S(2)}, u32[]{:S(2)}) collective-permute-start(bf16[512,256]{1,0:T(8,128)(2,1)} %collective-permute-done.15.refs_15_), channel_id=1, source_target_pairs={{0,4},{1,5},{2,6},{3,7},{4,0},{5,1},{6,2},{7,3},{8,12},{9,13},{10,... | collective-permute-start | bytes 786440 | tf_op jit(solution)/shard_map/ppermute | solution.py:38
  82.8 0.3 collective-permute-start.20
  83.1 7.2 %project.2 = (bf16[1024,256]{1,0:T(8,128)(2,1)}, bf16[768,256]{1,0:T(8,128)(2,1)}, bf16[768,256]{1,0:T(8,128)(2,1)}) custom-call(s32[3]{0:T(128)} %pad_add_fusion.place, bf16[256,4096]{1,0:T(8,128)(2,1)} %normalize.1.refs_0_, bf16[256,4096]{1,0:T(8,128)(2,1)} %collective-permute-done.4.refs_1_, bf16[256,4096]{1,0:T(8,128)(2,1)} %collective-permute-done.11.refs_2_, ...), custom_call_target="tpu_custom_call" | custom-call | flops 2147483648 | bytes 11010048 | tf_op jit(solution)/shard_map/project/pallas_call | solution.py:279
  90.3 5.3 %collective-permute-start.17 = (bf16[768,256]{1,0:T(8,128)(2,1)}, bf16[768,256]{1,0:T(8,128)(2,1)}, u32[]{:S(2)}, u32[]{:S(2)}) collective-permute-start(bf16[768,256]{1,0:T(8,128)(2,1)} %get-tuple-element.146), channel_id=1, source_target_pairs={{0,4},{1,5},{2,6},{3,7},{4,8},{5,9},{6,10},{7,11},{8,12},{9,13},{1... | collective-permute-start | bytes 1179656 | tf_op jit(solution)/shard_map/ppermute | solution.py:49
  95.6 1.2 collective-permute-start.22
  96.8 1.5 %collective-permute-start.18 = (bf16[768,256]{1,0:T(8,128)(2,1)}, bf16[768,256]{1,0:T(8,128)(2,1)}, u32[]{:S(2)}, u32[]{:S(2)}) collective-permute-start(bf16[768,256]{1,0:T(8,128)(2,1)} %get-tuple-element.148), channel_id=1, source_target_pairs={{4,0},{5,1},{6,2},{7,3},{8,4},{9,5},{10,6},{11,7},{12,8},{13,9},{1... | collective-permute-start | bytes 1179656 | tf_op jit(solution)/shard_map/ppermute | solution.py:49
  98.3 0.0 collective-permute-done.20.refs_16_
  98.3 9.5 %project.3 = (bf16[1024,256]{1,0:T(8,128)(2,1)}, f32[1024,256]{1,0:T(8,128)}, bf16[1024,512]{1,0:T(8,128)(2,1)}) custom-call(s32[3]{0:T(128)} %pad_add_fusion.place, bf16[256,4096]{1,0:T(8,128)(2,1)} %normalize.1.refs_0_, bf16[256,4096]{1,0:T(8,128)(2,1)} %collective-permute-done.4.refs_1_, bf16[256,4096]{1,0:T(8,128)(2,1)} %collective-permute-done.11.refs_2_, ...), custom_call_target="tpu_custom_call" | custom-call | flops 4294967296 | bytes 13631488 | tf_op jit(solution)/shard_map/project/pallas_call | solution.py:279
  107.8 0.0 collective-permute-done.22.refs_3_
  107.9 0.9 collective-permute-done.18.after
  108.7 6.0 %attend.3 = (bf16[256,512]{1,0:T(8,128)(2,1)}, bf16[256,512]{1,0:T(8,128)(2,1)}) custom-call(s32[16,128]{1,0:T(8,128)} %get-tuple-element.130.first_ref, s32[16,128]{1,0:T(8,128)} %get-tuple-element.131.count_ref, bf16[768,256]{1,0:T(8,128)(2,1)} %collective-permute-done.17.before, bf16[1024,256]{1,0:T(8,128)(2,1)} %get-tuple-element.147.own, ...), custom_call_target="tpu_custom_call" | custom-call | flops 939524096 | bytes 1835008 | tf_op jit(solution)/shard_map/attend/pallas_call | solution.py:427
  114.7 0.2 collective-permute-start.23
  115.0 3.3 %collective-permute-start.24 = (bf16[256,512]{1,0:T(8,128)(2,1)}, bf16[256,512]{1,0:T(8,128)(2,1)}, u32[]{:S(2)}, u32[]{:S(2)}) collective-permute-start(bf16[256,512]{1,0:T(8,128)(2,1)} %get-tuple-element.159), channel_id=1, source_target_pairs={{0,3},{1,2},{2,1},{3,0},{4,7},{5,6},{6,5},{7,4},{8,11},{9,10},{10,... | collective-permute-start | bytes 786440 | tf_op jit(solution)/shard_map/ppermute | solution.py:38
  118.2 6.0 %attend.2 = (bf16[256,512]{1,0:T(8,128)(2,1)}, bf16[256,512]{1,0:T(8,128)(2,1)}) custom-call(s32[16,128]{1,0:T(8,128)} %get-tuple-element.130.first_ref, s32[16,128]{1,0:T(8,128)} %get-tuple-element.131.count_ref, bf16[768,256]{1,0:T(8,128)(2,1)} %collective-permute-done.17.before, bf16[1024,256]{1,0:T(8,128)(2,1)} %get-tuple-element.147.own, ...), custom_call_target="tpu_custom_call" | custom-call | flops 939524096 | bytes 1835008 | tf_op jit(solution)/shard_map/attend/pallas_call | solution.py:427
  124.2 0.1 broadcast_in_dim.3
  124.3 1.0 constant_dynamic-update-slice_fusion.3
  125.3 0.0 collective-permute-done.23
  125.3 1.0 constant_dynamic-update-slice_fusion.2
  126.3 2.4 %collective-permute-done.24 = bf16[256,512]{1,0:T(8,128)(2,1)} collective-permute-done((bf16[256,512]{1,0:T(8,128)(2,1)}, bf16[256,512]{1,0:T(8,128)(2,1)}, u32[]{:S(2)}, u32[]{:S(2)}) %collective-permute-start.24) | collective-permute-done | bytes 262176 | tf_op jit(solution)/shard_map/ppermute | solution.py:38
  128.7 1.0 constant_dynamic-update-slice_fusion.1
  129.7 0.0 copy-start.2
  129.7 0.0 collective-permute-done.25
  129.7 1.0 copy-done.2
  130.7 0.7 constant_dynamic-update-slice_fusion
  (16 shorter events, 0.0 us)
Async XLA Ops:
  3.8 13.6 %collective-permute-start = (bf16[272,768]{1,0:T(8,128)(2,1)}, bf16[272,768]{1,0:T(8,128)(2,1)}, u32[]{:S(2)}, u32[]{:S(2)}) collective-permute-start(bf16[272,768]{1,0:T(8,128)(2,1)} %get-tuple-element.86), channel_id=1, source_target_pairs={{0,1},{1,0},{2,3},{3,2},{4,5},{5,4},{6,7},{7,6},{8,9},{9,8},{10,11... | collective-permute-start | bytes 1253384 | tf_op jit(solution)/shard_map/ppermute | solution.py:38
  4.0 8.7 %collective-permute-start.1 = (bf16[144,768]{1,0:T(8,128)(2,1)}, bf16[144,768]{1,0:T(8,128)(2,1)}, u32[]{:S(2)}, u32[]{:S(2)}) collective-permute-start(bf16[144,768]{1,0:T(8,128)(2,1)} %get-tuple-element.87), channel_id=1, source_target_pairs={{0,2},{1,3},{2,0},{3,1},{4,6},{5,7},{6,4},{7,5},{8,10},{9,11},{10,... | collective-permute-start | bytes 663560 | tf_op jit(solution)/shard_map/ppermute | solution.py:38
  6.7 10.8 %collective-permute-start.2 = (bf16[144,768]{1,0:T(8,128)(2,1)}, bf16[144,768]{1,0:T(8,128)(2,1)}, u32[]{:S(2)}, u32[]{:S(2)}) collective-permute-start(bf16[144,768]{1,0:T(8,128)(2,1)} %get-tuple-element.88), channel_id=1, source_target_pairs={{0,3},{1,2},{2,1},{3,0},{4,7},{5,6},{6,5},{7,4},{8,11},{9,10},{10,... | collective-permute-start | bytes 663560 | tf_op jit(solution)/shard_map/ppermute | solution.py:38
  19.7 16.8 %collective-permute-start.4 = (bf16[256,4096]{1,0:T(8,128)(2,1)}, bf16[256,4096]{1,0:T(8,128)(2,1)}, u32[]{:S(2)}, u32[]{:S(2)}) collective-permute-start(bf16[256,4096]{1,0:T(8,128)(2,1)} %normalize.1.refs_0_), channel_id=1, source_target_pairs={{0,1},{1,0},{2,3},{3,2},{4,5},{5,4},{6,7},{7,6},{8,9},{9,8},{10,11... | collective-permute-start | bytes 6291464 | tf_op jit(solution)/shard_map/ppermute | solution.py:38
  20.1 47.4 %collective-permute-start.11 = (bf16[256,4096]{1,0:T(8,128)(2,1)}, bf16[256,4096]{1,0:T(8,128)(2,1)}, u32[]{:S(2)}, u32[]{:S(2)}) collective-permute-start(bf16[256,4096]{1,0:T(8,128)(2,1)} %normalize.1.refs_0_), channel_id=1, source_target_pairs={{0,2},{1,3},{2,0},{3,1},{4,6},{5,7},{6,4},{7,5},{8,10},{9,11},{10,... | collective-permute-start | bytes 6291464 | tf_op jit(solution)/shard_map/ppermute | solution.py:38
  21.4 14.4 %collective-permute-start.3 = (bf16[256,768]{1,0:T(8,128)(2,1)}, bf16[256,768]{1,0:T(8,128)(2,1)S(1)}, u32[]{:S(2)}, u32[]{:S(2)}) collective-permute-start(bf16[256,768]{1,0:T(8,128)(2,1)} %get-tuple-element.93), channel_id=1, source_target_pairs={{0,16},{1,17},{2,18},{3,19},{4,20},{5,21},{6,22},{7,23},{8,24},{9,... | collective-permute-start | bytes 1179656 | tf_op jit(solution)/shard_map/ppermute | solution.py:38
  22.6 13.1 %collective-permute-start.5 = (bf16[528,256]{1,0:T(8,128)(2,1)}, bf16[528,256]{1,0:T(8,128)(2,1)S(1)}, u32[]{:S(2)}, u32[]{:S(2)}) collective-permute-start(bf16[528,256]{1,0:T(8,128)(2,1)} %get-tuple-element.113.refs_0_), channel_id=1, source_target_pairs={{0,4},{1,5},{2,6},{3,7},{4,0},{5,1},{6,2},{7,3},{8,12},{9,13},{10,... | collective-permute-start | bytes 811016 | tf_op jit(solution)/shard_map/ppermute | solution.py:38
  23.9 11.8 %collective-permute-start.6 = (bf16[528,256]{1,0:T(8,128)(2,1)}, bf16[528,256]{1,0:T(8,128)(2,1)S(1)}, u32[]{:S(2)}, u32[]{:S(2)}) collective-permute-start(bf16[528,256]{1,0:T(8,128)(2,1)} %get-tuple-element.113.refs_0_), channel_id=1, source_target_pairs={{0,8},{1,9},{2,10},{3,11},{4,12},{5,13},{6,14},{7,15},{8,0},{9,1},... | collective-permute-start | bytes 811016 | tf_op jit(solution)/shard_map/ppermute | solution.py:38
  35.8 19.6 %copy-start.1 = (bf16[528,256]{1,0:T(8,128)(2,1)}, bf16[528,256]{1,0:T(8,128)(2,1)S(1)}, u32[]{:S(2)}) copy-start(bf16[528,256]{1,0:T(8,128)(2,1)S(1)} %collective-permute-done.5.refs_1_.refs_9_) | copy-start | bytes 811012
  35.8 4.5 %copy-start = (bf16[528,256]{1,0:T(8,128)(2,1)}, bf16[528,256]{1,0:T(8,128)(2,1)S(1)}, u32[]{:S(2)}) copy-start(bf16[528,256]{1,0:T(8,128)(2,1)S(1)} %collective-permute-done.6.refs_2_.refs_11_) | copy-start | bytes 811012
  35.8 0.8 copy-start.3
  37.6 17.8 %collective-permute-start.9 = (bf16[1040,256]{1,0:T(8,128)(2,1)S(1)}, bf16[1040,256]{1,0:T(8,128)(2,1)}, u32[]{:S(2)}, u32[]{:S(2)}) collective-permute-start(bf16[1040,256]{1,0:T(8,128)(2,1)S(1)} %pad_maximum_fusion), channel_id=1, source_target_pairs={{0,4},{1,5},{2,6},{3,7},{4,0},{5,1},{6,2},{7,3},{8,12},{9,13},{10,... | collective-permute-start | bytes 1597448 | tf_op jit(solution)/shard_map/ppermute | solution.py:38
  40.0 15.3 %collective-permute-start.7 = (bf16[528,256]{1,0:T(8,128)(2,1)S(1)}, bf16[528,256]{1,0:T(8,128)(2,1)S(1)}, u32[]{:S(2)}, u32[]{:S(2)}) collective-permute-start(bf16[528,256]{1,0:T(8,128)(2,1)S(1)} %collective-permute-done.5.refs_1_.refs_9_), channel_id=1, source_target_pairs={{0,16},{1,17},{2,18},{3,19},{4,20},{5,21},{6,22},{7,23},{8,24},{9,... | collective-permute-start | bytes 811016 | tf_op jit(solution)/shard_map/ppermute | solution.py:38
  40.2 15.1 %collective-permute-start.8 = (bf16[528,256]{1,0:T(8,128)(2,1)S(1)}, bf16[528,256]{1,0:T(8,128)(2,1)S(1)}, u32[]{:S(2)}, u32[]{:S(2)}) collective-permute-start(bf16[528,256]{1,0:T(8,128)(2,1)S(1)} %collective-permute-done.6.refs_2_.refs_11_), channel_id=1, source_target_pairs={{0,16},{1,17},{2,18},{3,19},{4,20},{5,21},{6,22},{7,23},{8,24},{9,... | collective-permute-start | bytes 811016 | tf_op jit(solution)/shard_map/ppermute | solution.py:38
  41.4 13.9 %collective-permute-start.10 = (bf16[512,256]{1,0:T(8,128)(2,1)}, bf16[512,256]{1,0:T(8,128)(2,1)}, u32[]{:S(2)}, u32[]{:S(2)}) collective-permute-start(bf16[512,256]{1,0:T(8,128)(2,1)} %get-tuple-element.110), channel_id=1, source_target_pairs={{0,8},{1,9},{2,10},{3,11},{4,12},{5,13},{6,14},{7,15},{8,0},{9,1},... | collective-permute-start | bytes 786440 | tf_op jit(solution)/shard_map/ppermute | solution.py:38
  55.3 0.7 copy-start.4
  55.3 0.8 copy-start.5
  56.1 18.6 %collective-permute-start.12 = (bf16[1040,256]{1,0:T(8,128)(2,1)}, bf16[1040,256]{1,0:T(8,128)(2,1)}, u32[]{:S(2)}, u32[]{:S(2)}) collective-permute-start(bf16[1040,256]{1,0:T(8,128)(2,1)} %collective-permute-done.9.refs_3_.refs_13_.refs_9_), channel_id=1, source_target_pairs={{0,16},{1,17},{2,18},{3,19},{4,20},{5,21},{6,22},{7,23},{8,24},{9,... | collective-permute-start | bytes 1597448 | tf_op jit(solution)/shard_map/ppermute | solution.py:38
  58.2 16.5 %collective-permute-start.14 = (bf16[1024,256]{1,0:T(8,128)(2,1)}, bf16[1024,256]{1,0:T(8,128)(2,1)}, u32[]{:S(2)}, u32[]{:S(2)}) collective-permute-start(bf16[1024,256]{1,0:T(8,128)(2,1)} %pad_maximum_fusion.1), channel_id=1, source_target_pairs={{0,4},{1,5},{2,6},{3,7},{4,0},{5,1},{6,2},{7,3},{8,12},{9,13},{10,... | collective-permute-start | bytes 1572872 | tf_op jit(solution)/shard_map/ppermute | solution.py:38
  59.3 13.6 %collective-permute-start.13 = (bf16[512,256]{1,0:T(8,128)(2,1)}, bf16[512,256]{1,0:T(8,128)(2,1)}, u32[]{:S(2)}, u32[]{:S(2)}) collective-permute-start(bf16[512,256]{1,0:T(8,128)(2,1)} %collective-permute-done.10.refs_11_), channel_id=1, source_target_pairs={{0,16},{1,17},{2,18},{3,19},{4,20},{5,21},{6,22},{7,23},{8,24},{9,... | collective-permute-start | bytes 786440 | tf_op jit(solution)/shard_map/ppermute | solution.py:38
  60.6 12.4 %collective-permute-start.15 = (bf16[512,256]{1,0:T(8,128)(2,1)}, bf16[512,256]{1,0:T(8,128)(2,1)}, u32[]{:S(2)}, u32[]{:S(2)}) collective-permute-start(bf16[512,256]{1,0:T(8,128)(2,1)} %get-tuple-element.129), channel_id=1, source_target_pairs={{0,8},{1,9},{2,10},{3,11},{4,12},{5,13},{6,14},{7,15},{8,0},{9,1},... | collective-permute-start | bytes 786440 | tf_op jit(solution)/shard_map/ppermute | solution.py:38
  74.7 8.4 %collective-permute-start.16 = (bf16[256,4096]{1,0:T(8,128)(2,1)}, bf16[256,4096]{1,0:T(8,128)(2,1)}, u32[]{:S(2)}, u32[]{:S(2)}) collective-permute-start(bf16[256,4096]{1,0:T(8,128)(2,1)} %collective-permute-done.11.refs_2_), channel_id=1, source_target_pairs={{0,1},{1,0},{2,3},{3,2},{4,5},{5,4},{6,7},{7,6},{8,9},{9,8},{10,11... | collective-permute-start | bytes 6291464 | tf_op jit(solution)/shard_map/ppermute | solution.py:38
  78.5 19.8 %collective-permute-start.19 = (bf16[1024,256]{1,0:T(8,128)(2,1)}, bf16[1024,256]{1,0:T(8,128)(2,1)}, u32[]{:S(2)}, u32[]{:S(2)}) collective-permute-start(bf16[1024,256]{1,0:T(8,128)(2,1)} %collective-permute-done.14.refs_13_), channel_id=1, source_target_pairs={{0,16},{1,17},{2,18},{3,19},{4,20},{5,21},{6,22},{7,23},{8,24},{9,... | collective-permute-start | bytes 1572872 | tf_op jit(solution)/shard_map/ppermute | solution.py:38
  79.7 15.9 %collective-permute-start.21 = (bf16[512,256]{1,0:T(8,128)(2,1)}, bf16[512,256]{1,0:T(8,128)(2,1)}, u32[]{:S(2)}, u32[]{:S(2)}) collective-permute-start(bf16[512,256]{1,0:T(8,128)(2,1)} %collective-permute-done.15.refs_15_), channel_id=1, source_target_pairs={{0,4},{1,5},{2,6},{3,7},{4,0},{5,1},{6,2},{7,3},{8,12},{9,13},{10,... | collective-permute-start | bytes 786440 | tf_op jit(solution)/shard_map/ppermute | solution.py:38
  82.8 15.5 %collective-permute-start.20 = (bf16[512,256]{1,0:T(8,128)(2,1)}, bf16[512,256]{1,0:T(8,128)(2,1)}, u32[]{:S(2)}, u32[]{:S(2)}) collective-permute-start(bf16[512,256]{1,0:T(8,128)(2,1)} %collective-permute-done.15.refs_15_), channel_id=1, source_target_pairs={{0,16},{1,17},{2,18},{3,19},{4,20},{5,21},{6,22},{7,23},{8,24},{9,... | collective-permute-start | bytes 786440 | tf_op jit(solution)/shard_map/ppermute | solution.py:38
  90.3 17.6 %collective-permute-start.17 = (bf16[768,256]{1,0:T(8,128)(2,1)}, bf16[768,256]{1,0:T(8,128)(2,1)}, u32[]{:S(2)}, u32[]{:S(2)}) collective-permute-start(bf16[768,256]{1,0:T(8,128)(2,1)} %get-tuple-element.146), channel_id=1, source_target_pairs={{0,4},{1,5},{2,6},{3,7},{4,8},{5,9},{6,10},{7,11},{8,12},{9,13},{1... | collective-permute-start | bytes 1179656 | tf_op jit(solution)/shard_map/ppermute | solution.py:49
  95.6 12.2 %collective-permute-start.22 = (bf16[512,256]{1,0:T(8,128)(2,1)}, bf16[512,256]{1,0:T(8,128)(2,1)}, u32[]{:S(2)}, u32[]{:S(2)}) collective-permute-start(bf16[512,256]{1,0:T(8,128)(2,1)} %collective-permute-done.21.refs_17_), channel_id=1, source_target_pairs={{0,16},{1,17},{2,18},{3,19},{4,20},{5,21},{6,22},{7,23},{8,24},{9,... | collective-permute-start | bytes 786440 | tf_op jit(solution)/shard_map/ppermute | solution.py:38
  96.8 11.9 %collective-permute-start.18 = (bf16[768,256]{1,0:T(8,128)(2,1)}, bf16[768,256]{1,0:T(8,128)(2,1)}, u32[]{:S(2)}, u32[]{:S(2)}) collective-permute-start(bf16[768,256]{1,0:T(8,128)(2,1)} %get-tuple-element.148), channel_id=1, source_target_pairs={{4,0},{5,1},{6,2},{7,3},{8,4},{9,5},{10,6},{11,7},{12,8},{13,9},{1... | collective-permute-start | bytes 1179656 | tf_op jit(solution)/shard_map/ppermute | solution.py:49
  114.7 10.6 %collective-permute-start.23 = (bf16[256,512]{1,0:T(8,128)(2,1)}, bf16[256,512]{1,0:T(8,128)(2,1)}, u32[]{:S(2)}, u32[]{:S(2)}) collective-permute-start(bf16[256,512]{1,0:T(8,128)(2,1)} %get-tuple-element.158), channel_id=1, source_target_pairs={{0,2},{1,3},{2,0},{3,1},{4,6},{5,7},{6,4},{7,5},{8,10},{9,11},{10,... | collective-permute-start | bytes 786440 | tf_op jit(solution)/shard_map/ppermute | solution.py:38
  115.0 13.8 %collective-permute-start.24 = (bf16[256,512]{1,0:T(8,128)(2,1)}, bf16[256,512]{1,0:T(8,128)(2,1)}, u32[]{:S(2)}, u32[]{:S(2)}) collective-permute-start(bf16[256,512]{1,0:T(8,128)(2,1)} %get-tuple-element.159), channel_id=1, source_target_pairs={{0,3},{1,2},{2,1},{3,0},{4,7},{5,6},{6,5},{7,4},{8,11},{9,10},{10,... | collective-permute-start | bytes 786440 | tf_op jit(solution)/shard_map/ppermute | solution.py:38
  124.2 5.5 %collective-permute-start.25 = (bf16[256,512]{1,0:T(8,128)(2,1)}, bf16[256,512]{1,0:T(8,128)(2,1)S(1)}, u32[]{:S(2)}, u32[]{:S(2)}) collective-permute-start(bf16[256,512]{1,0:T(8,128)(2,1)} %get-tuple-element.160), channel_id=1, source_target_pairs={{0,1},{1,0},{2,3},{3,2},{4,5},{5,4},{6,7},{7,6},{8,9},{9,8},{10,11... | collective-permute-start | bytes 786440 | tf_op jit(solution)/shard_map/ppermute | solution.py:38
  129.7 1.0 copy-start.2

commit v5 on v4

--- a/solution.py
+++ b/solution.py
@@ -38,12 +38,12 @@
     return lax.ppermute(value, AXES, pairs)
 
 
-def from_layer(value, team, by):
+def swap_outward(value, team):
     groups, peers = lax.axis_size("groups"), lax.axis_size("seq")
     pairs = []
     for g in range(groups):
         for s in range(peers):
-            to = s - by * team
+            to = s + team if s // team % 2 else s - team
             if 0 <= to < peers:
                 pairs.append((g * peers + s, g * peers + to))
     return lax.ppermute(value, AXES, pairs)
@@ -75,7 +75,8 @@
     )(tokens, norm_gain.reshape(1, width))
 
 
-def pack_kernel(team, part, notes, count, place, numbers, *refs):
+def pack_kernel(team, part, notes, count, numbers, *refs):
+    group, member = lax.axis_index("groups"), lax.rem(lax.axis_index("seq"), team)
     weights, outs = refs[:count], refs[count : count + team]
     loaded, sems = refs[count + team : -1], refs[-1]
     copies = [
@@ -98,13 +99,13 @@
         width = weight.shape[1] // team
         for r, out in enumerate(outs):
             length = out.shape[0] - notes
-            first = 0 if r < 2 else pl.multiple_of(place[0] * part, part)
-            columns = pl.ds(pl.multiple_of((place[2] ^ r) * width, width), width)
+            first = 0 if r < 2 else pl.multiple_of(group * part, part)
+            columns = pl.ds(pl.multiple_of((member ^ r) * width, width), width)
             out[:length, column : column + width] = weight[pl.ds(first, length), columns]
         column += width
 
 
-def pack(place, numbers, weights, team, groups, notes=0):
+def pack(numbers, weights, team, groups, notes=0):
     depth = weights[0].shape[0]
     width = sum(weight.shape[1] for weight in weights) // team
     lengths = [depth if r < 2 else depth // groups for r in range(team)]
@@ -114,14 +115,14 @@
             jax.ShapeDtypeStruct((length + notes, width), jnp.bfloat16)
             for length in lengths
         ],
-        in_specs=[IN_SMEM] * 2 + [IN_HBM] * len(weights),
+        in_specs=[IN_SMEM] + [IN_HBM] * len(weights),
         out_specs=[IN_VMEM] * team,
         scratch_shapes=[pltpu.VMEM(w.shape, w.dtype) for w in weights]
         + [pltpu.SemaphoreType.DMA((len(weights),))],
         compiler_params=PARAMS,
         cost_estimate=cost(0, 4 * team * depth * width),
         name="pack",
-    )(place, numbers, *weights)
+    )(numbers, *weights)
 
 
 def shards_kernel(team, part, blocks, place, *refs):
@@ -165,11 +166,22 @@
 
 
 def project_kernel(items, counts, chunk, margin, rest, team, groups, depth, place, *refs):
-    held, arrays, wanted = counts
+    held, arrays, wanted, carried = counts
     sources, refs = refs[:held], refs[held:]
     stored, refs = refs[:arrays], refs[arrays:]
-    outs, (tokens, weights, total, token_sems, sems) = refs[:-5], refs[-5:]
+    begun, refs = refs[: 2 * carried], refs[2 * carried :]
+    outs, (tokens, weights, total, lefts, token_sems, sems) = refs[:-6], refs[-6:]
     part = depth // groups
+    span = 2 * sources[0].shape[0]
+    if carried:
+        near = pl.ds(0, span)
+        pairs = [(begun[0], total.at[near]), (begun[1], lefts)]
+        carries = [
+            pltpu.make_async_copy(*pair, sems.at[sems.shape[0] - 2 + i])
+            for i, pair in enumerate(pairs)
+        ]
+        for copy in carries:
+            copy.start()
     group, layer, member = place[0], place[1], place[2]
     layer_wide = team * depth
     layers = sorted({described[0][0] for described, _ in items})
@@ -214,21 +226,36 @@
             lefts.append(tokens[own, pl.ds(pl.multiple_of(first, LANES), wide)])
         return lefts[0] if len(lefts) == 1 else jnp.concatenate(lefts, axis=1)
 
-    span = tokens.shape[0] // 2
+    shift = span if carried else 0
+    if carried:
+        for copy in carries:
+            copy.wait()
     for step, (loads, matched) in enumerate(plan):
         for copy in loads:
             copy.wait()
-        for half in range(2):
+        for half in range(tokens.shape[0] // span):
             own = pl.ds(half * span, span)
+            to = pl.ds(half * span + shift, span)
             for i, (described, offset, deep, wide) in enumerate(matched):
                 right = weights[pl.ds(offset, deep), :wide]
                 term = jnp.dot(
                     columns_of(own, described), right, preferred_element_type=jnp.float32
                 )
                 if i == 0 and step == 0:
-                    total[own, :wide] = term
+                    total[to, :wide] = term
                 else:
-                    total[own, :wide] += term
+                    total[to, :wide] += term
+        if carried:
+            column = 0
+            for described in rest:
+                for other, offset, deep, wide in matched:
+                    if other == described:
+                        total[near, :wide] += jnp.dot(
+                            lefts[:, column : column + deep],
+                            weights[pl.ds(offset, deep), :wide],
+                            preferred_element_type=jnp.float32,
+                        )
+                column += sum(depth if bits[2] is None else part for bits in described)
     if wanted:
         column = 0
         for described in rest:
@@ -239,7 +266,7 @@
     chunks = total.shape[1] // chunk
     for c in range(chunks):
         columns = slice(c * chunk, (c + 1) * chunk)
-        if rest and c + 1 == chunks:
+        if rest and not carried and c + 1 == chunks:
             outs[c][...] = total[:, columns]
             continue
         for r in range(team):
@@ -249,14 +276,27 @@
             made = total[r * rows : (r + 1) * rows, columns]
             outs[c][pl.ds(first, rows), :] = made.astype(jnp.bfloat16)
     if margin is not None:
-        outs[chunks][...] = outs[0][total.shape[0] - margin :, :]
-        outs[chunks + 1][...] = outs[0][:margin, :]
+        late, odd = total.shape[0] - margin, lax.rem(layer, 2)
+        for out, first in ((outs[chunks], (1 - odd) * late), (outs[chunks + 1], odd * late)):
+            out[...] = outs[0][pl.ds(pl.multiple_of(first, LANES), margin), :]
 
 
 def project(
-    place, team, tokens, arrays, items, chunk, groups, depth, margin=None, rest=(), wanted=False
+    place,
+    team,
+    tokens,
+    arrays,
+    items,
+    chunk,
+    groups,
+    depth,
+    margin=None,
+    rest=(),
+    wanted=False,
+    carried=(),
 ):
-    count, width = sum(value.shape[0] for value in tokens), tokens[0].shape[1]
+    taken, width = sum(value.shape[0] for value in tokens), tokens[0].shape[1]
+    count = taken + (carried[0].shape[0] if carried else 0)
     chunks = max(len(parts) for _, parts in items)
     names = sorted({name for _, parts in items for name, _, _ in parts})
     items = [
@@ -270,7 +310,8 @@
 
     deep = deep_of([described for described, _ in items])
     copies = sum(len(parts) for _, parts in items)
-    kinds = [jnp.bfloat16] * (chunks - bool(rest)) + [jnp.float32] * bool(rest)
+    lacking = bool(rest) and not carried
+    kinds = [jnp.bfloat16] * (chunks - lacking) + [jnp.float32] * lacking
     shapes = [jax.ShapeDtypeStruct((count, chunk), kind) for kind in kinds]
     if margin is not None:
         shapes += [jax.ShapeDtypeStruct((margin, chunk), jnp.bfloat16)] * 2
@@ -280,7 +321,7 @@
         functools.partial(
             project_kernel,
             items,
-            (len(tokens), len(names), wanted),
+            (len(tokens), len(names), wanted, bool(carried)),
             chunk,
             margin,
             rest,
@@ -289,22 +330,23 @@
             depth,
         ),
         out_shape=shapes,
-        in_specs=[IN_SMEM] + [IN_HBM] * (len(tokens) + len(names)),
+        in_specs=[IN_SMEM] + [IN_HBM] * (len(tokens) + len(names) + len(carried)),
         out_specs=[IN_VMEM] * len(shapes),
         scratch_shapes=[
-            pltpu.VMEM((count, width), jnp.bfloat16),
+            pltpu.VMEM((taken, width), jnp.bfloat16),
             pltpu.VMEM((deep, chunks * chunk), jnp.bfloat16),
             pltpu.VMEM((count, chunks * chunk), jnp.float32),
+            pltpu.VMEM(carried[1].shape if carried else (NOTES, LANES), jnp.bfloat16),
             pltpu.SemaphoreType.DMA((len(tokens) * width // (team * depth),)),
-            pltpu.SemaphoreType.DMA((copies,)),
+            pltpu.SemaphoreType.DMA((copies + len(carried),)),
         ],
         compiler_params=PARAMS,
         cost_estimate=cost(
-            2 * count * deep * chunks * chunk,
-            2 * chunks * chunk * (count + deep) + 2 * count * width,
+            2 * taken * deep * chunks * chunk,
+            2 * chunks * chunk * (count + deep) + 2 * taken * width,
         ),
         name="project",
-    )(place, *tokens, *[arrays[name] for name in names])
+    )(place, *tokens, *[arrays[name] for name in names], *carried)
 
 
 def places_kernel(blocks, firsts, place, *refs):
@@ -348,31 +390,39 @@
 
 
 def attend_kernel(
-    base, block, deep, firsts, first_ref, count_ref, before, own, after, *refs
+    base, block, deep, firsts, first_ref, count_ref, place, inner, own, outer, *refs
 ):
     outs, (window, query) = refs[:-2][-(len(refs) - 2 - firsts[0]) :], refs[-2:]
     ins = refs[: firsts[0]]
     per_out = outs[0].shape[0] // block
     total_blocks = per_out * len(outs)
-    mine = pl.ds(base * block, total_blocks * block)
     column = 0
     for ref in ins[: firsts[0] - (2 + len(firsts[1]) if deep else 0)]:
-        query[:, column : column + ref.shape[1]] = ref[mine, :]
+        query[:, column : column + ref.shape[1]] = ref[...]
         column += ref.shape[1]
     if deep:
         begun, left, *weights = ins[firsts[0] - 2 - len(firsts[1]) :]
-        total = begun[mine, :]
+        total = begun[...]
         for i, (weight, start) in enumerate(zip(weights, firsts[1])):
             total += jnp.dot(
-                left[mine, i * deep : (i + 1) * deep],
+                left[:, i * deep : (i + 1) * deep],
                 weight[start : start + deep, :],
                 preferred_element_type=jnp.float32,
             )
         query[:, column:] = total.astype(jnp.bfloat16)
-    offset = 0
-    for ref in (before, own, after):
-        window[offset : offset + ref.shape[0], :] = ref[...]
-        offset += ref.shape[0]
+    margin, odd = inner.shape[0], lax.rem(place[1], 2)
+    window[margin : margin + own.shape[0], :] = own[...]
+
+    @pl.when(odd == 0)
+    def _():
+        window[:margin, :] = outer[...]
+        window[margin + own.shape[0] :, :] = inner[...]
+
+    @pl.when(odd == 1)
+    def _():
+        window[:margin, :] = inner[...]
+        window[margin + own.shape[0] :, :] = outer[...]
+
     heads = query.shape[1] // HD
     span = MOST_BLK * block
     row = lax.broadcasted_iota(jnp.int32, (span, 1), 0)
@@ -414,7 +464,7 @@
         scores = upcoming
 
 
-def attend(first, count, query, before, own, after, block, base, rows, parts):
+def attend(first, count, place, query, inner, own, outer, block, base, rows, parts):
     if isinstance(query, tuple):
         done, begun, left, late = query
         ins = [*done, begun, left] + [array for array, _ in late]
@@ -423,11 +473,20 @@
         columns = sum(value.shape[1] for value in done) + begun.shape[1]
     else:
         ins, firsts, deep, columns = [query], (1, []), 0, query.shape[1]
-    span = before.shape[0] + own.shape[0] + after.shape[0]
+    span = 2 * inner.shape[0] + own.shape[0]
+    size = parts * rows
+    by_rows = [value.shape[0] == own.shape[0] and i < len(ins) - len(firsts[1])
+               for i, value in enumerate(ins)]
+    specs = [
+        pl.BlockSpec((size, value.shape[1]), lambda i: (base * block // size, 0))
+        if cut else IN_VMEM
+        for value, cut in zip(ins, by_rows)
+    ]
     return pl.pallas_call(
         functools.partial(attend_kernel, base, block, deep, firsts),
         out_shape=[jax.ShapeDtypeStruct((rows, columns), jnp.bfloat16)] * parts,
-        in_specs=[IN_SMEM] * 2 + [IN_VMEM] * (3 + len(ins)),
+        grid=(1,),
+        in_specs=[IN_SMEM] * 3 + [IN_VMEM] * 3 + specs,
         out_specs=[IN_VMEM] * parts,
         scratch_shapes=[
             pltpu.VMEM((span, own.shape[1]), jnp.bfloat16),
@@ -440,7 +499,7 @@
             parts * rows * MOST_BLK * block * (columns // HD),
         ),
         name="attend",
-    )(first, count, before, own, after, *ins)
+    )(first, count, place, inner, own, outer, *ins)
 
 
 def on_device(tokens, norm_gain, w_query, w_key, w_value, passage_blocks):
@@ -460,7 +519,7 @@
     if depth // groups % LANES == 0 and team * blocks <= NOTES:
         chunk = 2 * HD
         weights = [w_key, w_value, w_query]
-        packed = pack(place, passage_blocks, weights, team, groups, NOTES)
+        packed = pack(passage_blocks, weights, team, groups, NOTES)
         moved = [swap(packed[r], team, 0, 0, r) for r in range(1, team)]
         (normed,) = normalize(tie(tokens, packed[0]), norm_gain, [rows])
         *shards, far = make_shards(
@@ -494,16 +553,19 @@
                 for bits in layer_bits:
                     if bits:
                         described = [(bits, r, other) for r in range(team)]
-                        where = [crossed[c, bits, other] if other else held[c, bits] for c in cs]
+                        where = [
+                            crossed.get((c, bits, other), held[c, bits]) if other else held[c, bits]
+                            for c in cs
+                        ]
                         items.append((described, [(n, first, 0) for n, first, _ in where]))
             return items
 
         hardest = [bits for bits in range(layers) if bits.bit_count() == hops]
 
-        def without_last(cs):
+        def without_last(cs, slow):
             items, rest, late = [], [], []
             for described, parts in items_of(cs):
-                if described[0][2] and described[0][0] in hardest:
+                if described[0][2] and described[0][0] in slow:
                     name, first, _ = parts[-1]
                     late.append((name, first))
                     rest.append(described)
@@ -516,7 +578,9 @@
             waited = phase == chunks + hops - 1
             long = {} if waited else {n: arrays.pop(n) for n in LONG if n in arrays}
             if phase < chunks + hops:
+                final = {n: arrays.pop(n) for n in [f"phase{phase - 1}from{layers // 2}"] if n in arrays}
                 arrays = lax.optimization_barrier(arrays)
+                arrays = lax.optimization_barrier({**arrays, **final})
             arrays.update(long)
             sends = []
             ways = {}
@@ -529,7 +593,7 @@
                 sends.append((0, 0, 1, "diagonal", arrays["far_tokens"]))
             for name, listed in received.items():
                 for other in range(1, groups):
-                    value = tie(arrays[name], *[arrays[n] for n in ("tail",) if n in arrays])
+                    value = tie(arrays[name], *[arrays[n] for n in ("inward",) if n in arrays])
                     sends.append((other, 0, 0, f"{name}_{other}", value))
                     for c, bits in listed:
                         _, first, n = held[c, bits]
@@ -549,6 +613,20 @@
                 for other in range(1, groups):
                     sends.append((other, 0, 0, f"far{other}", arrays["far"]))
             if phase == hops + 1:
+                items, rest, _ = without_last([0], hardest)
+                near_tokens = [normed, arrays["near"]]
+                arrays["kv_sum"], arrays["kv_left"] = project(
+                    place,
+                    team,
+                    near_tokens,
+                    arrays,
+                    items,
+                    chunk,
+                    groups,
+                    depth,
+                    rest=rest,
+                    wanted=True,
+                )
                 noted = []
                 for bits in range(layers):
                     name, start, _ = held[0, bits]
@@ -562,11 +640,22 @@
                 names = ("normed", "near", "far_tokens", "diagonal")
                 team_tokens = [arrays[n] for n in names]
                 made = project(
-                    place, team, team_tokens, arrays, items_of([0]), chunk, groups, depth, margin
+                    place,
+                    team,
+                    team_tokens[2:],
+                    arrays,
+                    items_of([0]),
+                    chunk,
+                    groups,
+                    depth,
+                    margin,
+                    rest=without_last([0], hardest)[1],
+                    carried=(arrays["kv_sum"], arrays["kv_left"]),
                 )
-                arrays.update(zip(("keys_values", "tail", "head"), made))
-        keys_values, tail, head = (arrays[n] for n in ("keys_values", "tail", "head"))
-        items, rest, late = without_last(range(1, chunks))
+                arrays.update(zip(("keys_values", "inward", "outward"), made))
+        names = ("keys_values", "inward", "outward")
+        keys_values, inward, outward = (arrays[n] for n in names)
+        items, rest, late = without_last(range(1, chunks), [layers // 2] + hardest)
         *query, begun, left = project(
             place,
             team,
@@ -599,7 +688,8 @@
         keys_values = jnp.concatenate(
             [dense(w_key, in_order), dense(w_value, in_order)], axis=1
         )
-        tail, head = keys_values[-margin:], keys_values[:margin]
+        tail, head, odd = keys_values[-margin:], keys_values[:margin], layer % 2 == 1
+        inward, outward = jnp.where(odd, head, tail), jnp.where(odd, tail, head)
         query = dense(w_query, stacked.reshape(team * rows, tokens.shape[1]))
         ids = lax.all_gather(passage_blocks, "seq", axis=0, tiled=True)
         mine = jnp.concatenate(
@@ -614,18 +704,19 @@
         first = first - layer * team * blocks + (MOST_BLK - 1)
         first, count = first[:, None], count[:, None]
 
-    before = from_layer(tail, team, -1)
-    after = from_layer(head, team, 1)
+    inner = swap(inward, team, 0, 1, 0)
+    outer = swap_outward(outward, team)
 
     pieces = [None] * team
     for start, end in ((2, team), (0, 2)):
         made = attend(
             first,
             count,
+            place,
             query,
-            before,
+            inner,
             keys_values,
-            after,
+            outer,
             block,
             start * blocks,
             rows,

time: 132 us -> 127 us (0.962)
  waiting for transfers between devices: 43.1 us -> 35.6 us
  Pallas kernels: 40.4 us -> 47 us
  starting transfers between devices: 37.9 us -> 34.4 us
    ppermute x24 -> x25, waiting for transfers between devices: 42.2 us -> 35.6 us  [swap(): return lax.ppermute(value, AXES, pairs)]
    ppermute x2 -> x1, starting transfers between devices: 6.78 us -> 1.4 us  [swap_outward(): return lax.ppermute(value, AXES, pairs)]
    pallas_call x2 -> x3, Pallas kernels: 16.7 us -> 21.8 us  [project(): pl.pallas_call(functools.partial(project_kernel, items, (len(tokens), len...]
    ppermute x24 -> x25, starting transfers between devices: 31.2 us -> 33 us  [swap(): return lax.ppermute(value, AXES, pairs)]
    pallas_call x2, Pallas kernels: 12 us -> 13.5 us  [attend(): pl.pallas_call(functools.partial(attend_kernel, base, block, deep, firsts...]
  transfers between devices with their start and end apart: 26 -> 26, of which waited for: 9 -> 10; matrix products, arithmetic and copies ran while one was open for 4% -> 5% of each run, Pallas kernels for 22% -> 27%
where the time goes in v5:
time: 127 us; the launch traced here: 126 us
  Pallas kernels  47 us (37%)
  waiting for transfers between devices  35.6 us (28%)
  starting transfers between devices  34.4 us (27%)
  local copies, waits for them, and re-layouts  5.51 us (4%)
  other arithmetic  3.52 us (3%)
    ppermute x25, waiting for transfers between devices, swap(): return lax.ppermute(value, AXES, pairs)  35.6 us
    ppermute x25, starting transfers between devices, swap(): return lax.ppermute(value, AXES, pairs)  33 us
    pallas_call x3, Pallas kernels, project(): pl.pallas_call(functools.partial(project_kernel, items, (len(tokens), len...  21.8 us
    pallas_call x2, Pallas kernels, attend(): pl.pallas_call(functools.partial(attend_kernel, base, block, deep, firsts...  13.5 us
    pallas_call x1, Pallas kernels, normalize(): pl.pallas_call(norm_kernel, out_shape=[jax.ShapeDtypeStruct((n, width), j...  4.11 us
    dynamic_update_slice x4, local copies, waits for them, and re-layouts, on_device(): lax.dynamic_update_slice(out, piece, (0, (member ^ r) * piece.shape[1]))  3.65 us
    pallas_call x1, Pallas kernels, pack(): pl.pallas_call(functools.partial(pack_kernel, team, depth // groups, note...  3.18 us
    concatenate x2, other arithmetic, join(): return views[0] if len(views) == 1 else jnp.concatenate(views, axis=0)  2.95 us
  transfers between devices with their start and end apart: 26, of which 10 were waited for; matrix products, arithmetic and copies ran while one was open for 5% of the time, Pallas kernels for 27%

profile of v5, /device:TPU:1, one launch (start us, length us, event | category | flops | bytes accessed | tf_op | source)
XLA Modules:
  0.0 126.2 jit_solution(16445325347995050683)
XLA Ops:
  0.0 3.2 %pack.1 = (bf16[272,768]{1,0:T(8,128)(2,1)}, bf16[272,768]{1,0:T(8,128)(2,1)}, bf16[144,768]{1,0:T(8,128)(2,1)}, bf16[144,768]{1,0:T(8,128)(2,1)}) custom-call(s32[2]{0:T(128)} %numbers.1, bf16[256,512]{1,0:T(8,128)(2,1)} %refs_0_.1, bf16[256,512]{1,0:T(8,128)(2,1)} %refs_1_.1, bf16[256,2048]{1,0:T(8,128)(2,1)} %refs_2_.1), custom_call_target="tpu_custom_call" | custom-call | bytes 3145728 | tf_op jit(solution)/shard_map/pack/pallas_call | solution.py:112
  3.2 0.1 collective-permute-start
  3.3 2.7 %collective-permute-start.1 = (bf16[144,768]{1,0:T(8,128)(2,1)}, bf16[144,768]{1,0:T(8,128)(2,1)}, u32[]{:S(2)}, u32[]{:S(2)}) collective-permute-start(bf16[144,768]{1,0:T(8,128)(2,1)} %get-tuple-element.135), channel_id=1, source_target_pairs={{0,2},{1,3},{2,0},{3,1},{4,6},{5,7},{6,4},{7,5},{8,10},{9,11},{10,... | collective-permute-start | bytes 663560 | tf_op jit(solution)/shard_map/ppermute | solution.py:38
  6.0 0.0 collective-permute-start.2
  6.1 4.1 %normalize.1.refs_0_ = bf16[256,4096]{1,0:T(8,128)(2,1)} custom-call(bf16[256,4096]{1,0:T(8,128)(2,1)} %tokens_ref, f32[1,4096]{1,0:T(1,128)} %bitcast.4), custom_call_target="tpu_custom_call" | custom-call | flops 6291456 | bytes 4194304 | tf_op jit(solution)/shard_map/normalize/pallas_call | solution.py:67
  10.2 0.6 pad_add_fusion.place
  10.7 1.3 %collective-permute-done.1.refs_2_.refs_5_.refs_7_ = bf16[144,768]{1,0:T(8,128)(2,1)} collective-permute-done((bf16[144,768]{1,0:T(8,128)(2,1)}, bf16[144,768]{1,0:T(8,128)(2,1)}, u32[]{:S(2)}, u32[]{:S(2)}) %collective-permute-start.1) | collective-permute-done | bytes 221216 | tf_op jit(solution)/shard_map/ppermute | solution.py:38
  12.0 4.7 %collective-permute-done.2.refs_3_.refs_6_.refs_8_ = bf16[144,768]{1,0:T(8,128)(2,1)} collective-permute-done((bf16[144,768]{1,0:T(8,128)(2,1)}, bf16[144,768]{1,0:T(8,128)(2,1)}, u32[]{:S(2)}, u32[]{:S(2)}) %collective-permute-start.2) | collective-permute-done | bytes 221216 | tf_op jit(solution)/shard_map/ppermute | solution.py:38
  16.8 0.0 collective-permute-done.refs_1_.refs_4_.refs_6_
  16.8 2.3 %shards.1 = (bf16[528,256]{1,0:T(8,128)(2,1)}, bf16[512,256]{1,0:T(8,128)(2,1)}, bf16[512,256]{1,0:T(8,128)(2,1)}, bf16[256,768]{1,0:T(8,128)(2,1)}) custom-call(s32[3]{0:T(128)} %pad_add_fusion.place, bf16[272,768]{1,0:T(8,128)(2,1)} %get-tuple-element.228.refs_0_.refs_3_.refs_5_, bf16[272,768]{1,0:T(8,128)(2,1)} %collective-permute-done.refs_1_.refs_4_.refs_6_, ...), custom_call_target="tpu_custom_call" | custom-call | bytes 2359296 | tf_op jit(solution)/shard_map/shards/pallas_call | solution.py:157
  19.1 0.4 collective-permute-start.4
  19.5 1.3 %collective-permute-start.11 = (bf16[256,4096]{1,0:T(8,128)(2,1)}, bf16[256,4096]{1,0:T(8,128)(2,1)}, u32[]{:S(2)}, u32[]{:S(2)}) collective-permute-start(bf16[256,4096]{1,0:T(8,128)(2,1)} %normalize.1.refs_0_), channel_id=1, source_target_pairs={{0,2},{1,3},{2,0},{3,1},{4,6},{5,7},{6,4},{7,5},{8,10},{9,11},{10,... | collective-permute-start | bytes 6291464 | tf_op jit(solution)/shard_map/ppermute | solution.py:38
  20.8 1.2 collective-permute-start.3
  22.0 1.3 %collective-permute-start.5 = (bf16[528,256]{1,0:T(8,128)(2,1)}, bf16[528,256]{1,0:T(8,128)(2,1)S(1)}, u32[]{:S(2)}, u32[]{:S(2)}) collective-permute-start(bf16[528,256]{1,0:T(8,128)(2,1)} %get-tuple-element.184.refs_0_), channel_id=1, source_target_pairs={{0,4},{1,5},{2,6},{3,7},{4,0},{5,1},{6,2},{7,3},{8,12},{9,13},{10,... | collective-permute-start | bytes 811016 | tf_op jit(solution)/shard_map/ppermute | solution.py:38
  23.3 2.3 %collective-permute-start.6 = (bf16[528,256]{1,0:T(8,128)(2,1)}, bf16[528,256]{1,0:T(8,128)(2,1)S(1)}, u32[]{:S(2)}, u32[]{:S(2)}) collective-permute-start(bf16[528,256]{1,0:T(8,128)(2,1)} %get-tuple-element.184.refs_0_), channel_id=1, source_target_pairs={{0,8},{1,9},{2,10},{3,11},{4,12},{5,13},{6,14},{7,15},{8,0},{9,1},... | collective-permute-start | bytes 811016 | tf_op jit(solution)/shard_map/ppermute | solution.py:38
  25.6 9.5 %collective-permute-done.5.refs_1_.refs_7_ = bf16[528,256]{1,0:T(8,128)(2,1)S(1)} collective-permute-done((bf16[528,256]{1,0:T(8,128)(2,1)}, bf16[528,256]{1,0:T(8,128)(2,1)S(1)}, u32[]{:S(2)}, u32[]{:S(2)}) %collective-permute-start.5) | collective-permute-done | bytes 270368 | tf_op jit(solution)/shard_map/ppermute | solution.py:38
  35.1 0.0 collective-permute-done.3.refs_2_.refs_4_
  35.1 0.8 copy-done.2
  35.9 0.0 collective-permute-done.4.refs_1_
  35.9 0.0 collective-permute-done.6.refs_2_.refs_9_
  35.9 1.1 pad_maximum_fusion
  37.0 1.6 %collective-permute-start.9 = (bf16[1040,256]{1,0:T(8,128)(2,1)S(1)}, bf16[1040,256]{1,0:T(8,128)(2,1)}, u32[]{:S(2)}, u32[]{:S(2)}) collective-permute-start(bf16[1040,256]{1,0:T(8,128)(2,1)S(1)} %pad_maximum_fusion), channel_id=1, source_target_pairs={{0,4},{1,5},{2,6},{3,7},{4,0},{5,1},{6,2},{7,3},{8,12},{9,13},{10,... | collective-permute-start | bytes 1597448 | tf_op jit(solution)/shard_map/ppermute | solution.py:38
  38.7 0.3 collective-permute-start.7
  38.9 1.2 collective-permute-start.8
  40.1 1.0 collective-permute-start.10
  41.2 3.5 %collective-permute-done.7.refs_8_ = bf16[528,256]{1,0:T(8,128)(2,1)S(1)} collective-permute-done((bf16[528,256]{1,0:T(8,128)(2,1)S(1)}, bf16[528,256]{1,0:T(8,128)(2,1)S(1)}, u32[]{:S(2)}, u32[]{:S(2)}) %collective-permute-start.7) | collective-permute-done | bytes 270368 | tf_op jit(solution)/shard_map/ppermute | solution.py:38
  44.7 5.8 %collective-permute-done.8.refs_10_ = bf16[528,256]{1,0:T(8,128)(2,1)S(1)} collective-permute-done((bf16[528,256]{1,0:T(8,128)(2,1)S(1)}, bf16[528,256]{1,0:T(8,128)(2,1)S(1)}, u32[]{:S(2)}, u32[]{:S(2)}) %collective-permute-start.8) | collective-permute-done | bytes 270368 | tf_op jit(solution)/shard_map/ppermute | solution.py:38
  50.5 2.9 %collective-permute-done.9.refs_3_.refs_11_.refs_9_ = bf16[1040,256]{1,0:T(8,128)(2,1)} collective-permute-done((bf16[1040,256]{1,0:T(8,128)(2,1)S(1)}, bf16[1040,256]{1,0:T(8,128)(2,1)}, u32[]{:S(2)}, u32[]{:S(2)}) %collective-permute-start.9) | collective-permute-done | bytes 532512 | tf_op jit(solution)/shard_map/ppermute | solution.py:38
  53.4 0.6 collective-permute-done.10.refs_11_
  54.0 0.3 collective-permute-start.12
  54.3 1.9 %pad_maximum_fusion.1 = bf16[1024,256]{1,0:T(8,128)(2,1)} fusion(bf16[512,256]{1,0:T(8,128)(2,1)} %get-tuple-element.202, bf16[512,256]{1,0:T(8,128)(2,1)} %collective-permute-done.10.refs_11_), kind=kLoop, calls=%fused_computation.1 | loop fusion | flops 1048576 | bytes 1048576 | tf_op jit(solution)/shard_map/concatenate | solution.py:541
  56.1 1.1 collective-permute-start.14
  57.2 1.2 collective-permute-start.13
  58.4 2.0 %collective-permute-start.15 = (bf16[512,256]{1,0:T(8,128)(2,1)}, bf16[512,256]{1,0:T(8,128)(2,1)}, u32[]{:S(2)}, u32[]{:S(2)}) collective-permute-start(bf16[512,256]{1,0:T(8,128)(2,1)} %get-tuple-element.202), channel_id=1, source_target_pairs={{0,8},{1,9},{2,10},{3,11},{4,12},{5,13},{6,14},{7,15},{8,0},{9,1},... | collective-permute-start | bytes 786440 | tf_op jit(solution)/shard_map/ppermute | solution.py:38
  60.4 2.1 %places.1 = (s32[16,128]{1,0:T(8,128)}, s32[16,128]{1,0:T(8,128)}) custom-call(s32[3]{0:T(128)} %pad_add_fusion.place, bf16[528,256]{1,0:T(8,128)(2,1)} %get-tuple-element.184.refs_0_, bf16[528,256]{1,0:T(8,128)(2,1)} %copy-done.1, bf16[528,256]{1,0:T(8,128)(2,1)} %copy-done, bf16[1040,256]{1,0:T(8,128)(2,1)} %collective-permute-done.9.refs_3_.refs_11_.refs_9_), custom_call_target="tpu_custom_call" | custom-call | bytes 65536 | tf_op jit(solution)/shard_map/places/pallas_call | solution.py:376
  62.5 5.5 %project.3 = (f32[512,256]{1,0:T(8,128)}, bf16[512,512]{1,0:T(8,128)(2,1)}) custom-call(s32[3]{0:T(128)} %pad_add_fusion.place, bf16[256,4096]{1,0:T(8,128)(2,1)} %normalize.1.refs_0_, bf16[256,4096]{1,0:T(8,128)(2,1)} %collective-permute-done.4.refs_1_, bf16[256,768]{1,0:T(8,128)(2,1)} %copy-done.2, ...), custom_call_target="tpu_custom_call" | custom-call | flops 939524096 | bytes 6291456 | tf_op jit(solution)/shard_map/project/pallas_call | solution.py:320
  68.0 2.0 %collective-permute-done.13.refs_12_ = bf16[512,256]{1,0:T(8,128)(2,1)} collective-permute-done((bf16[512,256]{1,0:T(8,128)(2,1)}, bf16[512,256]{1,0:T(8,128)(2,1)}, u32[]{:S(2)}, u32[]{:S(2)}) %collective-permute-start.13) | collective-permute-done | bytes 262176 | tf_op jit(solution)/shard_map/ppermute | solution.py:38
  70.0 2.6 %collective-permute-done.14.refs_13_ = bf16[1024,256]{1,0:T(8,128)(2,1)} collective-permute-done((bf16[1024,256]{1,0:T(8,128)(2,1)}, bf16[1024,256]{1,0:T(8,128)(2,1)}, u32[]{:S(2)}, u32[]{:S(2)}) %collective-permute-start.14) | collective-permute-done | bytes 524320 | tf_op jit(solution)/shard_map/ppermute | solution.py:38
  72.6 3.8 %collective-permute-start.16 = (bf16[256,4096]{1,0:T(8,128)(2,1)}, bf16[256,4096]{1,0:T(8,128)(2,1)}, u32[]{:S(2)}, u32[]{:S(2)}) collective-permute-start(bf16[256,4096]{1,0:T(8,128)(2,1)} %collective-permute-done.11.refs_0_.refs_2_), channel_id=1, source_target_pairs={{0,1},{1,0},{2,3},{3,2},{4,5},{5,4},{6,7},{7,6},{8,9},{9,8},{10,11... | collective-permute-start | bytes 6291464 | tf_op jit(solution)/shard_map/ppermute | solution.py:38
  76.4 1.2 collective-permute-start.19
  77.6 3.1 %collective-permute-start.20 = (bf16[512,256]{1,0:T(8,128)(2,1)}, bf16[512,256]{1,0:T(8,128)(2,1)}, u32[]{:S(2)}, u32[]{:S(2)}) collective-permute-start(bf16[512,256]{1,0:T(8,128)(2,1)} %collective-permute-done.15.refs_15_), channel_id=1, source_target_pairs={{0,4},{1,5},{2,6},{3,7},{4,0},{5,1},{6,2},{7,3},{8,12},{9,13},{10,... | collective-permute-start | bytes 786440 | tf_op jit(solution)/shard_map/ppermute | solution.py:38
  80.7 0.3 collective-permute-start.21
  81.0 6.1 %project.4 = (bf16[1024,256]{1,0:T(8,128)(2,1)}, bf16[768,256]{1,0:T(8,128)(2,1)}, bf16[768,256]{1,0:T(8,128)(2,1)}) custom-call(s32[3]{0:T(128)} %pad_add_fusion.place, bf16[256,4096]{1,0:T(8,128)(2,1)} %collective-permute-done.11.refs_0_.refs_2_, bf16[256,4096]{1,0:T(8,128)(2,1)} %collective-permute-done.16.refs_1_.refs_3_, bf16[256,768]{1,0:T(8,128)(2,1)} %copy-done.2, ...), custom_call_target="tpu_custom_call" | custom-call | flops 1073741824 | bytes 6815744 | tf_op jit(solution)/shard_map/project/pallas_call | solution.py:320
  87.1 2.7 %collective-permute-start.17 = (bf16[768,256]{1,0:T(8,128)(2,1)}, bf16[768,256]{1,0:T(8,128)(2,1)}, u32[]{:S(2)}, u32[]{:S(2)}) collective-permute-start(bf16[768,256]{1,0:T(8,128)(2,1)} %get-tuple-element.240), channel_id=1, source_target_pairs={{0,4},{1,5},{2,6},{3,7},{4,0},{5,1},{6,2},{7,3},{8,12},{9,13},{10,... | collective-permute-start | bytes 1179656 | tf_op jit(solution)/shard_map/ppermute | solution.py:38
  89.8 1.2 collective-permute-start.22
  91.0 1.4 %collective-permute-start.18 = (bf16[768,256]{1,0:T(8,128)(2,1)}, bf16[768,256]{1,0:T(8,128)(2,1)}, u32[]{:S(2)}, u32[]{:S(2)}) collective-permute-start(bf16[768,256]{1,0:T(8,128)(2,1)} %get-tuple-element.242), channel_id=1, source_target_pairs={{4,8},{5,9},{6,10},{7,11},{8,4},{9,5},{10,6},{11,7},{20,24},{21,25... | collective-permute-start | bytes 1179656 | tf_op jit(solution)/shard_map/ppermute | solution.py:49
  92.5 10.2 %project.5 = (bf16[1024,256]{1,0:T(8,128)(2,1)}, f32[1024,256]{1,0:T(8,128)}, bf16[1024,1024]{1,0:T(8,128)(2,1)}) custom-call(s32[3]{0:T(128)} %pad_add_fusion.place, bf16[256,4096]{1,0:T(8,128)(2,1)} %normalize.1.refs_0_, bf16[256,4096]{1,0:T(8,128)(2,1)} %collective-permute-done.4.refs_1_, bf16[256,4096]{1,0:T(8,128)(2,1)} %collective-permute-done.11.refs_0_.refs_2_, ...), custom_call_target="tpu_custom_call" | custom-call | flops 4294967296 | bytes 13631488 | tf_op jit(solution)/shard_map/project/pallas_call | solution.py:320
  102.7 0.0 collective-permute-done.21.refs_3_
  102.7 0.0 collective-permute-done.22.refs_4_
  102.7 0.0 collective-permute-done.18.outer
  102.7 6.9 %attend.3 = (bf16[256,512]{1,0:T(8,128)(2,1)}, bf16[256,512]{1,0:T(8,128)(2,1)}) custom-call(s32[16,128]{1,0:T(8,128)} %get-tuple-element.224.first_ref, s32[16,128]{1,0:T(8,128)} %get-tuple-element.225.count_ref, s32[3]{0:T(128)} %pad_add_fusion.place, bf16[768,256]{1,0:T(8,128)(2,1)} %collective-permute-done.17.inner, ...), custom_call_target="tpu_custom_call" | custom-call | flops 939524096 | bytes 1835008 | tf_op jit(solution)/shard_map/attend/pallas_call | solution.py:485
  109.6 0.2 collective-permute-start.23
  109.8 2.3 %collective-permute-start.24 = (bf16[256,512]{1,0:T(8,128)(2,1)}, bf16[256,512]{1,0:T(8,128)(2,1)}, u32[]{:S(2)}, u32[]{:S(2)}) collective-permute-start(bf16[256,512]{1,0:T(8,128)(2,1)} %get-tuple-element.255), channel_id=1, source_target_pairs={{0,3},{1,2},{2,1},{3,0},{4,7},{5,6},{6,5},{7,4},{8,11},{9,10},{10,... | collective-permute-start | bytes 786440 | tf_op jit(solution)/shard_map/ppermute | solution.py:38
  112.2 6.6 %attend.2 = (bf16[256,512]{1,0:T(8,128)(2,1)}, bf16[256,512]{1,0:T(8,128)(2,1)}) custom-call(s32[16,128]{1,0:T(8,128)} %get-tuple-element.224.first_ref, s32[16,128]{1,0:T(8,128)} %get-tuple-element.225.count_ref, s32[3]{0:T(128)} %pad_add_fusion.place, bf16[768,256]{1,0:T(8,128)(2,1)} %collective-permute-done.17.inner, ...), custom_call_target="tpu_custom_call" | custom-call | flops 939524096 | bytes 1835008 | tf_op jit(solution)/shard_map/attend/pallas_call | solution.py:485
  118.8 0.0 collective-permute-start.25
  118.8 0.1 broadcast_in_dim.3
  118.9 1.0 constant_dynamic-update-slice_fusion.3
  119.9 1.0 constant_dynamic-update-slice_fusion.2
  120.9 2.7 %collective-permute-done.24 = bf16[256,512]{1,0:T(8,128)(2,1)} collective-permute-done((bf16[256,512]{1,0:T(8,128)(2,1)}, bf16[256,512]{1,0:T(8,128)(2,1)}, u32[]{:S(2)}, u32[]{:S(2)}) %collective-permute-start.24) | collective-permute-done | bytes 262176 | tf_op jit(solution)/shard_map/ppermute | solution.py:38
  123.6 1.0 constant_dynamic-update-slice_fusion.1
  124.5 0.0 copy-start.5
  124.6 0.0 collective-permute-done.25
  124.6 1.0 copy-done.5
  125.5 0.7 constant_dynamic-update-slice_fusion
  (17 shorter events, 0.0 us)
Async XLA Ops:
  3.2 13.6 %collective-permute-start = (bf16[272,768]{1,0:T(8,128)(2,1)}, bf16[272,768]{1,0:T(8,128)(2,1)}, u32[]{:S(2)}, u32[]{:S(2)}) collective-permute-start(bf16[272,768]{1,0:T(8,128)(2,1)} %get-tuple-element.134), channel_id=1, source_target_pairs={{0,1},{1,0},{2,3},{3,2},{4,5},{5,4},{6,7},{7,6},{8,9},{9,8},{10,11... | collective-permute-start | bytes 1253384 | tf_op jit(solution)/shard_map/ppermute | solution.py:38
  3.3 8.7 %collective-permute-start.1 = (bf16[144,768]{1,0:T(8,128)(2,1)}, bf16[144,768]{1,0:T(8,128)(2,1)}, u32[]{:S(2)}, u32[]{:S(2)}) collective-permute-start(bf16[144,768]{1,0:T(8,128)(2,1)} %get-tuple-element.135), channel_id=1, source_target_pairs={{0,2},{1,3},{2,0},{3,1},{4,6},{5,7},{6,4},{7,5},{8,10},{9,11},{10,... | collective-permute-start | bytes 663560 | tf_op jit(solution)/shard_map/ppermute | solution.py:38
  6.0 10.8 %collective-permute-start.2 = (bf16[144,768]{1,0:T(8,128)(2,1)}, bf16[144,768]{1,0:T(8,128)(2,1)}, u32[]{:S(2)}, u32[]{:S(2)}) collective-permute-start(bf16[144,768]{1,0:T(8,128)(2,1)} %get-tuple-element.136), channel_id=1, source_target_pairs={{0,3},{1,2},{2,1},{3,0},{4,7},{5,6},{6,5},{7,4},{8,11},{9,10},{10,... | collective-permute-start | bytes 663560 | tf_op jit(solution)/shard_map/ppermute | solution.py:38
  19.1 16.8 %collective-permute-start.4 = (bf16[256,4096]{1,0:T(8,128)(2,1)}, bf16[256,4096]{1,0:T(8,128)(2,1)}, u32[]{:S(2)}, u32[]{:S(2)}) collective-permute-start(bf16[256,4096]{1,0:T(8,128)(2,1)} %normalize.1.refs_0_), channel_id=1, source_target_pairs={{0,1},{1,0},{2,3},{3,2},{4,5},{5,4},{6,7},{7,6},{8,9},{9,8},{10,11... | collective-permute-start | bytes 6291464 | tf_op jit(solution)/shard_map/ppermute | solution.py:38
  19.5 48.5 %collective-permute-start.11 = (bf16[256,4096]{1,0:T(8,128)(2,1)}, bf16[256,4096]{1,0:T(8,128)(2,1)}, u32[]{:S(2)}, u32[]{:S(2)}) collective-permute-start(bf16[256,4096]{1,0:T(8,128)(2,1)} %normalize.1.refs_0_), channel_id=1, source_target_pairs={{0,2},{1,3},{2,0},{3,1},{4,6},{5,7},{6,4},{7,5},{8,10},{9,11},{10,... | collective-permute-start | bytes 6291464 | tf_op jit(solution)/shard_map/ppermute | solution.py:38
  20.8 14.4 %collective-permute-start.3 = (bf16[256,768]{1,0:T(8,128)(2,1)}, bf16[256,768]{1,0:T(8,128)(2,1)S(1)}, u32[]{:S(2)}, u32[]{:S(2)}) collective-permute-start(bf16[256,768]{1,0:T(8,128)(2,1)} %get-tuple-element.141), channel_id=1, source_target_pairs={{0,16},{1,17},{2,18},{3,19},{4,20},{5,21},{6,22},{7,23},{8,24},{9,... | collective-permute-start | bytes 1179656 | tf_op jit(solution)/shard_map/ppermute | solution.py:38
  22.0 13.1 %collective-permute-start.5 = (bf16[528,256]{1,0:T(8,128)(2,1)}, bf16[528,256]{1,0:T(8,128)(2,1)S(1)}, u32[]{:S(2)}, u32[]{:S(2)}) collective-permute-start(bf16[528,256]{1,0:T(8,128)(2,1)} %get-tuple-element.184.refs_0_), channel_id=1, source_target_pairs={{0,4},{1,5},{2,6},{3,7},{4,0},{5,1},{6,2},{7,3},{8,12},{9,13},{10,... | collective-permute-start | bytes 811016 | tf_op jit(solution)/shard_map/ppermute | solution.py:38
  23.3 12.6 %collective-permute-start.6 = (bf16[528,256]{1,0:T(8,128)(2,1)}, bf16[528,256]{1,0:T(8,128)(2,1)S(1)}, u32[]{:S(2)}, u32[]{:S(2)}) collective-permute-start(bf16[528,256]{1,0:T(8,128)(2,1)} %get-tuple-element.184.refs_0_), channel_id=1, source_target_pairs={{0,8},{1,9},{2,10},{3,11},{4,12},{5,13},{6,14},{7,15},{8,0},{9,1},... | collective-permute-start | bytes 811016 | tf_op jit(solution)/shard_map/ppermute | solution.py:38
  35.1 15.3 %copy-start.1 = (bf16[528,256]{1,0:T(8,128)(2,1)}, bf16[528,256]{1,0:T(8,128)(2,1)S(1)}, u32[]{:S(2)}) copy-start(bf16[528,256]{1,0:T(8,128)(2,1)S(1)} %collective-permute-done.5.refs_1_.refs_7_) | copy-start | bytes 811012
  35.1 0.8 copy-start.2
  35.9 3.0 %copy-start = (bf16[528,256]{1,0:T(8,128)(2,1)}, bf16[528,256]{1,0:T(8,128)(2,1)S(1)}, u32[]{:S(2)}) copy-start(bf16[528,256]{1,0:T(8,128)(2,1)S(1)} %collective-permute-done.6.refs_2_.refs_9_) | copy-start | bytes 811012
  37.0 16.4 %collective-permute-start.9 = (bf16[1040,256]{1,0:T(8,128)(2,1)S(1)}, bf16[1040,256]{1,0:T(8,128)(2,1)}, u32[]{:S(2)}, u32[]{:S(2)}) collective-permute-start(bf16[1040,256]{1,0:T(8,128)(2,1)S(1)} %pad_maximum_fusion), channel_id=1, source_target_pairs={{0,4},{1,5},{2,6},{3,7},{4,0},{5,1},{6,2},{7,3},{8,12},{9,13},{10,... | collective-permute-start | bytes 1597448 | tf_op jit(solution)/shard_map/ppermute | solution.py:38
  38.7 6.0 %collective-permute-start.7 = (bf16[528,256]{1,0:T(8,128)(2,1)S(1)}, bf16[528,256]{1,0:T(8,128)(2,1)S(1)}, u32[]{:S(2)}, u32[]{:S(2)}) collective-permute-start(bf16[528,256]{1,0:T(8,128)(2,1)S(1)} %collective-permute-done.5.refs_1_.refs_7_), channel_id=1, source_target_pairs={{0,16},{1,17},{2,18},{3,19},{4,20},{5,21},{6,22},{7,23},{8,24},{9,... | collective-permute-start | bytes 811016 | tf_op jit(solution)/shard_map/ppermute | solution.py:38
  38.9 11.5 %collective-permute-start.8 = (bf16[528,256]{1,0:T(8,128)(2,1)S(1)}, bf16[528,256]{1,0:T(8,128)(2,1)S(1)}, u32[]{:S(2)}, u32[]{:S(2)}) collective-permute-start(bf16[528,256]{1,0:T(8,128)(2,1)S(1)} %collective-permute-done.6.refs_2_.refs_9_), channel_id=1, source_target_pairs={{0,16},{1,17},{2,18},{3,19},{4,20},{5,21},{6,22},{7,23},{8,24},{9,... | collective-permute-start | bytes 811016 | tf_op jit(solution)/shard_map/ppermute | solution.py:38
  40.1 13.9 %collective-permute-start.10 = (bf16[512,256]{1,0:T(8,128)(2,1)}, bf16[512,256]{1,0:T(8,128)(2,1)}, u32[]{:S(2)}, u32[]{:S(2)}) collective-permute-start(bf16[512,256]{1,0:T(8,128)(2,1)} %get-tuple-element.168), channel_id=1, source_target_pairs={{0,8},{1,9},{2,10},{3,11},{4,12},{5,13},{6,14},{7,15},{8,0},{9,1},... | collective-permute-start | bytes 786440 | tf_op jit(solution)/shard_map/ppermute | solution.py:38
  44.7 8.7 %copy-start.3 = (bf16[528,256]{1,0:T(8,128)(2,1)}, bf16[528,256]{1,0:T(8,128)(2,1)S(1)}, u32[]{:S(2)}) copy-start(bf16[528,256]{1,0:T(8,128)(2,1)S(1)} %collective-permute-done.7.refs_8_) | copy-start | bytes 811012
  50.5 3.5 %copy-start.4 = (bf16[528,256]{1,0:T(8,128)(2,1)}, bf16[528,256]{1,0:T(8,128)(2,1)S(1)}, u32[]{:S(2)}) copy-start(bf16[528,256]{1,0:T(8,128)(2,1)S(1)} %collective-permute-done.8.refs_10_) | copy-start | bytes 811012
  54.0 18.6 %collective-permute-start.12 = (bf16[1040,256]{1,0:T(8,128)(2,1)}, bf16[1040,256]{1,0:T(8,128)(2,1)}, u32[]{:S(2)}, u32[]{:S(2)}) collective-permute-start(bf16[1040,256]{1,0:T(8,128)(2,1)} %collective-permute-done.9.refs_3_.refs_11_.refs_9_), channel_id=1, source_target_pairs={{0,16},{1,17},{2,18},{3,19},{4,20},{5,21},{6,22},{7,23},{8,24},{9,... | collective-permute-start | bytes 1597448 | tf_op jit(solution)/shard_map/ppermute | solution.py:38
  56.1 16.5 %collective-permute-start.14 = (bf16[1024,256]{1,0:T(8,128)(2,1)}, bf16[1024,256]{1,0:T(8,128)(2,1)}, u32[]{:S(2)}, u32[]{:S(2)}) collective-permute-start(bf16[1024,256]{1,0:T(8,128)(2,1)} %pad_maximum_fusion.1), channel_id=1, source_target_pairs={{0,4},{1,5},{2,6},{3,7},{4,0},{5,1},{6,2},{7,3},{8,12},{9,13},{10,... | collective-permute-start | bytes 1572872 | tf_op jit(solution)/shard_map/ppermute | solution.py:38
  57.2 12.8 %collective-permute-start.13 = (bf16[512,256]{1,0:T(8,128)(2,1)}, bf16[512,256]{1,0:T(8,128)(2,1)}, u32[]{:S(2)}, u32[]{:S(2)}) collective-permute-start(bf16[512,256]{1,0:T(8,128)(2,1)} %collective-permute-done.10.refs_11_), channel_id=1, source_target_pairs={{0,16},{1,17},{2,18},{3,19},{4,20},{5,21},{6,22},{7,23},{8,24},{9,... | collective-permute-start | bytes 786440 | tf_op jit(solution)/shard_map/ppermute | solution.py:38
  58.4 14.2 %collective-permute-start.15 = (bf16[512,256]{1,0:T(8,128)(2,1)}, bf16[512,256]{1,0:T(8,128)(2,1)}, u32[]{:S(2)}, u32[]{:S(2)}) collective-permute-start(bf16[512,256]{1,0:T(8,128)(2,1)} %get-tuple-element.202), channel_id=1, source_target_pairs={{0,8},{1,9},{2,10},{3,11},{4,12},{5,13},{6,14},{7,15},{8,0},{9,1},... | collective-permute-start | bytes 786440 | tf_op jit(solution)/shard_map/ppermute | solution.py:38
  72.6 8.3 %collective-permute-start.16 = (bf16[256,4096]{1,0:T(8,128)(2,1)}, bf16[256,4096]{1,0:T(8,128)(2,1)}, u32[]{:S(2)}, u32[]{:S(2)}) collective-permute-start(bf16[256,4096]{1,0:T(8,128)(2,1)} %collective-permute-done.11.refs_0_.refs_2_), channel_id=1, source_target_pairs={{0,1},{1,0},{2,3},{3,2},{4,5},{5,4},{6,7},{7,6},{8,9},{9,8},{10,11... | collective-permute-start | bytes 6291464 | tf_op jit(solution)/shard_map/ppermute | solution.py:38
  76.4 16.0 %collective-permute-start.19 = (bf16[1024,256]{1,0:T(8,128)(2,1)}, bf16[1024,256]{1,0:T(8,128)(2,1)}, u32[]{:S(2)}, u32[]{:S(2)}) collective-permute-start(bf16[1024,256]{1,0:T(8,128)(2,1)} %collective-permute-done.14.refs_13_), channel_id=1, source_target_pairs={{0,16},{1,17},{2,18},{3,19},{4,20},{5,21},{6,22},{7,23},{8,24},{9,... | collective-permute-start | bytes 1572872 | tf_op jit(solution)/shard_map/ppermute | solution.py:38
  77.6 12.2 %collective-permute-start.20 = (bf16[512,256]{1,0:T(8,128)(2,1)}, bf16[512,256]{1,0:T(8,128)(2,1)}, u32[]{:S(2)}, u32[]{:S(2)}) collective-permute-start(bf16[512,256]{1,0:T(8,128)(2,1)} %collective-permute-done.15.refs_15_), channel_id=1, source_target_pairs={{0,4},{1,5},{2,6},{3,7},{4,0},{5,1},{6,2},{7,3},{8,12},{9,13},{10,... | collective-permute-start | bytes 786440 | tf_op jit(solution)/shard_map/ppermute | solution.py:38
  80.7 22.0 %collective-permute-start.21 = (bf16[512,256]{1,0:T(8,128)(2,1)}, bf16[512,256]{1,0:T(8,128)(2,1)}, u32[]{:S(2)}, u32[]{:S(2)}) collective-permute-start(bf16[512,256]{1,0:T(8,128)(2,1)} %collective-permute-done.15.refs_15_), channel_id=1, source_target_pairs={{0,16},{1,17},{2,18},{3,19},{4,20},{5,21},{6,22},{7,23},{8,24},{9,... | collective-permute-start | bytes 786440 | tf_op jit(solution)/shard_map/ppermute | solution.py:38
  87.1 15.6 %collective-permute-start.17 = (bf16[768,256]{1,0:T(8,128)(2,1)}, bf16[768,256]{1,0:T(8,128)(2,1)}, u32[]{:S(2)}, u32[]{:S(2)}) collective-permute-start(bf16[768,256]{1,0:T(8,128)(2,1)} %get-tuple-element.240), channel_id=1, source_target_pairs={{0,4},{1,5},{2,6},{3,7},{4,0},{5,1},{6,2},{7,3},{8,12},{9,13},{10,... | collective-permute-start | bytes 1179656 | tf_op jit(solution)/shard_map/ppermute | solution.py:38
  89.8 12.9 %collective-permute-start.22 = (bf16[512,256]{1,0:T(8,128)(2,1)}, bf16[512,256]{1,0:T(8,128)(2,1)}, u32[]{:S(2)}, u32[]{:S(2)}) collective-permute-start(bf16[512,256]{1,0:T(8,128)(2,1)} %collective-permute-done.20.refs_16_), channel_id=1, source_target_pairs={{0,16},{1,17},{2,18},{3,19},{4,20},{5,21},{6,22},{7,23},{8,24},{9,... | collective-permute-start | bytes 786440 | tf_op jit(solution)/shard_map/ppermute | solution.py:38
  91.0 11.7 %collective-permute-start.18 = (bf16[768,256]{1,0:T(8,128)(2,1)}, bf16[768,256]{1,0:T(8,128)(2,1)}, u32[]{:S(2)}, u32[]{:S(2)}) collective-permute-start(bf16[768,256]{1,0:T(8,128)(2,1)} %get-tuple-element.242), channel_id=1, source_target_pairs={{4,8},{5,9},{6,10},{7,11},{8,4},{9,5},{10,6},{11,7},{20,24},{21,25... | collective-permute-start | bytes 1179656 | tf_op jit(solution)/shard_map/ppermute | solution.py:49
  109.6 10.3 %collective-permute-start.23 = (bf16[256,512]{1,0:T(8,128)(2,1)}, bf16[256,512]{1,0:T(8,128)(2,1)}, u32[]{:S(2)}, u32[]{:S(2)}) collective-permute-start(bf16[256,512]{1,0:T(8,128)(2,1)} %get-tuple-element.254), channel_id=1, source_target_pairs={{0,2},{1,3},{2,0},{3,1},{4,6},{5,7},{6,4},{7,5},{8,10},{9,11},{10,... | collective-permute-start | bytes 786440 | tf_op jit(solution)/shard_map/ppermute | solution.py:38
  109.8 13.7 %collective-permute-start.24 = (bf16[256,512]{1,0:T(8,128)(2,1)}, bf16[256,512]{1,0:T(8,128)(2,1)}, u32[]{:S(2)}, u32[]{:S(2)}) collective-permute-start(bf16[256,512]{1,0:T(8,128)(2,1)} %get-tuple-element.255), channel_id=1, source_target_pairs={{0,3},{1,2},{2,1},{3,0},{4,7},{5,6},{6,5},{7,4},{8,11},{9,10},{10,... | collective-permute-start | bytes 786440 | tf_op jit(solution)/shard_map/ppermute | solution.py:38
  118.8 5.8 %collective-permute-start.25 = (bf16[256,512]{1,0:T(8,128)(2,1)}, bf16[256,512]{1,0:T(8,128)(2,1)S(1)}, u32[]{:S(2)}, u32[]{:S(2)}) collective-permute-start(bf16[256,512]{1,0:T(8,128)(2,1)} %get-tuple-element.256), channel_id=1, source_target_pairs={{0,1},{1,0},{2,3},{3,2},{4,5},{5,4},{6,7},{7,6},{8,9},{9,8},{10,11... | collective-permute-start | bytes 786440 | tf_op jit(solution)/shard_map/ppermute | solution.py:38
  124.5 1.0 copy-start.5

commit v6 on v5

--- a/solution.py
+++ b/solution.py
@@ -425,7 +425,6 @@
 
     heads = query.shape[1] // HD
     span = MOST_BLK * block
-    row = lax.broadcasted_iota(jnp.int32, (span, 1), 0)
 
     def place_of(b):
         return pl.ds(pl.multiple_of(first_ref[base + b, 0] * block, block), span)
@@ -445,7 +444,14 @@
     scores = score(0)
     for b in range(total_blocks):
         upcoming = score(b + 1) if b + 1 < total_blocks else None
-        scores = jnp.where(row < count_ref[base + b, 0] * block, scores, -1e30)
+        scores = jnp.concatenate(
+            [scores[:block]]
+            + [
+                jnp.where(count_ref[base + b, 0] > k, scores[k * block : (k + 1) * block], -1e30)
+                for k in range(1, MOST_BLK)
+            ],
+            axis=0,
+        )
         row_max = jnp.max(scores, axis=0, keepdims=True)
         weights = jnp.exp2((scores - row_max) * (HD ** (-0.5) * LOG2_E))
         row_total = jnp.sum(weights, axis=0, keepdims=True)
@@ -500,6 +506,27 @@
         ),
         name="attend",
     )(first, count, place, inner, own, outer, *ins)
+
+
+def assemble_kernel(place, *refs):
+    pieces, out = refs[:-1], refs[-1]
+    for r, piece in enumerate(pieces):
+        width = piece.shape[1]
+        first = pl.multiple_of((place[2] ^ r) * width, width)
+        out[:, pl.ds(first, width)] = piece[...]
+
+
+def assemble(place, pieces):
+    rows, width = pieces[0].shape
+    return pl.pallas_call(
+        assemble_kernel,
+        out_shape=jax.ShapeDtypeStruct((rows, width * len(pieces)), jnp.bfloat16),
+        in_specs=[IN_SMEM] + [IN_VMEM] * len(pieces),
+        out_specs=IN_VMEM,
+        compiler_params=PARAMS,
+        cost_estimate=cost(0, 4 * rows * width * len(pieces)),
+        name="assemble",
+    )(place, *pieces)
 
 
 def on_device(tokens, norm_gain, w_query, w_key, w_value, passage_blocks):
@@ -724,11 +751,9 @@
         )
         for r, piece in enumerate(made, start):
             pieces[r] = swap(piece, team, 0, 0, r) if r else piece
-    out = jnp.zeros((rows, w_query.shape[1]), jnp.bfloat16)
-    for r in [0, *range(2, team), 1]:
-        piece = pieces[r]
-        out = lax.dynamic_update_slice(out, piece, (0, (member ^ r) * piece.shape[1]))
-    return out
+    pieces[2:] = lax.optimization_barrier(pieces[2:])
+    pieces = lax.optimization_barrier(pieces)
+    return assemble(place, pieces)
 
 
 def solution(mesh):

time: 127 us -> 126 us (level)
  local copies, waits for them, and re-layouts: 5.51 us -> 0.8 us
  waiting for transfers between devices: 35.6 us -> 37.9 us
  Pallas kernels: 47 us -> 48.7 us
    dynamic_update_slice x4 -> x0, local copies, waits for them, and re-layouts: 3.65 us -> none  [on_device(): lax.dynamic_update_slice(out, piece, (0, (member ^ r) * piece.shape[1]))]
    ppermute x25, waiting for transfers between devices: 35.6 us -> 37.9 us  [swap(): return lax.ppermute(value, AXES, pairs)]
    pallas_call x0 -> x1, Pallas kernels: none -> 2.24 us  [assemble(): pl.pallas_call(assemble_kernel, out_shape=jax.ShapeDtypeStruct((rows, wid...]
  transfers between devices with their start and end apart: 26 -> 26, of which waited for: 10 -> 10; matrix products, arithmetic and copies ran while one was open for 5% -> 3% of each run, Pallas kernels for 27% -> 27%
where the time goes in v6:
time: 126 us; the launch traced here: 125 us
  Pallas kernels  48.7 us (39%)
  waiting for transfers between devices  37.9 us (30%)
  starting transfers between devices  34.4 us (27%)
  other arithmetic  3.62 us (3%)
    ppermute x25, waiting for transfers between devices, swap(): return lax.ppermute(value, AXES, pairs)  37.9 us
    ppermute x25, starting transfers between devices, swap(): return lax.ppermute(value, AXES, pairs)  32.9 us
    pallas_call x3, Pallas kernels, project(): pl.pallas_call(functools.partial(project_kernel, items, (len(tokens), len...  21.8 us
    pallas_call x2, Pallas kernels, attend(): pl.pallas_call(functools.partial(attend_kernel, base, block, deep, firsts...  12.9 us
    pallas_call x1, Pallas kernels, normalize(): pl.pallas_call(norm_kernel, out_shape=[jax.ShapeDtypeStruct((n, width), j...  4.11 us
    pallas_call x1, Pallas kernels, pack(): pl.pallas_call(functools.partial(pack_kernel, team, depth // groups, note...  3.19 us
    concatenate x2, other arithmetic, join(): return views[0] if len(views) == 1 else jnp.concatenate(views, axis=0)  2.95 us
  transfers between devices with their start and end apart: 26, of which 10 were waited for; matrix products, arithmetic and copies ran while one was open for 3% of the time, Pallas kernels for 27%

profile of v6, /device:TPU:1, one launch (start us, length us, event | category | flops | bytes accessed | tf_op | source)
XLA Modules:
  0.0 125.5 jit_solution(10240483898330986762)
XLA Ops:
  0.0 3.2 %pack.1 = (bf16[272,768]{1,0:T(8,128)(2,1)}, bf16[272,768]{1,0:T(8,128)(2,1)}, bf16[144,768]{1,0:T(8,128)(2,1)}, bf16[144,768]{1,0:T(8,128)(2,1)}) custom-call(s32[2]{0:T(128)} %numbers.1, bf16[256,512]{1,0:T(8,128)(2,1)} %refs_0_.1, bf16[256,512]{1,0:T(8,128)(2,1)} %refs_1_.1, bf16[256,2048]{1,0:T(8,128)(2,1)} %refs_2_.1), custom_call_target="tpu_custom_call" | custom-call | bytes 3145728 | tf_op jit(solution)/shard_map/pack/pallas_call | solution.py:112
  3.2 0.1 collective-permute-start
  3.3 2.7 %collective-permute-start.1 = (bf16[144,768]{1,0:T(8,128)(2,1)}, bf16[144,768]{1,0:T(8,128)(2,1)}, u32[]{:S(2)}, u32[]{:S(2)}) collective-permute-start(bf16[144,768]{1,0:T(8,128)(2,1)} %get-tuple-element.141), channel_id=1, source_target_pairs={{0,2},{1,3},{2,0},{3,1},{4,6},{5,7},{6,4},{7,5},{8,10},{9,11},{10,... | collective-permute-start | bytes 663560 | tf_op jit(solution)/shard_map/ppermute | solution.py:38
  6.0 0.0 collective-permute-start.2
  6.1 4.1 %normalize.1.refs_0_ = bf16[256,4096]{1,0:T(8,128)(2,1)} custom-call(bf16[256,4096]{1,0:T(8,128)(2,1)} %tokens_ref, f32[1,4096]{1,0:T(1,128)} %bitcast.4), custom_call_target="tpu_custom_call" | custom-call | flops 6291456 | bytes 4194304 | tf_op jit(solution)/shard_map/normalize/pallas_call | solution.py:67
  10.2 0.7 pad_add_fusion.place
  10.8 1.2 collective-permute-done.1.refs_2_.refs_5_.refs_7_
  12.0 4.7 %collective-permute-done.2.refs_3_.refs_6_.refs_8_ = bf16[144,768]{1,0:T(8,128)(2,1)} collective-permute-done((bf16[144,768]{1,0:T(8,128)(2,1)}, bf16[144,768]{1,0:T(8,128)(2,1)}, u32[]{:S(2)}, u32[]{:S(2)}) %collective-permute-start.2) | collective-permute-done | bytes 221216 | tf_op jit(solution)/shard_map/ppermute | solution.py:38
  16.8 0.0 collective-permute-done.refs_1_.refs_4_.refs_6_
  16.8 2.3 %shards.1 = (bf16[528,256]{1,0:T(8,128)(2,1)}, bf16[512,256]{1,0:T(8,128)(2,1)}, bf16[512,256]{1,0:T(8,128)(2,1)}, bf16[256,768]{1,0:T(8,128)(2,1)}) custom-call(s32[3]{0:T(128)} %pad_add_fusion.place, bf16[272,768]{1,0:T(8,128)(2,1)} %get-tuple-element.234.refs_0_.refs_3_.refs_5_, bf16[272,768]{1,0:T(8,128)(2,1)} %collective-permute-done.refs_1_.refs_4_.refs_6_, ...), custom_call_target="tpu_custom_call" | custom-call | bytes 2359296 | tf_op jit(solution)/shard_map/shards/pallas_call | solution.py:157
  19.1 0.4 collective-permute-start.4
  19.5 1.3 %collective-permute-start.11 = (bf16[256,4096]{1,0:T(8,128)(2,1)}, bf16[256,4096]{1,0:T(8,128)(2,1)}, u32[]{:S(2)}, u32[]{:S(2)}) collective-permute-start(bf16[256,4096]{1,0:T(8,128)(2,1)} %normalize.1.refs_0_), channel_id=1, source_target_pairs={{0,2},{1,3},{2,0},{3,1},{4,6},{5,7},{6,4},{7,5},{8,10},{9,11},{10,... | collective-permute-start | bytes 6291464 | tf_op jit(solution)/shard_map/ppermute | solution.py:38
  20.8 1.2 collective-permute-start.3
  22.0 1.3 %collective-permute-start.5 = (bf16[528,256]{1,0:T(8,128)(2,1)}, bf16[528,256]{1,0:T(8,128)(2,1)S(1)}, u32[]{:S(2)}, u32[]{:S(2)}) collective-permute-start(bf16[528,256]{1,0:T(8,128)(2,1)} %get-tuple-element.190.refs_0_), channel_id=1, source_target_pairs={{0,4},{1,5},{2,6},{3,7},{4,0},{5,1},{6,2},{7,3},{8,12},{9,13},{10,... | collective-permute-start | bytes 811016 | tf_op jit(solution)/shard_map/ppermute | solution.py:38
  23.3 2.3 %collective-permute-start.6 = (bf16[528,256]{1,0:T(8,128)(2,1)}, bf16[528,256]{1,0:T(8,128)(2,1)S(1)}, u32[]{:S(2)}, u32[]{:S(2)}) collective-permute-start(bf16[528,256]{1,0:T(8,128)(2,1)} %get-tuple-element.190.refs_0_), channel_id=1, source_target_pairs={{0,8},{1,9},{2,10},{3,11},{4,12},{5,13},{6,14},{7,15},{8,0},{9,1},... | collective-permute-start | bytes 811016 | tf_op jit(solution)/shard_map/ppermute | solution.py:38
  25.6 9.5 %collective-permute-done.5.refs_1_.refs_7_ = bf16[528,256]{1,0:T(8,128)(2,1)S(1)} collective-permute-done((bf16[528,256]{1,0:T(8,128)(2,1)}, bf16[528,256]{1,0:T(8,128)(2,1)S(1)}, u32[]{:S(2)}, u32[]{:S(2)}) %collective-permute-start.5) | collective-permute-done | bytes 270368 | tf_op jit(solution)/shard_map/ppermute | solution.py:38
  35.1 0.0 collective-permute-done.3.refs_2_.refs_4_
  35.1 0.8 copy-done.2
  35.9 0.0 collective-permute-done.4.refs_1_
  35.9 0.0 collective-permute-done.6.refs_2_.refs_9_
  35.9 1.1 pad_maximum_fusion
  37.0 1.6 %collective-permute-start.9 = (bf16[1040,256]{1,0:T(8,128)(2,1)S(1)}, bf16[1040,256]{1,0:T(8,128)(2,1)}, u32[]{:S(2)}, u32[]{:S(2)}) collective-permute-start(bf16[1040,256]{1,0:T(8,128)(2,1)S(1)} %pad_maximum_fusion), channel_id=1, source_target_pairs={{0,4},{1,5},{2,6},{3,7},{4,0},{5,1},{6,2},{7,3},{8,12},{9,13},{10,... | collective-permute-start | bytes 1597448 | tf_op jit(solution)/shard_map/ppermute | solution.py:38
  38.7 0.3 collective-permute-start.7
  38.9 1.2 collective-permute-start.8
  40.1 1.0 collective-permute-start.10
  41.2 3.5 %collective-permute-done.7.refs_8_ = bf16[528,256]{1,0:T(8,128)(2,1)S(1)} collective-permute-done((bf16[528,256]{1,0:T(8,128)(2,1)S(1)}, bf16[528,256]{1,0:T(8,128)(2,1)S(1)}, u32[]{:S(2)}, u32[]{:S(2)}) %collective-permute-start.7) | collective-permute-done | bytes 270368 | tf_op jit(solution)/shard_map/ppermute | solution.py:38
  44.7 5.8 %collective-permute-done.8.refs_10_ = bf16[528,256]{1,0:T(8,128)(2,1)S(1)} collective-permute-done((bf16[528,256]{1,0:T(8,128)(2,1)S(1)}, bf16[528,256]{1,0:T(8,128)(2,1)S(1)}, u32[]{:S(2)}, u32[]{:S(2)}) %collective-permute-start.8) | collective-permute-done | bytes 270368 | tf_op jit(solution)/shard_map/ppermute | solution.py:38
  50.5 2.9 %collective-permute-done.9.refs_3_.refs_11_.refs_9_ = bf16[1040,256]{1,0:T(8,128)(2,1)} collective-permute-done((bf16[1040,256]{1,0:T(8,128)(2,1)S(1)}, bf16[1040,256]{1,0:T(8,128)(2,1)}, u32[]{:S(2)}, u32[]{:S(2)}) %collective-permute-start.9) | collective-permute-done | bytes 532512 | tf_op jit(solution)/shard_map/ppermute | solution.py:38
  53.4 0.6 collective-permute-done.10.refs_11_
  54.0 0.3 collective-permute-start.12
  54.3 1.9 %pad_maximum_fusion.1 = bf16[1024,256]{1,0:T(8,128)(2,1)} fusion(bf16[512,256]{1,0:T(8,128)(2,1)} %get-tuple-element.208, bf16[512,256]{1,0:T(8,128)(2,1)} %collective-permute-done.10.refs_11_), kind=kLoop, calls=%fused_computation.1 | loop fusion | flops 1048576 | bytes 1048576 | tf_op jit(solution)/shard_map/concatenate | solution.py:568
  56.1 1.1 collective-permute-start.14
  57.2 1.2 collective-permute-start.13
  58.4 2.0 %collective-permute-start.15 = (bf16[512,256]{1,0:T(8,128)(2,1)}, bf16[512,256]{1,0:T(8,128)(2,1)}, u32[]{:S(2)}, u32[]{:S(2)}) collective-permute-start(bf16[512,256]{1,0:T(8,128)(2,1)} %get-tuple-element.208), channel_id=1, source_target_pairs={{0,8},{1,9},{2,10},{3,11},{4,12},{5,13},{6,14},{7,15},{8,0},{9,1},... | collective-permute-start | bytes 786440 | tf_op jit(solution)/shard_map/ppermute | solution.py:38
  60.4 2.1 %places.1 = (s32[16,128]{1,0:T(8,128)}, s32[16,128]{1,0:T(8,128)}) custom-call(s32[3]{0:T(128)} %pad_add_fusion.place, bf16[528,256]{1,0:T(8,128)(2,1)} %get-tuple-element.190.refs_0_, bf16[528,256]{1,0:T(8,128)(2,1)} %copy-done.1, bf16[528,256]{1,0:T(8,128)(2,1)} %copy-done, bf16[1040,256]{1,0:T(8,128)(2,1)} %collective-permute-done.9.refs_3_.refs_11_.refs_9_), custom_call_target="tpu_custom_call" | custom-call | bytes 65536 | tf_op jit(solution)/shard_map/places/pallas_call | solution.py:376
  62.6 5.5 %project.3 = (f32[512,256]{1,0:T(8,128)}, bf16[512,512]{1,0:T(8,128)(2,1)}) custom-call(s32[3]{0:T(128)} %pad_add_fusion.place, bf16[256,4096]{1,0:T(8,128)(2,1)} %normalize.1.refs_0_, bf16[256,4096]{1,0:T(8,128)(2,1)} %collective-permute-done.4.refs_1_, bf16[256,768]{1,0:T(8,128)(2,1)} %copy-done.2, ...), custom_call_target="tpu_custom_call" | custom-call | flops 939524096 | bytes 6291456 | tf_op jit(solution)/shard_map/project/pallas_call | solution.py:320
  68.0 0.0 collective-permute-done.11.refs_0_.refs_2_
  68.1 1.9 %collective-permute-done.13.refs_12_ = bf16[512,256]{1,0:T(8,128)(2,1)} collective-permute-done((bf16[512,256]{1,0:T(8,128)(2,1)}, bf16[512,256]{1,0:T(8,128)(2,1)}, u32[]{:S(2)}, u32[]{:S(2)}) %collective-permute-start.13) | collective-permute-done | bytes 262176 | tf_op jit(solution)/shard_map/ppermute | solution.py:38
  70.0 2.6 %collective-permute-done.14.refs_13_ = bf16[1024,256]{1,0:T(8,128)(2,1)} collective-permute-done((bf16[1024,256]{1,0:T(8,128)(2,1)}, bf16[1024,256]{1,0:T(8,128)(2,1)}, u32[]{:S(2)}, u32[]{:S(2)}) %collective-permute-start.14) | collective-permute-done | bytes 524320 | tf_op jit(solution)/shard_map/ppermute | solution.py:38
  72.6 0.0 collective-permute-done.12.refs_12_.refs_10_
  72.6 0.0 collective-permute-done.15.refs_15_
  72.6 3.8 %collective-permute-start.16 = (bf16[256,4096]{1,0:T(8,128)(2,1)}, bf16[256,4096]{1,0:T(8,128)(2,1)}, u32[]{:S(2)}, u32[]{:S(2)}) collective-permute-start(bf16[256,4096]{1,0:T(8,128)(2,1)} %collective-permute-done.11.refs_0_.refs_2_), channel_id=1, source_target_pairs={{0,1},{1,0},{2,3},{3,2},{4,5},{5,4},{6,7},{7,6},{8,9},{9,8},{10,11... | collective-permute-start | bytes 6291464 | tf_op jit(solution)/shard_map/ppermute | solution.py:38
  76.4 1.2 collective-permute-start.19
  77.6 3.1 %collective-permute-start.20 = (bf16[512,256]{1,0:T(8,128)(2,1)}, bf16[512,256]{1,0:T(8,128)(2,1)}, u32[]{:S(2)}, u32[]{:S(2)}) collective-permute-start(bf16[512,256]{1,0:T(8,128)(2,1)} %collective-permute-done.15.refs_15_), channel_id=1, source_target_pairs={{0,4},{1,5},{2,6},{3,7},{4,0},{5,1},{6,2},{7,3},{8,12},{9,13},{10,... | collective-permute-start | bytes 786440 | tf_op jit(solution)/shard_map/ppermute | solution.py:38
  80.7 0.3 collective-permute-start.21
  81.0 0.0 collective-permute-done.16.refs_1_.refs_3_
  81.0 6.1 %project.4 = (bf16[1024,256]{1,0:T(8,128)(2,1)}, bf16[768,256]{1,0:T(8,128)(2,1)}, bf16[768,256]{1,0:T(8,128)(2,1)}) custom-call(s32[3]{0:T(128)} %pad_add_fusion.place, bf16[256,4096]{1,0:T(8,128)(2,1)} %collective-permute-done.11.refs_0_.refs_2_, bf16[256,4096]{1,0:T(8,128)(2,1)} %collective-permute-done.16.refs_1_.refs_3_, bf16[256,768]{1,0:T(8,128)(2,1)} %copy-done.2, ...), custom_call_target="tpu_custom_call" | custom-call | flops 1073741824 | bytes 6815744 | tf_op jit(solution)/shard_map/project/pallas_call | solution.py:320
  87.1 2.7 %collective-permute-start.17 = (bf16[768,256]{1,0:T(8,128)(2,1)}, bf16[768,256]{1,0:T(8,128)(2,1)}, u32[]{:S(2)}, u32[]{:S(2)}) collective-permute-start(bf16[768,256]{1,0:T(8,128)(2,1)} %get-tuple-element.246), channel_id=1, source_target_pairs={{0,4},{1,5},{2,6},{3,7},{4,0},{5,1},{6,2},{7,3},{8,12},{9,13},{10,... | collective-permute-start | bytes 1179656 | tf_op jit(solution)/shard_map/ppermute | solution.py:38
  89.8 0.0 collective-permute-done.20.refs_16_
  89.8 1.2 collective-permute-start.22
  91.1 1.4 %collective-permute-start.18 = (bf16[768,256]{1,0:T(8,128)(2,1)}, bf16[768,256]{1,0:T(8,128)(2,1)}, u32[]{:S(2)}, u32[]{:S(2)}) collective-permute-start(bf16[768,256]{1,0:T(8,128)(2,1)} %get-tuple-element.248), channel_id=1, source_target_pairs={{4,8},{5,9},{6,10},{7,11},{8,4},{9,5},{10,6},{11,7},{20,24},{21,25... | collective-permute-start | bytes 1179656 | tf_op jit(solution)/shard_map/ppermute | solution.py:49
  92.5 0.0 collective-permute-done.19.refs_14_
  92.5 10.2 %project.5 = (bf16[1024,256]{1,0:T(8,128)(2,1)}, f32[1024,256]{1,0:T(8,128)}, bf16[1024,1024]{1,0:T(8,128)(2,1)}) custom-call(s32[3]{0:T(128)} %pad_add_fusion.place, bf16[256,4096]{1,0:T(8,128)(2,1)} %normalize.1.refs_0_, bf16[256,4096]{1,0:T(8,128)(2,1)} %collective-permute-done.4.refs_1_, bf16[256,4096]{1,0:T(8,128)(2,1)} %collective-permute-done.11.refs_0_.refs_2_, ...), custom_call_target="tpu_custom_call" | custom-call | flops 4294967296 | bytes 13631488 | tf_op jit(solution)/shard_map/project/pallas_call | solution.py:320
  102.7 0.0 collective-permute-done.21.refs_3_
  102.7 0.0 collective-permute-done.22.refs_4_
  102.7 0.0 collective-permute-done.18.outer
  102.7 6.6 %attend.3 = (bf16[256,512]{1,0:T(8,128)(2,1)}, bf16[256,512]{1,0:T(8,128)(2,1)}) custom-call(s32[16,128]{1,0:T(8,128)} %get-tuple-element.230.first_ref, s32[16,128]{1,0:T(8,128)} %get-tuple-element.231.count_ref, s32[3]{0:T(128)} %pad_add_fusion.place, bf16[768,256]{1,0:T(8,128)(2,1)} %collective-permute-done.17.inner, ...), custom_call_target="tpu_custom_call" | custom-call | flops 939524096 | bytes 1835008 | tf_op jit(solution)/shard_map/attend/pallas_call | solution.py:491
  109.3 0.2 collective-permute-start.24
  109.5 2.3 %collective-permute-start.25 = (bf16[256,512]{1,0:T(8,128)(2,1)}, bf16[256,512]{1,0:T(8,128)(2,1)}, u32[]{:S(2)}, u32[]{:S(2)}) collective-permute-start(bf16[256,512]{1,0:T(8,128)(2,1)} %get-tuple-element.262), channel_id=1, source_target_pairs={{0,3},{1,2},{2,1},{3,0},{4,7},{5,6},{6,5},{7,4},{8,11},{9,10},{10,... | collective-permute-start | bytes 786440 | tf_op jit(solution)/shard_map/ppermute | solution.py:38
  111.8 6.4 %attend.2 = (bf16[256,512]{1,0:T(8,128)(2,1)}, bf16[256,512]{1,0:T(8,128)(2,1)}) custom-call(s32[16,128]{1,0:T(8,128)} %get-tuple-element.230.first_ref, s32[16,128]{1,0:T(8,128)} %get-tuple-element.231.count_ref, s32[3]{0:T(128)} %pad_add_fusion.place, bf16[768,256]{1,0:T(8,128)(2,1)} %collective-permute-done.17.inner, ...), custom_call_target="tpu_custom_call" | custom-call | flops 939524096 | bytes 1835008 | tf_op jit(solution)/shard_map/attend/pallas_call | solution.py:491
  118.2 0.0 collective-permute-start.23
  118.2 0.0 collective-permute-done.24.refs_2_
  118.2 5.0 %collective-permute-done.25.refs_3_ = bf16[256,512]{1,0:T(8,128)(2,1)} collective-permute-done((bf16[256,512]{1,0:T(8,128)(2,1)}, bf16[256,512]{1,0:T(8,128)(2,1)}, u32[]{:S(2)}, u32[]{:S(2)}) %collective-permute-start.25) | collective-permute-done | bytes 262176 | tf_op jit(solution)/shard_map/ppermute | solution.py:38
  123.3 2.2 %assemble.1 = bf16[256,2048]{1,0:T(8,128)(2,1)} custom-call(s32[3]{0:T(128)} %pad_add_fusion.place, bf16[256,512]{1,0:T(8,128)(2,1)} %get-tuple-element.265.refs_0_, bf16[256,512]{1,0:T(8,128)(2,1)} %collective-permute-done.23.refs_1_, bf16[256,512]{1,0:T(8,128)(2,1)} %collective-permute-done.24.refs_2_, bf16[256,512]{1,0:T(8,128)(2,1)} %collective-permute-done.25.refs_3_), custom_call_target="tpu_custom_call" | custom-call | bytes 2097152 | tf_op jit(solution)/shard_map/assemble/pallas_call | solution.py:521
  (11 shorter events, 0.0 us)
Async XLA Ops:
  3.2 13.6 %collective-permute-start = (bf16[272,768]{1,0:T(8,128)(2,1)}, bf16[272,768]{1,0:T(8,128)(2,1)}, u32[]{:S(2)}, u32[]{:S(2)}) collective-permute-start(bf16[272,768]{1,0:T(8,128)(2,1)} %get-tuple-element.140), channel_id=1, source_target_pairs={{0,1},{1,0},{2,3},{3,2},{4,5},{5,4},{6,7},{7,6},{8,9},{9,8},{10,11... | collective-permute-start | bytes 1253384 | tf_op jit(solution)/shard_map/ppermute | solution.py:38
  3.3 8.7 %collective-permute-start.1 = (bf16[144,768]{1,0:T(8,128)(2,1)}, bf16[144,768]{1,0:T(8,128)(2,1)}, u32[]{:S(2)}, u32[]{:S(2)}) collective-permute-start(bf16[144,768]{1,0:T(8,128)(2,1)} %get-tuple-element.141), channel_id=1, source_target_pairs={{0,2},{1,3},{2,0},{3,1},{4,6},{5,7},{6,4},{7,5},{8,10},{9,11},{10,... | collective-permute-start | bytes 663560 | tf_op jit(solution)/shard_map/ppermute | solution.py:38
  6.0 10.8 %collective-permute-start.2 = (bf16[144,768]{1,0:T(8,128)(2,1)}, bf16[144,768]{1,0:T(8,128)(2,1)}, u32[]{:S(2)}, u32[]{:S(2)}) collective-permute-start(bf16[144,768]{1,0:T(8,128)(2,1)} %get-tuple-element.142), channel_id=1, source_target_pairs={{0,3},{1,2},{2,1},{3,0},{4,7},{5,6},{6,5},{7,4},{8,11},{9,10},{10,... | collective-permute-start | bytes 663560 | tf_op jit(solution)/shard_map/ppermute | solution.py:38
  19.1 16.8 %collective-permute-start.4 = (bf16[256,4096]{1,0:T(8,128)(2,1)}, bf16[256,4096]{1,0:T(8,128)(2,1)}, u32[]{:S(2)}, u32[]{:S(2)}) collective-permute-start(bf16[256,4096]{1,0:T(8,128)(2,1)} %normalize.1.refs_0_), channel_id=1, source_target_pairs={{0,1},{1,0},{2,3},{3,2},{4,5},{5,4},{6,7},{7,6},{8,9},{9,8},{10,11... | collective-permute-start | bytes 6291464 | tf_op jit(solution)/shard_map/ppermute | solution.py:38
  19.5 48.6 %collective-permute-start.11 = (bf16[256,4096]{1,0:T(8,128)(2,1)}, bf16[256,4096]{1,0:T(8,128)(2,1)}, u32[]{:S(2)}, u32[]{:S(2)}) collective-permute-start(bf16[256,4096]{1,0:T(8,128)(2,1)} %normalize.1.refs_0_), channel_id=1, source_target_pairs={{0,2},{1,3},{2,0},{3,1},{4,6},{5,7},{6,4},{7,5},{8,10},{9,11},{10,... | collective-permute-start | bytes 6291464 | tf_op jit(solution)/shard_map/ppermute | solution.py:38
  20.8 14.4 %collective-permute-start.3 = (bf16[256,768]{1,0:T(8,128)(2,1)}, bf16[256,768]{1,0:T(8,128)(2,1)S(1)}, u32[]{:S(2)}, u32[]{:S(2)}) collective-permute-start(bf16[256,768]{1,0:T(8,128)(2,1)} %get-tuple-element.147), channel_id=1, source_target_pairs={{0,16},{1,17},{2,18},{3,19},{4,20},{5,21},{6,22},{7,23},{8,24},{9,... | collective-permute-start | bytes 1179656 | tf_op jit(solution)/shard_map/ppermute | solution.py:38
  22.0 13.1 %collective-permute-start.5 = (bf16[528,256]{1,0:T(8,128)(2,1)}, bf16[528,256]{1,0:T(8,128)(2,1)S(1)}, u32[]{:S(2)}, u32[]{:S(2)}) collective-permute-start(bf16[528,256]{1,0:T(8,128)(2,1)} %get-tuple-element.190.refs_0_), channel_id=1, source_target_pairs={{0,4},{1,5},{2,6},{3,7},{4,0},{5,1},{6,2},{7,3},{8,12},{9,13},{10,... | collective-permute-start | bytes 811016 | tf_op jit(solution)/shard_map/ppermute | solution.py:38
  23.3 12.6 %collective-permute-start.6 = (bf16[528,256]{1,0:T(8,128)(2,1)}, bf16[528,256]{1,0:T(8,128)(2,1)S(1)}, u32[]{:S(2)}, u32[]{:S(2)}) collective-permute-start(bf16[528,256]{1,0:T(8,128)(2,1)} %get-tuple-element.190.refs_0_), channel_id=1, source_target_pairs={{0,8},{1,9},{2,10},{3,11},{4,12},{5,13},{6,14},{7,15},{8,0},{9,1},... | collective-permute-start | bytes 811016 | tf_op jit(solution)/shard_map/ppermute | solution.py:38
  35.1 15.3 %copy-start.1 = (bf16[528,256]{1,0:T(8,128)(2,1)}, bf16[528,256]{1,0:T(8,128)(2,1)S(1)}, u32[]{:S(2)}) copy-start(bf16[528,256]{1,0:T(8,128)(2,1)S(1)} %collective-permute-done.5.refs_1_.refs_7_) | copy-start | bytes 811012
  35.1 0.8 copy-start.2
  35.9 3.0 %copy-start = (bf16[528,256]{1,0:T(8,128)(2,1)}, bf16[528,256]{1,0:T(8,128)(2,1)S(1)}, u32[]{:S(2)}) copy-start(bf16[528,256]{1,0:T(8,128)(2,1)S(1)} %collective-permute-done.6.refs_2_.refs_9_) | copy-start | bytes 811012
  37.0 16.4 %collective-permute-start.9 = (bf16[1040,256]{1,0:T(8,128)(2,1)S(1)}, bf16[1040,256]{1,0:T(8,128)(2,1)}, u32[]{:S(2)}, u32[]{:S(2)}) collective-permute-start(bf16[1040,256]{1,0:T(8,128)(2,1)S(1)} %pad_maximum_fusion), channel_id=1, source_target_pairs={{0,4},{1,5},{2,6},{3,7},{4,0},{5,1},{6,2},{7,3},{8,12},{9,13},{10,... | collective-permute-start | bytes 1597448 | tf_op jit(solution)/shard_map/ppermute | solution.py:38
  38.7 6.0 %collective-permute-start.7 = (bf16[528,256]{1,0:T(8,128)(2,1)S(1)}, bf16[528,256]{1,0:T(8,128)(2,1)S(1)}, u32[]{:S(2)}, u32[]{:S(2)}) collective-permute-start(bf16[528,256]{1,0:T(8,128)(2,1)S(1)} %collective-permute-done.5.refs_1_.refs_7_), channel_id=1, source_target_pairs={{0,16},{1,17},{2,18},{3,19},{4,20},{5,21},{6,22},{7,23},{8,24},{9,... | collective-permute-start | bytes 811016 | tf_op jit(solution)/shard_map/ppermute | solution.py:38
  38.9 11.5 %collective-permute-start.8 = (bf16[528,256]{1,0:T(8,128)(2,1)S(1)}, bf16[528,256]{1,0:T(8,128)(2,1)S(1)}, u32[]{:S(2)}, u32[]{:S(2)}) collective-permute-start(bf16[528,256]{1,0:T(8,128)(2,1)S(1)} %collective-permute-done.6.refs_2_.refs_9_), channel_id=1, source_target_pairs={{0,16},{1,17},{2,18},{3,19},{4,20},{5,21},{6,22},{7,23},{8,24},{9,... | collective-permute-start | bytes 811016 | tf_op jit(solution)/shard_map/ppermute | solution.py:38
  40.1 13.9 %collective-permute-start.10 = (bf16[512,256]{1,0:T(8,128)(2,1)}, bf16[512,256]{1,0:T(8,128)(2,1)}, u32[]{:S(2)}, u32[]{:S(2)}) collective-permute-start(bf16[512,256]{1,0:T(8,128)(2,1)} %get-tuple-element.174), channel_id=1, source_target_pairs={{0,8},{1,9},{2,10},{3,11},{4,12},{5,13},{6,14},{7,15},{8,0},{9,1},... | collective-permute-start | bytes 786440 | tf_op jit(solution)/shard_map/ppermute | solution.py:38
  44.7 8.7 %copy-start.3 = (bf16[528,256]{1,0:T(8,128)(2,1)}, bf16[528,256]{1,0:T(8,128)(2,1)S(1)}, u32[]{:S(2)}) copy-start(bf16[528,256]{1,0:T(8,128)(2,1)S(1)} %collective-permute-done.7.refs_8_) | copy-start | bytes 811012
  50.5 3.5 %copy-start.4 = (bf16[528,256]{1,0:T(8,128)(2,1)}, bf16[528,256]{1,0:T(8,128)(2,1)S(1)}, u32[]{:S(2)}) copy-start(bf16[528,256]{1,0:T(8,128)(2,1)S(1)} %collective-permute-done.8.refs_10_) | copy-start | bytes 811012
  54.0 18.6 %collective-permute-start.12 = (bf16[1040,256]{1,0:T(8,128)(2,1)}, bf16[1040,256]{1,0:T(8,128)(2,1)}, u32[]{:S(2)}, u32[]{:S(2)}) collective-permute-start(bf16[1040,256]{1,0:T(8,128)(2,1)} %collective-permute-done.9.refs_3_.refs_11_.refs_9_), channel_id=1, source_target_pairs={{0,16},{1,17},{2,18},{3,19},{4,20},{5,21},{6,22},{7,23},{8,24},{9,... | collective-permute-start | bytes 1597448 | tf_op jit(solution)/shard_map/ppermute | solution.py:38
  56.1 16.5 %collective-permute-start.14 = (bf16[1024,256]{1,0:T(8,128)(2,1)}, bf16[1024,256]{1,0:T(8,128)(2,1)}, u32[]{:S(2)}, u32[]{:S(2)}) collective-permute-start(bf16[1024,256]{1,0:T(8,128)(2,1)} %pad_maximum_fusion.1), channel_id=1, source_target_pairs={{0,4},{1,5},{2,6},{3,7},{4,0},{5,1},{6,2},{7,3},{8,12},{9,13},{10,... | collective-permute-start | bytes 1572872 | tf_op jit(solution)/shard_map/ppermute | solution.py:38
  57.2 12.8 %collective-permute-start.13 = (bf16[512,256]{1,0:T(8,128)(2,1)}, bf16[512,256]{1,0:T(8,128)(2,1)}, u32[]{:S(2)}, u32[]{:S(2)}) collective-permute-start(bf16[512,256]{1,0:T(8,128)(2,1)} %collective-permute-done.10.refs_11_), channel_id=1, source_target_pairs={{0,16},{1,17},{2,18},{3,19},{4,20},{5,21},{6,22},{7,23},{8,24},{9,... | collective-permute-start | bytes 786440 | tf_op jit(solution)/shard_map/ppermute | solution.py:38
  58.4 14.2 %collective-permute-start.15 = (bf16[512,256]{1,0:T(8,128)(2,1)}, bf16[512,256]{1,0:T(8,128)(2,1)}, u32[]{:S(2)}, u32[]{:S(2)}) collective-permute-start(bf16[512,256]{1,0:T(8,128)(2,1)} %get-tuple-element.208), channel_id=1, source_target_pairs={{0,8},{1,9},{2,10},{3,11},{4,12},{5,13},{6,14},{7,15},{8,0},{9,1},... | collective-permute-start | bytes 786440 | tf_op jit(solution)/shard_map/ppermute | solution.py:38
  72.6 8.3 %collective-permute-start.16 = (bf16[256,4096]{1,0:T(8,128)(2,1)}, bf16[256,4096]{1,0:T(8,128)(2,1)}, u32[]{:S(2)}, u32[]{:S(2)}) collective-permute-start(bf16[256,4096]{1,0:T(8,128)(2,1)} %collective-permute-done.11.refs_0_.refs_2_), channel_id=1, source_target_pairs={{0,1},{1,0},{2,3},{3,2},{4,5},{5,4},{6,7},{7,6},{8,9},{9,8},{10,11... | collective-permute-start | bytes 6291464 | tf_op jit(solution)/shard_map/ppermute | solution.py:38
  76.4 16.1 %collective-permute-start.19 = (bf16[1024,256]{1,0:T(8,128)(2,1)}, bf16[1024,256]{1,0:T(8,128)(2,1)}, u32[]{:S(2)}, u32[]{:S(2)}) collective-permute-start(bf16[1024,256]{1,0:T(8,128)(2,1)} %collective-permute-done.14.refs_13_), channel_id=1, source_target_pairs={{0,16},{1,17},{2,18},{3,19},{4,20},{5,21},{6,22},{7,23},{8,24},{9,... | collective-permute-start | bytes 1572872 | tf_op jit(solution)/shard_map/ppermute | solution.py:38
  77.6 12.2 %collective-permute-start.20 = (bf16[512,256]{1,0:T(8,128)(2,1)}, bf16[512,256]{1,0:T(8,128)(2,1)}, u32[]{:S(2)}, u32[]{:S(2)}) collective-permute-start(bf16[512,256]{1,0:T(8,128)(2,1)} %collective-permute-done.15.refs_15_), channel_id=1, source_target_pairs={{0,4},{1,5},{2,6},{3,7},{4,0},{5,1},{6,2},{7,3},{8,12},{9,13},{10,... | collective-permute-start | bytes 786440 | tf_op jit(solution)/shard_map/ppermute | solution.py:38
  80.7 22.0 %collective-permute-start.21 = (bf16[512,256]{1,0:T(8,128)(2,1)}, bf16[512,256]{1,0:T(8,128)(2,1)}, u32[]{:S(2)}, u32[]{:S(2)}) collective-permute-start(bf16[512,256]{1,0:T(8,128)(2,1)} %collective-permute-done.15.refs_15_), channel_id=1, source_target_pairs={{0,16},{1,17},{2,18},{3,19},{4,20},{5,21},{6,22},{7,23},{8,24},{9,... | collective-permute-start | bytes 786440 | tf_op jit(solution)/shard_map/ppermute | solution.py:38
  87.1 15.6 %collective-permute-start.17 = (bf16[768,256]{1,0:T(8,128)(2,1)}, bf16[768,256]{1,0:T(8,128)(2,1)}, u32[]{:S(2)}, u32[]{:S(2)}) collective-permute-start(bf16[768,256]{1,0:T(8,128)(2,1)} %get-tuple-element.246), channel_id=1, source_target_pairs={{0,4},{1,5},{2,6},{3,7},{4,0},{5,1},{6,2},{7,3},{8,12},{9,13},{10,... | collective-permute-start | bytes 1179656 | tf_op jit(solution)/shard_map/ppermute | solution.py:38
  89.8 12.9 %collective-permute-start.22 = (bf16[512,256]{1,0:T(8,128)(2,1)}, bf16[512,256]{1,0:T(8,128)(2,1)}, u32[]{:S(2)}, u32[]{:S(2)}) collective-permute-start(bf16[512,256]{1,0:T(8,128)(2,1)} %collective-permute-done.20.refs_16_), channel_id=1, source_target_pairs={{0,16},{1,17},{2,18},{3,19},{4,20},{5,21},{6,22},{7,23},{8,24},{9,... | collective-permute-start | bytes 786440 | tf_op jit(solution)/shard_map/ppermute | solution.py:38
  91.1 11.7 %collective-permute-start.18 = (bf16[768,256]{1,0:T(8,128)(2,1)}, bf16[768,256]{1,0:T(8,128)(2,1)}, u32[]{:S(2)}, u32[]{:S(2)}) collective-permute-start(bf16[768,256]{1,0:T(8,128)(2,1)} %get-tuple-element.248), channel_id=1, source_target_pairs={{4,8},{5,9},{6,10},{7,11},{8,4},{9,5},{10,6},{11,7},{20,24},{21,25... | collective-permute-start | bytes 1179656 | tf_op jit(solution)/shard_map/ppermute | solution.py:49
  109.3 8.9 %collective-permute-start.24 = (bf16[256,512]{1,0:T(8,128)(2,1)}, bf16[256,512]{1,0:T(8,128)(2,1)}, u32[]{:S(2)}, u32[]{:S(2)}) collective-permute-start(bf16[256,512]{1,0:T(8,128)(2,1)} %get-tuple-element.261), channel_id=1, source_target_pairs={{0,2},{1,3},{2,0},{3,1},{4,6},{5,7},{6,4},{7,5},{8,10},{9,11},{10,... | collective-permute-start | bytes 786440 | tf_op jit(solution)/shard_map/ppermute | solution.py:38
  109.5 13.7 %collective-permute-start.25 = (bf16[256,512]{1,0:T(8,128)(2,1)}, bf16[256,512]{1,0:T(8,128)(2,1)}, u32[]{:S(2)}, u32[]{:S(2)}) collective-permute-start(bf16[256,512]{1,0:T(8,128)(2,1)} %get-tuple-element.262), channel_id=1, source_target_pairs={{0,3},{1,2},{2,1},{3,0},{4,7},{5,6},{6,5},{7,4},{8,11},{9,10},{10,... | collective-permute-start | bytes 786440 | tf_op jit(solution)/shard_map/ppermute | solution.py:38
  118.2 5.0 %collective-permute-start.23 = (bf16[256,512]{1,0:T(8,128)(2,1)}, bf16[256,512]{1,0:T(8,128)(2,1)}, u32[]{:S(2)}, u32[]{:S(2)}) collective-permute-start(bf16[256,512]{1,0:T(8,128)(2,1)} %get-tuple-element.260), channel_id=1, source_target_pairs={{0,1},{1,0},{2,3},{3,2},{4,5},{5,4},{6,7},{7,6},{8,9},{9,8},{10,11... | collective-permute-start | bytes 786440 | tf_op jit(solution)/shard_map/ppermute | solution.py:38

commit v7 on v6

--- a/solution.py
+++ b/solution.py
@@ -605,7 +605,7 @@
             waited = phase == chunks + hops - 1
             long = {} if waited else {n: arrays.pop(n) for n in LONG if n in arrays}
             if phase < chunks + hops:
-                final = {n: arrays.pop(n) for n in [f"phase{phase - 1}from{layers // 2}"] if n in arrays}
+                final = {n: arrays.pop(n) for n in [f"phase{phase - 1}from{layers // 2}", f"phase{phase - 1}from1"] if n in arrays}
                 arrays = lax.optimization_barrier(arrays)
                 arrays = lax.optimization_barrier({**arrays, **final})
             arrays.update(long)

time: 126 us -> 126 us (level)
  transfers between devices with their start and end apart: 26 -> 26, of which waited for: 10 -> 11; matrix products, arithmetic and copies ran while one was open for 3% -> 3% of each run, Pallas kernels for 27% -> 27%
where the time goes in v7:
time: 126 us
  Pallas kernels  48.7 us (39%)
  waiting for transfers between devices  38.7 us (31%)
  starting transfers between devices  34.4 us (27%)
  other arithmetic  3.62 us (3%)
    ppermute x25, waiting for transfers between devices, swap(): return lax.ppermute(value, AXES, pairs)  38.7 us
    ppermute x25, starting transfers between devices, swap(): return lax.ppermute(value, AXES, pairs)  33 us
    pallas_call x3, Pallas kernels, project(): pl.pallas_call(functools.partial(project_kernel, items, (len(tokens), len...  21.8 us
    pallas_call x2, Pallas kernels, attend(): pl.pallas_call(functools.partial(attend_kernel, base, block, deep, firsts...  13 us
    pallas_call x1, Pallas kernels, normalize(): pl.pallas_call(norm_kernel, out_shape=[jax.ShapeDtypeStruct((n, width), j...  4.11 us
    pallas_call x1, Pallas kernels, pack(): pl.pallas_call(functools.partial(pack_kernel, team, depth // groups, note...  3.18 us
    concatenate x2, other arithmetic, join(): return views[0] if len(views) == 1 else jnp.concatenate(views, axis=0)  3.04 us
  transfers between devices with their start and end apart: 26, of which 11 were waited for; matrix products, arithmetic and copies ran while one was open for 3% of the time, Pallas kernels for 27%

profile of v7, /device:TPU:1, one launch (start us, length us, event | category | flops | bytes accessed | tf_op | source)
XLA Modules:
  0.0 125.6 jit_solution(15395375077931468161)
XLA Ops:
  0.0 3.2 %pack.1 = (bf16[272,768]{1,0:T(8,128)(2,1)}, bf16[272,768]{1,0:T(8,128)(2,1)}, bf16[144,768]{1,0:T(8,128)(2,1)}, bf16[144,768]{1,0:T(8,128)(2,1)}) custom-call(s32[2]{0:T(128)} %numbers.1, bf16[256,512]{1,0:T(8,128)(2,1)} %refs_0_.1, bf16[256,512]{1,0:T(8,128)(2,1)} %refs_1_.1, bf16[256,2048]{1,0:T(8,128)(2,1)} %refs_2_.1), custom_call_target="tpu_custom_call" | custom-call | bytes 3145728 | tf_op jit(solution)/shard_map/pack/pallas_call | solution.py:112
  3.2 0.1 collective-permute-start
  3.3 2.7 %collective-permute-start.1 = (bf16[144,768]{1,0:T(8,128)(2,1)}, bf16[144,768]{1,0:T(8,128)(2,1)}, u32[]{:S(2)}, u32[]{:S(2)}) collective-permute-start(bf16[144,768]{1,0:T(8,128)(2,1)} %get-tuple-element.138), channel_id=1, source_target_pairs={{0,2},{1,3},{2,0},{3,1},{4,6},{5,7},{6,4},{7,5},{8,10},{9,11},{10,... | collective-permute-start | bytes 663560 | tf_op jit(solution)/shard_map/ppermute | solution.py:38
  6.0 0.0 collective-permute-start.2
  6.1 4.1 %normalize.1.refs_0_ = bf16[256,4096]{1,0:T(8,128)(2,1)} custom-call(bf16[256,4096]{1,0:T(8,128)(2,1)} %tokens_ref, f32[1,4096]{1,0:T(1,128)} %bitcast.4), custom_call_target="tpu_custom_call" | custom-call | flops 6291456 | bytes 4194304 | tf_op jit(solution)/shard_map/normalize/pallas_call | solution.py:67
  10.2 0.6 pad_add_fusion.place
  10.7 1.3 %collective-permute-done.1.refs_2_.refs_5_.refs_7_ = bf16[144,768]{1,0:T(8,128)(2,1)} collective-permute-done((bf16[144,768]{1,0:T(8,128)(2,1)}, bf16[144,768]{1,0:T(8,128)(2,1)}, u32[]{:S(2)}, u32[]{:S(2)}) %collective-permute-start.1) | collective-permute-done | bytes 221216 | tf_op jit(solution)/shard_map/ppermute | solution.py:38
  12.0 4.7 %collective-permute-done.2.refs_3_.refs_6_.refs_8_ = bf16[144,768]{1,0:T(8,128)(2,1)} collective-permute-done((bf16[144,768]{1,0:T(8,128)(2,1)}, bf16[144,768]{1,0:T(8,128)(2,1)}, u32[]{:S(2)}, u32[]{:S(2)}) %collective-permute-start.2) | collective-permute-done | bytes 221216 | tf_op jit(solution)/shard_map/ppermute | solution.py:38
  16.8 0.0 collective-permute-done.refs_1_.refs_4_.refs_6_
  16.8 2.3 %shards.1 = (bf16[528,256]{1,0:T(8,128)(2,1)}, bf16[512,256]{1,0:T(8,128)(2,1)}, bf16[512,256]{1,0:T(8,128)(2,1)}, bf16[256,768]{1,0:T(8,128)(2,1)}) custom-call(s32[3]{0:T(128)} %pad_add_fusion.place, bf16[272,768]{1,0:T(8,128)(2,1)} %get-tuple-element.228.refs_0_.refs_3_.refs_5_, bf16[272,768]{1,0:T(8,128)(2,1)} %collective-permute-done.refs_1_.refs_4_.refs_6_, ...), custom_call_target="tpu_custom_call" | custom-call | bytes 2359296 | tf_op jit(solution)/shard_map/shards/pallas_call | solution.py:157
  19.1 0.4 collective-permute-start.4
  19.5 1.3 %collective-permute-start.11 = (bf16[256,4096]{1,0:T(8,128)(2,1)}, bf16[256,4096]{1,0:T(8,128)(2,1)}, u32[]{:S(2)}, u32[]{:S(2)}) collective-permute-start(bf16[256,4096]{1,0:T(8,128)(2,1)} %normalize.1.refs_0_), channel_id=1, source_target_pairs={{0,2},{1,3},{2,0},{3,1},{4,6},{5,7},{6,4},{7,5},{8,10},{9,11},{10,... | collective-permute-start | bytes 6291464 | tf_op jit(solution)/shard_map/ppermute | solution.py:38
  20.8 1.2 collective-permute-start.3
  22.0 1.3 %collective-permute-start.5 = (bf16[528,256]{1,0:T(8,128)(2,1)}, bf16[528,256]{1,0:T(8,128)(2,1)S(1)}, u32[]{:S(2)}, u32[]{:S(2)}) collective-permute-start(bf16[528,256]{1,0:T(8,128)(2,1)} %get-tuple-element.185.refs_0_), channel_id=1, source_target_pairs={{0,4},{1,5},{2,6},{3,7},{4,0},{5,1},{6,2},{7,3},{8,12},{9,13},{10,... | collective-permute-start | bytes 811016 | tf_op jit(solution)/shard_map/ppermute | solution.py:38
  23.3 2.3 %collective-permute-start.6 = (bf16[528,256]{1,0:T(8,128)(2,1)}, bf16[528,256]{1,0:T(8,128)(2,1)S(1)}, u32[]{:S(2)}, u32[]{:S(2)}) collective-permute-start(bf16[528,256]{1,0:T(8,128)(2,1)} %get-tuple-element.185.refs_0_), channel_id=1, source_target_pairs={{0,8},{1,9},{2,10},{3,11},{4,12},{5,13},{6,14},{7,15},{8,0},{9,1},... | collective-permute-start | bytes 811016 | tf_op jit(solution)/shard_map/ppermute | solution.py:38
  25.6 5.6 %collective-permute-done.3.refs_2_.refs_4_ = bf16[256,768]{1,0:T(8,128)(2,1)S(1)} collective-permute-done((bf16[256,768]{1,0:T(8,128)(2,1)}, bf16[256,768]{1,0:T(8,128)(2,1)S(1)}, u32[]{:S(2)}, u32[]{:S(2)}) %collective-permute-start.3) | collective-permute-done | bytes 393248 | tf_op jit(solution)/shard_map/ppermute | solution.py:38
  31.2 0.0 collective-permute-done.4.refs_1_
  31.2 3.9 %collective-permute-done.5.refs_1_.refs_7_ = bf16[528,256]{1,0:T(8,128)(2,1)S(1)} collective-permute-done((bf16[528,256]{1,0:T(8,128)(2,1)}, bf16[528,256]{1,0:T(8,128)(2,1)S(1)}, u32[]{:S(2)}, u32[]{:S(2)}) %collective-permute-start.5) | collective-permute-done | bytes 270368 | tf_op jit(solution)/shard_map/ppermute | solution.py:38
  35.1 0.0 collective-permute-done.6.refs_2_.refs_9_
  35.2 1.2 pad_maximum_fusion
  36.3 2.3 %collective-permute-start.9 = (bf16[1040,256]{1,0:T(8,128)(2,1)S(1)}, bf16[1040,256]{1,0:T(8,128)(2,1)}, u32[]{:S(2)}, u32[]{:S(2)}) collective-permute-start(bf16[1040,256]{1,0:T(8,128)(2,1)S(1)} %pad_maximum_fusion), channel_id=1, source_target_pairs={{0,4},{1,5},{2,6},{3,7},{4,0},{5,1},{6,2},{7,3},{8,12},{9,13},{10,... | collective-permute-start | bytes 1597448 | tf_op jit(solution)/shard_map/ppermute | solution.py:38
  38.7 0.3 collective-permute-start.7
  38.9 1.2 collective-permute-start.8
  40.1 0.4 collective-permute-start.10
  40.5 4.2 %collective-permute-done.7.refs_8_ = bf16[528,256]{1,0:T(8,128)(2,1)S(1)} collective-permute-done((bf16[528,256]{1,0:T(8,128)(2,1)S(1)}, bf16[528,256]{1,0:T(8,128)(2,1)S(1)}, u32[]{:S(2)}, u32[]{:S(2)}) %collective-permute-start.7) | collective-permute-done | bytes 270368 | tf_op jit(solution)/shard_map/ppermute | solution.py:38
  44.7 5.8 %collective-permute-done.8.refs_10_ = bf16[528,256]{1,0:T(8,128)(2,1)S(1)} collective-permute-done((bf16[528,256]{1,0:T(8,128)(2,1)S(1)}, bf16[528,256]{1,0:T(8,128)(2,1)S(1)}, u32[]{:S(2)}, u32[]{:S(2)}) %collective-permute-start.8) | collective-permute-done | bytes 270368 | tf_op jit(solution)/shard_map/ppermute | solution.py:38
  50.5 3.5 %collective-permute-done.10.refs_11_ = bf16[512,256]{1,0:T(8,128)(2,1)} collective-permute-done((bf16[512,256]{1,0:T(8,128)(2,1)}, bf16[512,256]{1,0:T(8,128)(2,1)}, u32[]{:S(2)}, u32[]{:S(2)}) %collective-permute-start.10) | collective-permute-done | bytes 262176 | tf_op jit(solution)/shard_map/ppermute | solution.py:38
  54.0 0.0 collective-permute-done.9.refs_3_.refs_11_.refs_9_
  54.0 0.3 collective-permute-start.12
  54.3 1.9 %pad_maximum_fusion.1 = bf16[1024,256]{1,0:T(8,128)(2,1)} fusion(bf16[512,256]{1,0:T(8,128)(2,1)} %get-tuple-element.203, bf16[512,256]{1,0:T(8,128)(2,1)} %collective-permute-done.10.refs_11_), kind=kLoop, calls=%fused_computation.1 | loop fusion | flops 1048576 | bytes 1048576 | tf_op jit(solution)/shard_map/concatenate | solution.py:568
  56.2 1.1 collective-permute-start.14
  57.3 1.2 collective-permute-start.13
  58.5 2.0 %collective-permute-start.15 = (bf16[512,256]{1,0:T(8,128)(2,1)}, bf16[512,256]{1,0:T(8,128)(2,1)}, u32[]{:S(2)}, u32[]{:S(2)}) collective-permute-start(bf16[512,256]{1,0:T(8,128)(2,1)} %get-tuple-element.203), channel_id=1, source_target_pairs={{0,8},{1,9},{2,10},{3,11},{4,12},{5,13},{6,14},{7,15},{8,0},{9,1},... | collective-permute-start | bytes 786440 | tf_op jit(solution)/shard_map/ppermute | solution.py:38
  60.5 2.1 %places.1 = (s32[16,128]{1,0:T(8,128)}, s32[16,128]{1,0:T(8,128)}) custom-call(s32[3]{0:T(128)} %pad_add_fusion.place, bf16[528,256]{1,0:T(8,128)(2,1)} %get-tuple-element.185.refs_0_, bf16[528,256]{1,0:T(8,128)(2,1)} %copy-done.1, bf16[528,256]{1,0:T(8,128)(2,1)} %copy-done, bf16[1040,256]{1,0:T(8,128)(2,1)} %collective-permute-done.9.refs_3_.refs_11_.refs_9_), custom_call_target="tpu_custom_call" | custom-call | bytes 65536 | tf_op jit(solution)/shard_map/places/pallas_call | solution.py:376
  62.6 5.5 %project.3 = (f32[512,256]{1,0:T(8,128)}, bf16[512,512]{1,0:T(8,128)(2,1)}) custom-call(s32[3]{0:T(128)} %pad_add_fusion.place, bf16[256,4096]{1,0:T(8,128)(2,1)} %normalize.1.refs_0_, bf16[256,4096]{1,0:T(8,128)(2,1)} %copy-done.2, bf16[256,768]{1,0:T(8,128)(2,1)} %copy-done.3, bf16[272,768]{1,0:T(8,128)(2,1)} %get-tuple-element.228.refs_0_.refs_3_.refs_5_, ...), custom_call_target="tpu_custom_call" | custom-call | flops 939524096 | bytes 6291456 | tf_op jit(solution)/shard_map/project/pallas_call | solution.py:320
  68.1 0.0 collective-permute-done.11.refs_0_.refs_2_
  68.1 2.1 %collective-permute-done.13.refs_12_ = bf16[512,256]{1,0:T(8,128)(2,1)} collective-permute-done((bf16[512,256]{1,0:T(8,128)(2,1)}, bf16[512,256]{1,0:T(8,128)(2,1)}, u32[]{:S(2)}, u32[]{:S(2)}) %collective-permute-start.13) | collective-permute-done | bytes 262176 | tf_op jit(solution)/shard_map/ppermute | solution.py:38
  70.2 0.0 collective-permute-done.12.refs_12_.refs_10_
  70.2 0.3 collective-permute-done.15.refs_15_
  70.5 2.2 %collective-permute-done.14.refs_13_ = bf16[1024,256]{1,0:T(8,128)(2,1)} collective-permute-done((bf16[1024,256]{1,0:T(8,128)(2,1)}, bf16[1024,256]{1,0:T(8,128)(2,1)}, u32[]{:S(2)}, u32[]{:S(2)}) %collective-permute-start.14) | collective-permute-done | bytes 524320 | tf_op jit(solution)/shard_map/ppermute | solution.py:38
  72.7 3.8 %collective-permute-start.16 = (bf16[256,4096]{1,0:T(8,128)(2,1)}, bf16[256,4096]{1,0:T(8,128)(2,1)}, u32[]{:S(2)}, u32[]{:S(2)}) collective-permute-start(bf16[256,4096]{1,0:T(8,128)(2,1)} %collective-permute-done.11.refs_0_.refs_2_), channel_id=1, source_target_pairs={{0,1},{1,0},{2,3},{3,2},{4,5},{5,4},{6,7},{7,6},{8,9},{9,8},{10,11... | collective-permute-start | bytes 6291464 | tf_op jit(solution)/shard_map/ppermute | solution.py:38
  76.5 1.2 collective-permute-start.19
  77.7 3.1 %collective-permute-start.20 = (bf16[512,256]{1,0:T(8,128)(2,1)}, bf16[512,256]{1,0:T(8,128)(2,1)}, u32[]{:S(2)}, u32[]{:S(2)}) collective-permute-start(bf16[512,256]{1,0:T(8,128)(2,1)} %collective-permute-done.15.refs_15_), channel_id=1, source_target_pairs={{0,4},{1,5},{2,6},{3,7},{4,0},{5,1},{6,2},{7,3},{8,12},{9,13},{10,... | collective-permute-start | bytes 786440 | tf_op jit(solution)/shard_map/ppermute | solution.py:38
  80.8 0.3 collective-permute-start.21
  81.0 0.0 collective-permute-done.16.refs_1_.refs_3_
  81.0 6.1 %project.4 = (bf16[1024,256]{1,0:T(8,128)(2,1)}, bf16[768,256]{1,0:T(8,128)(2,1)}, bf16[768,256]{1,0:T(8,128)(2,1)}) custom-call(s32[3]{0:T(128)} %pad_add_fusion.place, bf16[256,4096]{1,0:T(8,128)(2,1)} %collective-permute-done.11.refs_0_.refs_2_, bf16[256,4096]{1,0:T(8,128)(2,1)} %collective-permute-done.16.refs_1_.refs_3_, bf16[256,768]{1,0:T(8,128)(2,1)} %copy-done.3, ...), custom_call_target="tpu_custom_call" | custom-call | flops 1073741824 | bytes 6815744 | tf_op jit(solution)/shard_map/project/pallas_call | solution.py:320
  87.2 2.7 %collective-permute-start.17 = (bf16[768,256]{1,0:T(8,128)(2,1)}, bf16[768,256]{1,0:T(8,128)(2,1)}, u32[]{:S(2)}, u32[]{:S(2)}) collective-permute-start(bf16[768,256]{1,0:T(8,128)(2,1)} %get-tuple-element.240), channel_id=1, source_target_pairs={{0,4},{1,5},{2,6},{3,7},{4,0},{5,1},{6,2},{7,3},{8,12},{9,13},{10,... | collective-permute-start | bytes 1179656 | tf_op jit(solution)/shard_map/ppermute | solution.py:38
  89.9 0.0 collective-permute-done.20.refs_16_
  89.9 1.2 collective-permute-start.22
  91.1 1.4 %collective-permute-start.18 = (bf16[768,256]{1,0:T(8,128)(2,1)}, bf16[768,256]{1,0:T(8,128)(2,1)}, u32[]{:S(2)}, u32[]{:S(2)}) collective-permute-start(bf16[768,256]{1,0:T(8,128)(2,1)} %get-tuple-element.242), channel_id=1, source_target_pairs={{4,8},{5,9},{6,10},{7,11},{8,4},{9,5},{10,6},{11,7},{20,24},{21,25... | collective-permute-start | bytes 1179656 | tf_op jit(solution)/shard_map/ppermute | solution.py:49
  92.5 0.0 collective-permute-done.19.refs_14_
  92.5 10.2 %project.5 = (bf16[1024,256]{1,0:T(8,128)(2,1)}, f32[1024,256]{1,0:T(8,128)}, bf16[1024,1024]{1,0:T(8,128)(2,1)}) custom-call(s32[3]{0:T(128)} %pad_add_fusion.place, bf16[256,4096]{1,0:T(8,128)(2,1)} %normalize.1.refs_0_, bf16[256,4096]{1,0:T(8,128)(2,1)} %copy-done.2, bf16[256,4096]{1,0:T(8,128)(2,1)} %collective-permute-done.11.refs_0_.refs_2_, ...), custom_call_target="tpu_custom_call" | custom-call | flops 4294967296 | bytes 13631488 | tf_op jit(solution)/shard_map/project/pallas_call | solution.py:320
  102.8 0.0 collective-permute-done.21.refs_3_
  102.8 0.0 collective-permute-done.22.refs_4_
  102.8 0.0 collective-permute-done.17.inner
  102.8 6.6 %attend.3 = (bf16[256,512]{1,0:T(8,128)(2,1)}, bf16[256,512]{1,0:T(8,128)(2,1)}) custom-call(s32[16,128]{1,0:T(8,128)} %get-tuple-element.224.first_ref, s32[16,128]{1,0:T(8,128)} %get-tuple-element.225.count_ref, s32[3]{0:T(128)} %pad_add_fusion.place, bf16[768,256]{1,0:T(8,128)(2,1)} %collective-permute-done.17.inner, ...), custom_call_target="tpu_custom_call" | custom-call | flops 939524096 | bytes 1835008 | tf_op jit(solution)/shard_map/attend/pallas_call | solution.py:491
  109.4 0.2 collective-permute-start.24
  109.6 2.3 %collective-permute-start.25 = (bf16[256,512]{1,0:T(8,128)(2,1)}, bf16[256,512]{1,0:T(8,128)(2,1)}, u32[]{:S(2)}, u32[]{:S(2)}) collective-permute-start(bf16[256,512]{1,0:T(8,128)(2,1)} %get-tuple-element.256), channel_id=1, source_target_pairs={{0,3},{1,2},{2,1},{3,0},{4,7},{5,6},{6,5},{7,4},{8,11},{9,10},{10,... | collective-permute-start | bytes 786440 | tf_op jit(solution)/shard_map/ppermute | solution.py:38
  112.0 6.4 %attend.2 = (bf16[256,512]{1,0:T(8,128)(2,1)}, bf16[256,512]{1,0:T(8,128)(2,1)}) custom-call(s32[16,128]{1,0:T(8,128)} %get-tuple-element.224.first_ref, s32[16,128]{1,0:T(8,128)} %get-tuple-element.225.count_ref, s32[3]{0:T(128)} %pad_add_fusion.place, bf16[768,256]{1,0:T(8,128)(2,1)} %collective-permute-done.17.inner, ...), custom_call_target="tpu_custom_call" | custom-call | flops 939524096 | bytes 1835008 | tf_op jit(solution)/shard_map/attend/pallas_call | solution.py:491
  118.3 0.0 collective-permute-start.23
  118.3 0.0 collective-permute-done.24.refs_2_
  118.3 5.0 %collective-permute-done.25.refs_3_ = bf16[256,512]{1,0:T(8,128)(2,1)} collective-permute-done((bf16[256,512]{1,0:T(8,128)(2,1)}, bf16[256,512]{1,0:T(8,128)(2,1)}, u32[]{:S(2)}, u32[]{:S(2)}) %collective-permute-start.25) | collective-permute-done | bytes 262176 | tf_op jit(solution)/shard_map/ppermute | solution.py:38
  123.4 0.0 collective-permute-done.23.refs_1_
  123.4 2.2 %assemble.1 = bf16[256,2048]{1,0:T(8,128)(2,1)} custom-call(s32[3]{0:T(128)} %pad_add_fusion.place, bf16[256,512]{1,0:T(8,128)(2,1)} %get-tuple-element.259.refs_0_, bf16[256,512]{1,0:T(8,128)(2,1)} %collective-permute-done.23.refs_1_, bf16[256,512]{1,0:T(8,128)(2,1)} %collective-permute-done.24.refs_2_, bf16[256,512]{1,0:T(8,128)(2,1)} %collective-permute-done.25.refs_3_), custom_call_target="tpu_custom_call" | custom-call | bytes 2097152 | tf_op jit(solution)/shard_map/assemble/pallas_call | solution.py:521
  (13 shorter events, 0.0 us)
Async XLA Ops:
  3.2 13.6 %collective-permute-start = (bf16[272,768]{1,0:T(8,128)(2,1)}, bf16[272,768]{1,0:T(8,128)(2,1)}, u32[]{:S(2)}, u32[]{:S(2)}) collective-permute-start(bf16[272,768]{1,0:T(8,128)(2,1)} %get-tuple-element.137), channel_id=1, source_target_pairs={{0,1},{1,0},{2,3},{3,2},{4,5},{5,4},{6,7},{7,6},{8,9},{9,8},{10,11... | collective-permute-start | bytes 1253384 | tf_op jit(solution)/shard_map/ppermute | solution.py:38
  3.3 8.7 %collective-permute-start.1 = (bf16[144,768]{1,0:T(8,128)(2,1)}, bf16[144,768]{1,0:T(8,128)(2,1)}, u32[]{:S(2)}, u32[]{:S(2)}) collective-permute-start(bf16[144,768]{1,0:T(8,128)(2,1)} %get-tuple-element.138), channel_id=1, source_target_pairs={{0,2},{1,3},{2,0},{3,1},{4,6},{5,7},{6,4},{7,5},{8,10},{9,11},{10,... | collective-permute-start | bytes 663560 | tf_op jit(solution)/shard_map/ppermute | solution.py:38
  6.0 10.8 %collective-permute-start.2 = (bf16[144,768]{1,0:T(8,128)(2,1)}, bf16[144,768]{1,0:T(8,128)(2,1)}, u32[]{:S(2)}, u32[]{:S(2)}) collective-permute-start(bf16[144,768]{1,0:T(8,128)(2,1)} %get-tuple-element.139), channel_id=1, source_target_pairs={{0,3},{1,2},{2,1},{3,0},{4,7},{5,6},{6,5},{7,4},{8,11},{9,10},{10,... | collective-permute-start | bytes 663560 | tf_op jit(solution)/shard_map/ppermute | solution.py:38
  19.1 12.1 %collective-permute-start.4 = (bf16[256,4096]{1,0:T(8,128)(2,1)}, bf16[256,4096]{1,0:T(8,128)(2,1)S(1)}, u32[]{:S(2)}, u32[]{:S(2)}) collective-permute-start(bf16[256,4096]{1,0:T(8,128)(2,1)} %normalize.1.refs_0_), channel_id=1, source_target_pairs={{0,1},{1,0},{2,3},{3,2},{4,5},{5,4},{6,7},{7,6},{8,9},{9,8},{10,11... | collective-permute-start | bytes 6291464 | tf_op jit(solution)/shard_map/ppermute | solution.py:38
  19.5 48.6 %collective-permute-start.11 = (bf16[256,4096]{1,0:T(8,128)(2,1)}, bf16[256,4096]{1,0:T(8,128)(2,1)}, u32[]{:S(2)}, u32[]{:S(2)}) collective-permute-start(bf16[256,4096]{1,0:T(8,128)(2,1)} %normalize.1.refs_0_), channel_id=1, source_target_pairs={{0,2},{1,3},{2,0},{3,1},{4,6},{5,7},{6,4},{7,5},{8,10},{9,11},{10,... | collective-permute-start | bytes 6291464 | tf_op jit(solution)/shard_map/ppermute | solution.py:38
  20.8 10.4 %collective-permute-start.3 = (bf16[256,768]{1,0:T(8,128)(2,1)}, bf16[256,768]{1,0:T(8,128)(2,1)S(1)}, u32[]{:S(2)}, u32[]{:S(2)}) collective-permute-start(bf16[256,768]{1,0:T(8,128)(2,1)} %get-tuple-element.144), channel_id=1, source_target_pairs={{0,16},{1,17},{2,18},{3,19},{4,20},{5,21},{6,22},{7,23},{8,24},{9,... | collective-permute-start | bytes 1179656 | tf_op jit(solution)/shard_map/ppermute | solution.py:38
  22.0 13.1 %collective-permute-start.5 = (bf16[528,256]{1,0:T(8,128)(2,1)}, bf16[528,256]{1,0:T(8,128)(2,1)S(1)}, u32[]{:S(2)}, u32[]{:S(2)}) collective-permute-start(bf16[528,256]{1,0:T(8,128)(2,1)} %get-tuple-element.185.refs_0_), channel_id=1, source_target_pairs={{0,4},{1,5},{2,6},{3,7},{4,0},{5,1},{6,2},{7,3},{8,12},{9,13},{10,... | collective-permute-start | bytes 811016 | tf_op jit(solution)/shard_map/ppermute | solution.py:38
  23.3 11.9 %collective-permute-start.6 = (bf16[528,256]{1,0:T(8,128)(2,1)}, bf16[528,256]{1,0:T(8,128)(2,1)S(1)}, u32[]{:S(2)}, u32[]{:S(2)}) collective-permute-start(bf16[528,256]{1,0:T(8,128)(2,1)} %get-tuple-element.185.refs_0_), channel_id=1, source_target_pairs={{0,8},{1,9},{2,10},{3,11},{4,12},{5,13},{6,14},{7,15},{8,0},{9,1},... | collective-permute-start | bytes 811016 | tf_op jit(solution)/shard_map/ppermute | solution.py:38
  31.2 3.9 %copy-start.3 = (bf16[256,768]{1,0:T(8,128)(2,1)}, bf16[256,768]{1,0:T(8,128)(2,1)S(1)}, u32[]{:S(2)}) copy-start(bf16[256,768]{1,0:T(8,128)(2,1)S(1)} %collective-permute-done.3.refs_2_.refs_4_) | copy-start | bytes 1179652
  31.2 3.9 %copy-start.2 = (bf16[256,4096]{1,0:T(8,128)(2,1)}, bf16[256,4096]{1,0:T(8,128)(2,1)S(1)}, u32[]{:S(2)}) copy-start(bf16[256,4096]{1,0:T(8,128)(2,1)S(1)} %collective-permute-done.4.refs_1_) | copy-start | bytes 6291460
  35.1 15.3 %copy-start.1 = (bf16[528,256]{1,0:T(8,128)(2,1)}, bf16[528,256]{1,0:T(8,128)(2,1)S(1)}, u32[]{:S(2)}) copy-start(bf16[528,256]{1,0:T(8,128)(2,1)S(1)} %collective-permute-done.5.refs_1_.refs_7_) | copy-start | bytes 811012
  35.2 3.8 %copy-start = (bf16[528,256]{1,0:T(8,128)(2,1)}, bf16[528,256]{1,0:T(8,128)(2,1)S(1)}, u32[]{:S(2)}) copy-start(bf16[528,256]{1,0:T(8,128)(2,1)S(1)} %collective-permute-done.6.refs_2_.refs_9_) | copy-start | bytes 811012
  36.3 17.7 %collective-permute-start.9 = (bf16[1040,256]{1,0:T(8,128)(2,1)S(1)}, bf16[1040,256]{1,0:T(8,128)(2,1)}, u32[]{:S(2)}, u32[]{:S(2)}) collective-permute-start(bf16[1040,256]{1,0:T(8,128)(2,1)S(1)} %pad_maximum_fusion), channel_id=1, source_target_pairs={{0,4},{1,5},{2,6},{3,7},{4,0},{5,1},{6,2},{7,3},{8,12},{9,13},{10,... | collective-permute-start | bytes 1597448 | tf_op jit(solution)/shard_map/ppermute | solution.py:38
  38.7 6.0 %collective-permute-start.7 = (bf16[528,256]{1,0:T(8,128)(2,1)S(1)}, bf16[528,256]{1,0:T(8,128)(2,1)S(1)}, u32[]{:S(2)}, u32[]{:S(2)}) collective-permute-start(bf16[528,256]{1,0:T(8,128)(2,1)S(1)} %collective-permute-done.5.refs_1_.refs_7_), channel_id=1, source_target_pairs={{0,16},{1,17},{2,18},{3,19},{4,20},{5,21},{6,22},{7,23},{8,24},{9,... | collective-permute-start | bytes 811016 | tf_op jit(solution)/shard_map/ppermute | solution.py:38
  38.9 11.5 %collective-permute-start.8 = (bf16[528,256]{1,0:T(8,128)(2,1)S(1)}, bf16[528,256]{1,0:T(8,128)(2,1)S(1)}, u32[]{:S(2)}, u32[]{:S(2)}) collective-permute-start(bf16[528,256]{1,0:T(8,128)(2,1)S(1)} %collective-permute-done.6.refs_2_.refs_9_), channel_id=1, source_target_pairs={{0,16},{1,17},{2,18},{3,19},{4,20},{5,21},{6,22},{7,23},{8,24},{9,... | collective-permute-start | bytes 811016 | tf_op jit(solution)/shard_map/ppermute | solution.py:38
  40.1 13.9 %collective-permute-start.10 = (bf16[512,256]{1,0:T(8,128)(2,1)}, bf16[512,256]{1,0:T(8,128)(2,1)}, u32[]{:S(2)}, u32[]{:S(2)}) collective-permute-start(bf16[512,256]{1,0:T(8,128)(2,1)} %get-tuple-element.171), channel_id=1, source_target_pairs={{0,8},{1,9},{2,10},{3,11},{4,12},{5,13},{6,14},{7,15},{8,0},{9,1},... | collective-permute-start | bytes 786440 | tf_op jit(solution)/shard_map/ppermute | solution.py:38
  44.7 9.3 %copy-start.4 = (bf16[528,256]{1,0:T(8,128)(2,1)}, bf16[528,256]{1,0:T(8,128)(2,1)S(1)}, u32[]{:S(2)}) copy-start(bf16[528,256]{1,0:T(8,128)(2,1)S(1)} %collective-permute-done.7.refs_8_) | copy-start | bytes 811012
  50.5 3.5 %copy-start.5 = (bf16[528,256]{1,0:T(8,128)(2,1)}, bf16[528,256]{1,0:T(8,128)(2,1)S(1)}, u32[]{:S(2)}) copy-start(bf16[528,256]{1,0:T(8,128)(2,1)S(1)} %collective-permute-done.8.refs_10_) | copy-start | bytes 811012
  54.0 16.2 %collective-permute-start.12 = (bf16[1040,256]{1,0:T(8,128)(2,1)}, bf16[1040,256]{1,0:T(8,128)(2,1)}, u32[]{:S(2)}, u32[]{:S(2)}) collective-permute-start(bf16[1040,256]{1,0:T(8,128)(2,1)} %collective-permute-done.9.refs_3_.refs_11_.refs_9_), channel_id=1, source_target_pairs={{0,16},{1,17},{2,18},{3,19},{4,20},{5,21},{6,22},{7,23},{8,24},{9,... | collective-permute-start | bytes 1597448 | tf_op jit(solution)/shard_map/ppermute | solution.py:38
  56.2 16.5 %collective-permute-start.14 = (bf16[1024,256]{1,0:T(8,128)(2,1)}, bf16[1024,256]{1,0:T(8,128)(2,1)}, u32[]{:S(2)}, u32[]{:S(2)}) collective-permute-start(bf16[1024,256]{1,0:T(8,128)(2,1)} %pad_maximum_fusion.1), channel_id=1, source_target_pairs={{0,4},{1,5},{2,6},{3,7},{4,0},{5,1},{6,2},{7,3},{8,12},{9,13},{10,... | collective-permute-start | bytes 1572872 | tf_op jit(solution)/shard_map/ppermute | solution.py:38
  57.3 12.9 %collective-permute-start.13 = (bf16[512,256]{1,0:T(8,128)(2,1)}, bf16[512,256]{1,0:T(8,128)(2,1)}, u32[]{:S(2)}, u32[]{:S(2)}) collective-permute-start(bf16[512,256]{1,0:T(8,128)(2,1)} %collective-permute-done.10.refs_11_), channel_id=1, source_target_pairs={{0,16},{1,17},{2,18},{3,19},{4,20},{5,21},{6,22},{7,23},{8,24},{9,... | collective-permute-start | bytes 786440 | tf_op jit(solution)/shard_map/ppermute | solution.py:38
  58.5 12.0 %collective-permute-start.15 = (bf16[512,256]{1,0:T(8,128)(2,1)}, bf16[512,256]{1,0:T(8,128)(2,1)}, u32[]{:S(2)}, u32[]{:S(2)}) collective-permute-start(bf16[512,256]{1,0:T(8,128)(2,1)} %get-tuple-element.203), channel_id=1, source_target_pairs={{0,8},{1,9},{2,10},{3,11},{4,12},{5,13},{6,14},{7,15},{8,0},{9,1},... | collective-permute-start | bytes 786440 | tf_op jit(solution)/shard_map/ppermute | solution.py:38
  72.7 8.4 %collective-permute-start.16 = (bf16[256,4096]{1,0:T(8,128)(2,1)}, bf16[256,4096]{1,0:T(8,128)(2,1)}, u32[]{:S(2)}, u32[]{:S(2)}) collective-permute-start(bf16[256,4096]{1,0:T(8,128)(2,1)} %collective-permute-done.11.refs_0_.refs_2_), channel_id=1, source_target_pairs={{0,1},{1,0},{2,3},{3,2},{4,5},{5,4},{6,7},{7,6},{8,9},{9,8},{10,11... | collective-permute-start | bytes 6291464 | tf_op jit(solution)/shard_map/ppermute | solution.py:38
  76.5 16.1 %collective-permute-start.19 = (bf16[1024,256]{1,0:T(8,128)(2,1)}, bf16[1024,256]{1,0:T(8,128)(2,1)}, u32[]{:S(2)}, u32[]{:S(2)}) collective-permute-start(bf16[1024,256]{1,0:T(8,128)(2,1)} %collective-permute-done.14.refs_13_), channel_id=1, source_target_pairs={{0,16},{1,17},{2,18},{3,19},{4,20},{5,21},{6,22},{7,23},{8,24},{9,... | collective-permute-start | bytes 1572872 | tf_op jit(solution)/shard_map/ppermute | solution.py:38
  77.7 12.2 %collective-permute-start.20 = (bf16[512,256]{1,0:T(8,128)(2,1)}, bf16[512,256]{1,0:T(8,128)(2,1)}, u32[]{:S(2)}, u32[]{:S(2)}) collective-permute-start(bf16[512,256]{1,0:T(8,128)(2,1)} %collective-permute-done.15.refs_15_), channel_id=1, source_target_pairs={{0,4},{1,5},{2,6},{3,7},{4,0},{5,1},{6,2},{7,3},{8,12},{9,13},{10,... | collective-permute-start | bytes 786440 | tf_op jit(solution)/shard_map/ppermute | solution.py:38
  80.8 22.0 %collective-permute-start.21 = (bf16[512,256]{1,0:T(8,128)(2,1)}, bf16[512,256]{1,0:T(8,128)(2,1)}, u32[]{:S(2)}, u32[]{:S(2)}) collective-permute-start(bf16[512,256]{1,0:T(8,128)(2,1)} %collective-permute-done.15.refs_15_), channel_id=1, source_target_pairs={{0,16},{1,17},{2,18},{3,19},{4,20},{5,21},{6,22},{7,23},{8,24},{9,... | collective-permute-start | bytes 786440 | tf_op jit(solution)/shard_map/ppermute | solution.py:38
  87.2 15.6 %collective-permute-start.17 = (bf16[768,256]{1,0:T(8,128)(2,1)}, bf16[768,256]{1,0:T(8,128)(2,1)}, u32[]{:S(2)}, u32[]{:S(2)}) collective-permute-start(bf16[768,256]{1,0:T(8,128)(2,1)} %get-tuple-element.240), channel_id=1, source_target_pairs={{0,4},{1,5},{2,6},{3,7},{4,0},{5,1},{6,2},{7,3},{8,12},{9,13},{10,... | collective-permute-start | bytes 1179656 | tf_op jit(solution)/shard_map/ppermute | solution.py:38
  89.9 12.9 %collective-permute-start.22 = (bf16[512,256]{1,0:T(8,128)(2,1)}, bf16[512,256]{1,0:T(8,128)(2,1)}, u32[]{:S(2)}, u32[]{:S(2)}) collective-permute-start(bf16[512,256]{1,0:T(8,128)(2,1)} %collective-permute-done.20.refs_16_), channel_id=1, source_target_pairs={{0,16},{1,17},{2,18},{3,19},{4,20},{5,21},{6,22},{7,23},{8,24},{9,... | collective-permute-start | bytes 786440 | tf_op jit(solution)/shard_map/ppermute | solution.py:38
  91.1 11.7 %collective-permute-start.18 = (bf16[768,256]{1,0:T(8,128)(2,1)}, bf16[768,256]{1,0:T(8,128)(2,1)}, u32[]{:S(2)}, u32[]{:S(2)}) collective-permute-start(bf16[768,256]{1,0:T(8,128)(2,1)} %get-tuple-element.242), channel_id=1, source_target_pairs={{4,8},{5,9},{6,10},{7,11},{8,4},{9,5},{10,6},{11,7},{20,24},{21,25... | collective-permute-start | bytes 1179656 | tf_op jit(solution)/shard_map/ppermute | solution.py:49
  109.4 8.9 %collective-permute-start.24 = (bf16[256,512]{1,0:T(8,128)(2,1)}, bf16[256,512]{1,0:T(8,128)(2,1)}, u32[]{:S(2)}, u32[]{:S(2)}) collective-permute-start(bf16[256,512]{1,0:T(8,128)(2,1)} %get-tuple-element.255), channel_id=1, source_target_pairs={{0,2},{1,3},{2,0},{3,1},{4,6},{5,7},{6,4},{7,5},{8,10},{9,11},{10,... | collective-permute-start | bytes 786440 | tf_op jit(solution)/shard_map/ppermute | solution.py:38
  109.6 13.7 %collective-permute-start.25 = (bf16[256,512]{1,0:T(8,128)(2,1)}, bf16[256,512]{1,0:T(8,128)(2,1)}, u32[]{:S(2)}, u32[]{:S(2)}) collective-permute-start(bf16[256,512]{1,0:T(8,128)(2,1)} %get-tuple-element.256), channel_id=1, source_target_pairs={{0,3},{1,2},{2,1},{3,0},{4,7},{5,6},{6,5},{7,4},{8,11},{9,10},{10,... | collective-permute-start | bytes 786440 | tf_op jit(solution)/shard_map/ppermute | solution.py:38
  118.3 5.1 %collective-permute-start.23 = (bf16[256,512]{1,0:T(8,128)(2,1)}, bf16[256,512]{1,0:T(8,128)(2,1)}, u32[]{:S(2)}, u32[]{:S(2)}) collective-permute-start(bf16[256,512]{1,0:T(8,128)(2,1)} %get-tuple-element.254), channel_id=1, source_target_pairs={{0,1},{1,0},{2,3},{3,2},{4,5},{5,4},{6,7},{7,6},{8,9},{9,8},{10,11... | collective-permute-start | bytes 786440 | tf_op jit(solution)/shard_map/ppermute | solution.py:38
